TPU v7x, 256 devices: a whole 4x4x8 slice. The times are simulated.
256 devices in a mesh: seq: 32 (over y_hi, z, core), tensor: 8 (over y_lo, x).
Axes of the slice: x: 4, y: 4 (y_hi: 2, y_lo: 2; y = y_hi * 2 + y_lo), z: 8, core: 2. Of those that a mesh axis runs over, the one named last changes fastest.
Arguments:
- tokens: bfloat16 [2, 4096, 3072], P(None, 'seq'), as said below
- w_query: bfloat16 [3072, 3072], P(None, 'tensor'), as said below
- w_key: bfloat16 [3072, 3072], P(None, 'tensor'), as said below
- w_value: bfloat16 [3072, 3072], P(None, 'tensor'), as said below
- w_out: bfloat16 [3072, 3072], P('tensor'), as said below
- cotangent: bfloat16 [2, 4096, 3072], P(None, 'seq'), may hold values from -6 to 6
- noise_value: float32 [3072, 3072], P('seq', 'tensor'), may hold values from -6 to 6
- noise_out: float32 [3072, 3072], P('tensor', 'seq'), may hold values from -6 to 6
Outputs:
- grad_value: float32 [3072, 3072], P('seq', 'tensor')
- grad_out: float32 [3072, 3072], P('tensor', 'seq')
Inputs may be any that keep to these rules, and one draw needn't show every extreme that they name: `tokens`: patch activations. `w_query`: scaled by the fan-in. `w_key`: scaled by the fan-in. `w_value`: scaled by the fan-in. `w_out`: scaled by the fan-in.
All inputs are finite; a program needn't handle non-finite values.
Results may differ from a plain program's by a relative error of at most 0.023.
Values may be sent and summed in bfloat16 or wider, within the bound.
No kernel may reach another device: no remote copies, remote signals or barrier semaphores. Data moves between devices by JAX's collectives and lax.ppermute only.
A program may use at most 128 MiB of HBM per device.

v0:
```python
import math

import jax
import jax.numpy as jnp
from jax import lax
from jax.sharding import PartitionSpec as P

D = 3072
HEADS = 24
HEAD_DIM = 128


def local(tokens, w_query, w_key, w_value, w_out, cotangent, noise_value, noise_out):
    images, patch_rows, width = tokens.shape
    columns = w_query.shape[1]
    head_count = columns // HEAD_DIM
    score_scale = 1.0 / math.sqrt(HEAD_DIM)
    clip_bound = math.sqrt(2.0 * D * HEADS * HEAD_DIM)
    flat_tokens = tokens.reshape(images * patch_rows, width)

    def project(weight):
        product = jnp.dot(flat_tokens, weight, preferred_element_type=jnp.float32)
        return product.astype(jnp.bfloat16).reshape(images, patch_rows, head_count, HEAD_DIM)

    queries = project(w_query)
    key_local = project(w_key)
    value_local = project(w_value)
    keys_all, values_all = (
        lax.all_gather(key_local, "seq", axis=1, tiled=True),
        lax.all_gather(value_local, "seq", axis=1, tiled=True),
    )
    scores = (
        jnp.einsum("iqhd,ikhd->ihqk", queries, keys_all, preferred_element_type=jnp.float32)
        * score_scale
    )
    row_totals = jax.nn.logsumexp(scores, axis=-1)
    attn_probs = jnp.exp(scores - row_totals[..., None]).astype(jnp.bfloat16)
    attended = jnp.einsum(
        "ihqk,ikhd->iqhd", attn_probs, values_all, preferred_element_type=jnp.float32
    ).astype(jnp.bfloat16)
    flat_cotangent = cotangent.reshape(images * patch_rows, width)
    d_attn = jnp.einsum("rd,cd->rc", flat_cotangent, w_out, preferred_element_type=jnp.float32)
    d_attn = d_attn.astype(jnp.bfloat16).reshape(images, patch_rows, head_count, HEAD_DIM)
    summed = lax.psum_scatter(
        jnp.einsum(
            "ihqk,iqhd->kihd", attn_probs, d_attn, preferred_element_type=jnp.float32
        ).astype(jnp.bfloat16),
        "seq",
        scatter_dimension=0,
        tiled=True,
    )
    product = jnp.einsum("iqhd,iqe->ihde", attended, cotangent, preferred_element_type=jnp.float32)
    value_product = jnp.einsum("ipe,pihd->iehd", tokens, summed, preferred_element_type=jnp.float32)
    value_shard = lax.psum_scatter(
        value_product.reshape(images, width, columns).astype(jnp.bfloat16),
        "seq",
        scatter_dimension=1,
        tiled=True,
    ).astype(jnp.float32)
    out_shard = lax.psum_scatter(
        product.reshape(images, columns, width).astype(jnp.bfloat16),
        "seq",
        scatter_dimension=2,
        tiled=True,
    ).astype(jnp.float32)
    partial_value = jnp.sum(jnp.square(value_shard), axis=(1, 2)) + jnp.sum(
        jnp.square(out_shard), axis=(1, 2)
    )
    squares_all = lax.psum(partial_value, ("seq", "tensor"))
    factor = clip_bound / (jnp.sqrt(squares_all) + 0.01)
    grad_value = noise_value
    grad_out = noise_out
    for image_index in range(images):
        grad_value = grad_value + factor[image_index] * value_shard[image_index]
        grad_out = grad_out + factor[image_index] * out_shard[image_index]
    return (grad_value / images, grad_out / images)


def solution(mesh):
    placed = (
        P(None, "seq", None),
        P(None, "tensor"),
        P(None, "tensor"),
        P(None, "tensor"),
        P("tensor", None),
        P(None, "seq", None),
        P("seq", "tensor"),
        P("tensor", "seq"),
    )
    return jax.shard_map(
        local,
        mesh=mesh,
        in_specs=placed,
        out_specs=(P("seq", "tensor"), P("tensor", "seq")),
        check_vma=False,
    )
```

profile of v0, /device:TPU:1, one launch (start us, length us, event | category | flops | bytes accessed | tf_op | source)
XLA Modules:
  0.0 699.3 jit_solution(10537320843807913381)
XLA Ops:
  7.2 1.6 copy-done
  8.8 2.4 convolution_convert_fusion.4
  12.1 3.1 convolution_convert_fusion.3
  16.2 2.6 convolution_convert_fusion.5
  18.9 3.1 convolution_convert_fusion.6
  22.2 88.8 %all-gather.3.cloned.1.call-done = bf16[2,4096,3,128]{3,1,2,0:T(8,128)(2,1)} async-done(((bf16[2,128,3,128]{3,1,2,0:T(8,128)(2,1)}), bf16[2,4096,3,128]{3,1,2,0:T(8,128)(2,1)}) %all-gather.3.cloned.1.call-update) | async-done | bytes 6291472 | tf_op jit(solution)/shard_map/all_gather | solution.py:29
  111.0 4.7 multiply_reduce_fusion
  115.7 2.2 exponential_reduce_fusion
  117.9 2.4 copy-done.2
  120.2 4.8 convolution_convert_fusion
  125.0 8.7 %copy.44 = bf16[4096,768]{1,0:T(8,128)(2,1)} copy(bf16[4096,768]{0,1:T(8,128)(2,1)} %bitcast.62) | data formatting | bytes 12582912
  133.9 73.9 %all-gather.5.cloned.1.call-done = bf16[2,4096,3,128]{1,3,2,0:T(8,128)(2,1)} async-done(((bf16[2,128,3,128]{1,3,2,0:T(8,128)(2,1)}), bf16[2,4096,3,128]{1,3,2,0:T(8,128)(2,1)}) %all-gather.5.cloned.1.call-update) | async-done | bytes 6291472 | tf_op jit(solution)/shard_map/all_gather | solution.py:30
  207.9 12.8 %convolution_convert_fusion.1 = bf16[2,3,128,3072]{3,2,1,0:T(8,128)(2,1)} fusion(bf16[2,128,3072]{2,1,0:T(8,128)(2,1)} %param.13, bf16[2,4096,3,128]{1,3,2,0:T(8,128)(2,1)} %all-gather.5.cloned.1.call-done, f32[2,3,128,4096]{3,2,1,0:T(8,128)} %copy-done.2, f32[2,3,128]{2,1,0:T(4,128)S(1)} %log_add_fusion), kind=kOutput, calls=%fused_computation.4 | convolution fusion | flops 1421180928 | bytes 25168896 | tf_op jit(solution)/shard_map/iqhd,iqe->ihde/dot_general | solution.py:52
  220.7 6.7 copy.31
  227.5 113.6 %reduce-scatter.10.cloned.1.call-done = bf16[128,768]{1,0:T(8,128)(2,1)} async-done(((bf16[4096,768]{1,0:T(8,128)(2,1)}), bf16[128,768]{1,0:T(8,128)(2,1)}) %reduce-scatter.10.cloned.1.call-update) | async-done | bytes 196624
  341.1 1.1 copy.45
  342.2 3.6 convolution_convert_fusion.2
  345.8 6.9 copy.28
  352.7 120.7 %reduce-scatter.8.cloned.1.call-done = bf16[2,384,96]{1,2,0:T(8,128)(2,1)} async-done(((bf16[2,384,3072]{1,2,0:T(8,128)(2,1)}), bf16[2,384,96]{1,2,0:T(8,128)(2,1)}) %reduce-scatter.8.cloned.1.call-update) | async-done | bytes 147472 | tf_op jit(solution)/shard_map/reduce_scatter | solution.py:60
  474.4 132.2 %reduce-scatter.6.cloned.1.call-done = bf16[2,96,384]{2,1,0:T(8,128)(2,1)} async-done(((bf16[2,3072,384]{2,1,0:T(8,128)(2,1)}), bf16[2,96,384]{2,1,0:T(8,128)(2,1)}) %reduce-scatter.6.cloned.1.call-update) | async-done | bytes 147472 | tf_op jit(solution)/shard_map/reduce_scatter | solution.py:54
  606.6 1.0 multiply_reduce_fusion.2
  608.6 78.7 %psum.7 = f32[2]{0:T(128)S(1)} all-reduce(f32[2]{0:T(128)S(1)} %add.34), channel_id=1, replica_groups=mesh['seq'=32,'tensor'=8] {'seq','tensor'}, use_global_device_ids=true, to_apply=%region_7.0 | all-reduce | flops 2 | bytes 16 | tf_op jit(solution)/shard_map/psum | solution.py:69
  688.0 1.9 fusion.8
  690.8 1.9 fusion.13
  (34 shorter events, 5.8 us)
Async XLA Ops:
  7.2 1.7 copy-start
  7.2 103.8 %all-gather.3.cloned.1.call-start = ((), (), s32[]{:S(2)}) async-start(), calls=%async_computation.3 | async-start | bytes 6488064 | tf_op jit(solution)/shard_map/all_gather | solution.py:29
  11.2 5.0 copy-start.3
  12.0 195.8 %all-gather.5.cloned.1.call-start = ((), (), s32[]{:S(2)}) async-start(), calls=%async_computation.5 | async-start | bytes 6488064 | tf_op jit(solution)/shard_map/all_gather | solution.py:30
  16.2 324.9 %reduce-scatter.10.cloned.1.call-start = ((), (), s32[]{:S(2)}) async-start(), calls=%async_computation.7 | async-start | bytes 6488064
  115.7 4.6 copy-start.2
  133.7 339.7 %reduce-scatter.8.cloned.1.call-start = ((), (), s32[]{:S(2)}) async-start(), calls=%async_computation.6 | async-start | bytes 4866048 | tf_op jit(solution)/shard_map/reduce_scatter | solution.py:60
  227.4 379.2 %reduce-scatter.6.cloned.1.call-start = ((), (), s32[]{:S(2)}) async-start(), calls=%async_computation.4 | async-start | bytes 4866048 | tf_op jit(solution)/shard_map/reduce_scatter | solution.py:54
  345.8 347.0 %copy-start.1 = (bf16[3072,384]{1,0:T(8,128)(2,1)S(1)}, bf16[3072,384]{1,0:T(8,128)(2,1)}, u32[]{:S(2)}) copy-start(bf16[3072,384]{1,0:T(8,128)(2,1)} %param.10) | copy-start | bytes 7077892
  345.8 342.2 %copy-start.4 = (f32[384,96]{0,1:T(8,128)S(1)}, f32[384,96]{0,1:T(8,128)}, u32[]{:S(2)}) copy-start(f32[384,96]{0,1:T(8,128)} %param.15) | copy-start | bytes 442372
  345.8 345.0 %copy-start.5 = (f32[96,384]{1,0:T(8,128)S(1)}, f32[96,384]{1,0:T(8,128)}, u32[]{:S(2)}) copy-start(f32[96,384]{1,0:T(8,128)} %param.14) | copy-start | bytes 442372
Sparse Core Ops, SparseCore 0:
  12.2 98.7 all-gather.2
  113.6 94.2 all-gather.4
  212.2 128.8 reduce-scatter.9
  345.2 128.1 reduce-scatter.7
  478.0 128.5 reduce-scatter.5
where the time goes:
time: 700 us; the launch traced here: 699 us
  waiting for transfers between devices  529 us (76%)
  blocking collectives  78.7 us (11%)
  matrix products  37.2 us (5%)
  local copies, waits for them, and re-layouts  29.8 us (4%)
  between operations  13.9 us (2%)
  other arithmetic  10 us (1%)
    reduce_scatter x1, waiting for transfers between devices, local(): lax.psum_scatter(value_product.reshape(images, width, columns).astype(jnp...  132 us
    reduce_scatter x1, waiting for transfers between devices, local(): lax.psum_scatter(product.reshape(images, columns, width).astype(jnp.bfloa...  121 us
    unnamed x6, waiting for transfers between devices  114 us
    all_gather x1, waiting for transfers between devices, local(): lax.all_gather(key_local, 'seq', axis=1, tiled=True)  88.8 us
    psum x1, blocking collectives, local(): squares_all = lax.psum(partial_value, ('seq', 'tensor'))  78.7 us
    all_gather x1, waiting for transfers between devices, local(): lax.all_gather(value_local, 'seq', axis=1, tiled=True)  73.9 us
  transfers between devices with their start and end apart: 5, of which 5 were waited for; matrix products, arithmetic and copies ran while one was open for 9% of the time, Pallas kernels for 0%

commit v1 on v0

v1 whole, which is shorter than its diff:
```python
import functools
import math

import jax
import jax.numpy as jnp
from jax import lax
from jax.experimental import pallas as pl
from jax.experimental.pallas import tpu as pltpu
from jax.sharding import Mesh, PartitionSpec as P

D = 3072
HEADS = 24
HEAD_DIM = 128
F32 = jnp.float32
BF16 = jnp.bfloat16
YH, Z, CORE = 2, 8, 2
SCALE = 1.0 / math.sqrt(HEAD_DIM)


def shift(x, axis, size, by):
    return lax.ppermute(x, axis, [(i, (i + by) % size) for i in range(size)])


def swap(x, axis, size, mask=1):
    return lax.ppermute(x, axis, [(i, i ^ mask) for i in range(size)])


def score_block(key_block, query_block):
    return (
        lax.dot_general(
            key_block, query_block, (((1,), (1,)), ((), ())), preferred_element_type=F32
        )
        * SCALE
    )


def stats_kernel(heads, pieces, *refs):
    q_ref, key_refs, out_ref = refs[0], refs[1 : 1 + pieces], refs[1 + pieces]
    rows = []
    for head in range(heads):
        cols = slice(head * HEAD_DIM, (head + 1) * HEAD_DIM)
        query = q_ref[:, cols]
        top = None
        total = None
        for ref in key_refs:
            scores = score_block(ref[:, cols], query)
            block_top = jnp.max(scores, axis=0, keepdims=True)
            if top is None:
                top = block_top
                total = jnp.sum(jnp.exp(scores - top), axis=0, keepdims=True)
            else:
                new_top = jnp.maximum(top, block_top)
                total = total * jnp.exp(top - new_top) + jnp.sum(
                    jnp.exp(scores - new_top), axis=0, keepdims=True
                )
                top = new_top
        rows.append(top + jnp.log(total))
    rows.append(jnp.zeros((8 - heads, rows[0].shape[1]), F32))
    out_ref[...] = jnp.concatenate(rows, axis=0)


def grad_kernel(heads, slots, z_ref, *refs):
    pieces = len(slots)
    q_ref, da_ref, mine_ref, other_ref = refs[:4]
    key_refs = refs[4 : 4 + pieces]
    dv_ref, att_ref = refs[4 + pieces :]
    width = heads * HEAD_DIM
    here = z_ref[0]
    mine, other = mine_ref[...], other_ref[...]
    top = jnp.maximum(mine, other)
    totals = top + jnp.log(jnp.exp(mine - top) + jnp.exp(other - top))
    for head in range(heads):
        cols = slice(head * HEAD_DIM, (head + 1) * HEAD_DIM)
        value_cols = slice(width + head * HEAD_DIM, width + (head + 1) * HEAD_DIM)
        query = q_ref[:, cols]
        d_attn = da_ref[:, cols]
        row_total = totals[head : head + 1, :]
        attended = None
        for ref, (distance, start) in zip(key_refs, slots):
            scores = score_block(ref[:, cols], query)
            probs = jnp.exp(scores - row_total).astype(BF16)
            d_value = jnp.dot(probs, d_attn, preferred_element_type=F32)
            owner = lax.rem(here + (Z - distance), Z)
            dv_ref[owner, start : start + ref.shape[0], cols] = d_value.astype(BF16)
            part = lax.dot_general(
                ref[:, value_cols], probs, (((0,), (0,)), ((), ())), preferred_element_type=F32
            )
            attended = part if attended is None else attended + part
        att_ref[cols, :] = attended.astype(BF16)


def local(tokens, w_query, w_key, w_value, w_out, cotangent, noise_value, noise_out):
    images, rows, width = tokens.shape
    columns = w_query.shape[1]
    heads = columns // HEAD_DIM
    image = lax.axis_index("yh")
    z = lax.axis_index("z")
    core = lax.axis_index("core")
    flat_tokens = tokens.reshape(images * rows, width)
    flat_cotangent = cotangent.reshape(images * rows, width)
    clip_bound = math.sqrt(2.0 * D * HEADS * HEAD_DIM)

    def project(weight):
        return jnp.dot(flat_tokens, weight, preferred_element_type=F32).astype(BF16)

    def pick(array, index):
        return lax.dynamic_index_in_dim(array, index, 0, keepdims=False)

    def image_rows(array):
        partner = swap(pick(array, 1 - image), "yh", YH)
        return jnp.concatenate([pick(array, image), partner], axis=0)

    def core_order(mine, other, axis=0):
        return jnp.where(
            core == 0,
            jnp.concatenate([mine, other], axis=axis),
            jnp.concatenate([other, mine], axis=axis),
        )

    def both_cores(array):
        return core_order(array, swap(array, "core", CORE))

    keys_values = jnp.concatenate([project(w_key), project(w_value)], axis=1)
    chunk = image_rows(keys_values.reshape(images, rows, 2 * columns))
    forward = backward = chunk
    pieces, slots = [chunk], [(0, 0)]
    for step in range(1, 4):
        forward = shift(forward, "z", Z, 1)
        backward = shift(backward, "z", Z, -1)
        pieces += [forward, backward]
        slots += [(step, 0), (Z - step, 0)]
    half = chunk.shape[0] // 2
    pieces += [shift(forward[:half], "z", Z, 1), shift(backward[half:], "z", Z, -1)]
    slots += [(4, 0), (4, half)]

    d_attn = jnp.einsum("rd,cd->rc", flat_cotangent, w_out, preferred_element_type=F32)
    queries_d = jnp.concatenate([project(w_query), d_attn.astype(BF16)], axis=1)
    queries_d = both_cores(image_rows(queries_d.reshape(images, rows, 2 * columns)))
    queries, d_attn = queries_d[:, :columns], queries_d[:, columns:]

    def half_width(array):
        array = image_rows(array).reshape(2 * rows, 2, width // 2)
        mine = lax.dynamic_index_in_dim(array, core, 1, keepdims=False)
        sent = lax.dynamic_index_in_dim(array, 1 - core, 1, keepdims=False)
        return core_order(mine, swap(sent, "core", CORE))

    tokens_half = half_width(tokens)
    cotangent_half = half_width(cotangent)

    chip_rows = queries.shape[0]
    vmem = pl.BlockSpec(memory_space=pltpu.VMEM)
    stats = pl.pallas_call(
        functools.partial(stats_kernel, heads, len(pieces)),
        out_shape=jax.ShapeDtypeStruct((8, chip_rows), F32),
        in_specs=[vmem] * (1 + len(pieces)),
        out_specs=vmem,
        compiler_params=pltpu.CompilerParams(vmem_limit_bytes=48 * 2**20),
        name="stats",
    )(queries, *pieces)
    other_stats = swap(stats, "core", CORE)
    d_value, attended = pl.pallas_call(
        functools.partial(grad_kernel, heads, tuple(slots)),
        out_shape=(
            jax.ShapeDtypeStruct((Z, 2 * rows, columns), BF16),
            jax.ShapeDtypeStruct((columns, chip_rows), BF16),
        ),
        in_specs=[pl.BlockSpec(memory_space=pltpu.SMEM)] + [vmem] * (4 + len(pieces)),
        out_specs=(vmem, vmem),
        compiler_params=pltpu.CompilerParams(vmem_limit_bytes=48 * 2**20),
        name="grads",
    )(z.reshape(1), queries, d_attn, stats, other_stats, *pieces)

    def scatter(array):
        got = lax.all_to_all(array, "z", 0, 0, tiled=True)
        return jnp.sum(got.astype(F32), axis=0)

    d_value = both_cores(scatter(d_value).astype(BF16))
    attended = (
        attended.astype(F32) + swap(attended, "core", CORE).astype(F32)
    ).astype(BF16)

    per_value = lax.dot_general(
        tokens_half, d_value, (((0,), (0,)), ((), ())), preferred_element_type=F32
    ).astype(BF16)
    per_out = lax.dot_general(
        cotangent_half, attended, (((0,), (1,)), ((), ())), preferred_element_type=F32
    ).astype(BF16)
    out_shard = scatter(per_out.reshape(Z, width // 2 // Z, columns))
    value_shard = scatter(per_value.reshape(Z, width // 2 // Z, columns))

    squares = jnp.sum(jnp.square(value_shard)) + jnp.sum(jnp.square(out_shard))
    squares = jnp.full((8, 128), squares, F32)
    for axis, size, mask in (
        ("core", 2, 1), ("z", 8, 1), ("z", 8, 3), ("z", 8, 7), ("yl", 2, 1), ("x", 4, 1), ("x", 4, 3),
    ):
        squares = squares + swap(squares, axis, size, mask)
    other_squares = swap(squares, "yh", YH)

    def to_factor(total):
        return clip_bound / (jnp.sqrt(total[0, 0]) + 0.01)

    shards = jnp.concatenate([value_shard, out_shard], axis=1)
    shards = shards.reshape(2, shards.shape[0] // 2, 2 * columns)
    pairs = ([(0, 0), (1, 2), (2, 1), (3, 3)], [(0, 1), (1, 3), (2, 0), (3, 2)])
    along = [
        [((s // 2 * Z + k) * 2 + s % 2, (t // 2 * Z + k) * 2 + t % 2) for k in range(Z) for s, t in pair]
        for pair in pairs
    ]
    axes = ("yh", "z", "core")
    of_core = lax.ppermute(pick(shards, image), axes, along[0])
    of_other = lax.ppermute(pick(shards, 1 - image), axes, along[1])
    own_factor, other_factor = to_factor(squares), to_factor(other_squares)
    same = core == image
    weighted = (
        jnp.where(same, own_factor, other_factor) * of_core
        + jnp.where(same, other_factor, own_factor) * of_other
    )
    grad_value = (weighted[:, :columns] + noise_value) / images
    grad_out = (weighted[:, columns:].T + noise_out) / images
    return grad_value, grad_out


def solution(mesh):
    fine = Mesh(mesh.devices.reshape(YH, Z, CORE, 2, 4), ("yh", "z", "core", "yl", "x"))
    seq, tensor = ("yh", "z", "core"), ("yl", "x")
    placed = (
        P(None, seq, None),
        P(None, tensor),
        P(None, tensor),
        P(None, tensor),
        P(tensor, None),
        P(None, seq, None),
        P(seq, tensor),
        P(tensor, seq),
    )
    return jax.shard_map(
        local,
        mesh=fine,
        in_specs=placed,
        out_specs=(P(seq, tensor), P(tensor, seq)),
        check_vma=False,
    )
```

time: 700 us -> 259 us (0.37)
  the two profiles are of different devices: /device:TPU:1 before, /device:TPU:22 now
where the time goes in v1:
time: 259 us; the launch traced here: 254 us
  waiting for transfers between devices  117 us (45%)
  starting transfers between devices  53.5 us (21%)
  local copies, waits for them, and re-layouts  33.3 us (13%)
  other arithmetic  16.2 us (6%)
  matrix products  15.9 us (6%)
  Pallas kernels  13.6 us (5%)
  between operations  4 us (2%)
    ppermute x18, waiting for transfers between devices, swap(): return lax.ppermute(x, axis, [(i, i ^ mask) for i in range(size)])  57.7 us
    all_to_all x3, waiting for transfers between devices, scatter(): got = lax.all_to_all(array, 'z', 0, 0, tiled=True)  39 us
    ppermute x8, waiting for transfers between devices, shift(): return lax.ppermute(x, axis, [(i, (i + by) % size) for i in range(size)])  20.5 us
    all_to_all x3, starting transfers between devices, scatter(): got = lax.all_to_all(array, 'z', 0, 0, tiled=True)  17.3 us
    ppermute x8, starting transfers between devices, shift(): return lax.ppermute(x, axis, [(i, (i + by) % size) for i in range(size)])  16.1 us
    unnamed x56, local copies, waits for them, and re-layouts  15.3 us
    ppermute x18, starting transfers between devices, swap(): return lax.ppermute(x, axis, [(i, i ^ mask) for i in range(size)])  14.8 us
    pallas_call x1, Pallas kernels, local(): pl.pallas_call(functools.partial(grad_kernel, heads, tuple(slots)), out_s...  8.14 us
  transfers between devices with their start and end apart: 31, of which 18 were waited for; matrix products, arithmetic and copies ran while one was open for 18% of the time, Pallas kernels for 0%

profile of v1, /device:TPU:22, one launch (start us, length us, event | category | flops | bytes accessed | tf_op | source)
XLA Modules:
  0.0 253.6 jit_solution(11791478612663904994)
XLA Ops:
  10.2 4.1 %collective-permute-done.4 = bf16[128,768]{1,0:T(8,128)(2,1)S(1)} collective-permute-done((bf16[128,768]{1,0:T(8,128)(2,1)S(1)}, bf16[128,768]{1,0:T(8,128)(2,1)S(1)}, u32[]{:S(2)}, u32[]{:S(2)}) %collective-permute-start.4) | collective-permute-done | bytes 196640 | tf_op jit(solution)/shard_map/ppermute | solution.py:25
  16.3 4.0 %collective-permute-start.6 = (bf16[256,768]{1,0:T(8,128)(2,1)S(1)}, bf16[256,768]{1,0:T(8,128)(2,1)S(1)}, u32[]{:S(2)}, u32[]{:S(2)}) collective-permute-start(bf16[256,768]{1,0:T(8,128)(2,1)S(1)} %pad_maximum_fusion.4.refs_1_.refs_4_), channel_id=1, source_target_pairs={{0,112},{16,0},{32,16},{48,32},{64,48},{80,64},{96,80},{112,96},{1... | collective-permute-start | bytes 1179656 | tf_op jit(solution)/shard_map/ppermute | solution.py:21
  21.8 6.6 %collective-permute-done.5.refs_2_.refs_5_ = bf16[256,768]{1,0:T(8,128)(2,1)S(1)} collective-permute-done((bf16[256,768]{1,0:T(8,128)(2,1)S(1)}, bf16[256,768]{1,0:T(8,128)(2,1)S(1)}, u32[]{:S(2)}, u32[]{:S(2)}) %collective-permute-start.5) | collective-permute-done | bytes 393248 | tf_op jit(solution)/shard_map/ppermute | solution.py:21
  32.6 6.5 %collective-permute-done.7.refs_4_.refs_7_ = bf16[256,768]{1,0:T(8,128)(2,1)} collective-permute-done((bf16[256,768]{1,0:T(8,128)(2,1)S(1)}, bf16[256,768]{1,0:T(8,128)(2,1)}, u32[]{:S(2)}, u32[]{:S(2)}) %collective-permute-start.7) | collective-permute-done | bytes 393248 | tf_op jit(solution)/shard_map/ppermute | solution.py:21
  39.2 3.3 %collective-permute-start.10 = (bf16[256,768]{1,0:T(8,128)(2,1)}, bf16[256,768]{1,0:T(8,128)(2,1)S(1)}, u32[]{:S(2)}, u32[]{:S(2)}) collective-permute-start(bf16[256,768]{1,0:T(8,128)(2,1)} %collective-permute-done.8.refs_5_.refs_8_), channel_id=1, source_target_pairs={{0,112},{16,0},{32,16},{48,32},{64,48},{80,64},{96,80},{112,96},{1... | collective-permute-start | bytes 1179656 | tf_op jit(solution)/shard_map/ppermute | solution.py:21
  44.0 4.9 %collective-permute-done.9.refs_6_.refs_9_ = bf16[256,768]{1,0:T(8,128)(2,1)S(1)} collective-permute-done((bf16[256,768]{1,0:T(8,128)(2,1)}, bf16[256,768]{1,0:T(8,128)(2,1)S(1)}, u32[]{:S(2)}, u32[]{:S(2)}) %collective-permute-start.9) | collective-permute-done | bytes 393248 | tf_op jit(solution)/shard_map/ppermute | solution.py:21
  49.9 3.5 %collective-permute-start.12 = (bf16[128,768]{1,0:T(8,128)(2,1)S(1)}, bf16[128,768]{1,0:T(8,128)(2,1)S(1)}, u32[]{:S(2)}, u32[]{:S(2)}) collective-permute-start(bf16[128,768]{1,0:T(8,128)(2,1)S(1)} %slice.35), channel_id=1, source_target_pairs={{0,112},{16,0},{32,16},{48,32},{64,48},{80,64},{96,80},{112,96},{1... | collective-permute-start | bytes 589832 | tf_op jit(solution)/shard_map/ppermute | solution.py:21
  56.5 5.4 %stats.1.refs_2_ = f32[8,512]{1,0:T(8,128)S(1)} custom-call(bf16[512,384]{1,0:T(8,128)(2,1)S(1)} %get-tuple-element.15.refs_0_, bf16[256,768]{1,0:T(8,128)(2,1)S(1)} %pad_maximum_fusion.4.refs_1_.refs_4_, bf16[256,768]{1,0:T(8,128)(2,1)S(1)} %copy-done.5, bf16[256,768]{1,0:T(8,128)(2,1)S(1)} %copy-done.8, ...), custom_call_target="tpu_custom_call" | custom-call | tf_op jit(solution)/shard_map/stats/pallas_call | solution.py:152
  69.2 8.1 %grads.1 = (bf16[8,256,384]{2,1,0:T(8,128)(2,1)S(1)}, bf16[384,512]{1,0:T(8,128)(2,1)S(1)}) custom-call(s32[1]{0:T(128)} %bitcast.5.z_ref, bf16[512,384]{1,0:T(8,128)(2,1)S(1)} %get-tuple-element.15.refs_0_, bf16[512,384]{1,0:T(8,128)(2,1)S(1)} %copy-done.11, f32[8,512]{1,0:T(8,128)S(1)} %stats.1.refs_2_, f32[8,512]{1,0:T(8,128)} %collective-permute-done.13.refs_3_, ...), custom_call_target="tpu_custom_call" | custom-call | tf_op jit(solution)/shard_map/grads/pallas_call | solution.py:161
  79.3 6.0 %all-to-all-start = ((bf16[8,256,384]{2,1,0:T(8,128)(2,1)}), bf16[8,256,384]{2,1,0:T(8,128)(2,1)}, u32[]{:S(2)}, u32[]{:S(2)}) async-start(bf16[8,256,384]{2,1,0:T(8,128)(2,1)} %copy-done.10), calls=%async_computation | async-start | bytes 3145728 | tf_op jit(solution)/shard_map/all_to_all | solution.py:174
  92.4 19.7 %collective-permute-done.15 = bf16[128,3072]{0,1:T(8,128)(2,1)} collective-permute-done((bf16[128,3072]{0,1:T(8,128)(2,1)}, bf16[128,3072]{0,1:T(8,128)(2,1)}, u32[]{:S(2)}, u32[]{:S(2)}) %collective-permute-start.15) | collective-permute-done | bytes 786464 | tf_op jit(solution)/shard_map/ppermute | solution.py:25
  116.8 9.2 %collective-permute-start.17 = (bf16[384,512]{1,0:T(8,128)(2,1)S(1)}, bf16[384,512]{1,0:T(8,128)(2,1)}, u32[]{:S(2)}, u32[]{:S(2)}) collective-permute-start(bf16[384,512]{1,0:T(8,128)(2,1)S(1)} %copy-done.17), channel_id=1, source_target_pairs={{0,8},{8,0},{1,9},{9,1},{2,10},{10,2},{3,11},{11,3},{4,12},{12,4},... | collective-permute-start | bytes 1179656 | tf_op jit(solution)/shard_map/ppermute | solution.py:25
  129.8 4.2 %convolution_convert_fusion = bf16[1536,384]{1,0:T(8,128)(2,1)} fusion(bf16[256,1536]{1,0:T(8,128)(2,1)} %collective-permute-done.16, bf16[256,1536]{1,0:T(8,128)(2,1)} %bitcast.62, pred[]{:T(512)S(6)} %eq.10, bf16[384,512]{1,0:T(8,128)(2,1)} %collective-permute-done.17, bf16[384,512]{1,0:T(8,128)(2,1)S(1)} %copy-done.17), kind=kOutput, calls=%fused_computation | convolution fusion | flops 612433920 | bytes 3538945 | tf_op jit(solution)/shard_map/dot_general | solution.py:185
  134.0 7.0 %all-to-all-start.2 = ((bf16[8,192,384]{2,1,0:T(8,128)(2,1)}), bf16[8,192,384]{2,1,0:T(8,128)(2,1)S(1)}, u32[]{:S(2)}, u32[]{:S(2)}) async-start(bf16[8,192,384]{2,1,0:T(8,128)(2,1)} %bitcast.55), calls=%async_computation.2 | async-start | bytes 2359296 | tf_op jit(solution)/shard_map/all_to_all | solution.py:174
  143.3 6.2 %collective-permute-done = bf16[128,3072]{0,1:T(8,128)(2,1)} collective-permute-done((bf16[128,3072]{0,1:T(8,128)(2,1)}, bf16[128,3072]{0,1:T(8,128)(2,1)}, u32[]{:S(2)}, u32[]{:S(2)}) %collective-permute-start) | collective-permute-done | bytes 786464 | tf_op jit(solution)/shard_map/ppermute | solution.py:25
  159.8 4.3 %convolution_convert_fusion.1 = bf16[1536,384]{1,0:T(8,128)(2,1)} fusion(bf16[256,1536]{1,0:T(8,128)(2,1)} %collective-permute-done.1, bf16[256,1536]{1,0:T(8,128)(2,1)} %bitcast.61, pred[]{:T(512)S(6)} %eq.10, bf16[256,384]{1,0:T(8,128)(2,1)} %collective-permute-done.14, bf16[256,384]{1,0:T(8,128)(2,1)} %reduce_sum.48), kind=kOutput, calls=%fused_computation.1 | convolution fusion | flops 613416960 | bytes 3145729 | tf_op jit(solution)/shard_map/dot_general | solution.py:182
  164.0 8.5 %all-to-all-done.2 = bf16[8,192,384]{2,1,0:T(8,128)(2,1)S(1)} async-done(((bf16[8,192,384]{2,1,0:T(8,128)(2,1)}), bf16[8,192,384]{2,1,0:T(8,128)(2,1)S(1)}, u32[]{:S(2)}, u32[]{:S(2)}) %all-to-all-start.2) | async-done | bytes 1179680 | tf_op jit(solution)/shard_map/all_to_all | solution.py:174
  172.5 4.3 %all-to-all-start.1 = ((bf16[8,192,384]{2,1,0:T(8,128)(2,1)}), bf16[8,192,384]{2,1,0:T(8,128)(2,1)}, u32[]{:S(2)}, u32[]{:S(2)}) async-start(bf16[8,192,384]{2,1,0:T(8,128)(2,1)} %bitcast.56), calls=%async_computation.1 | async-start | bytes 2359296 | tf_op jit(solution)/shard_map/all_to_all | solution.py:174
  178.3 30.5 %all-to-all-done.1 = bf16[8,192,384]{2,1,0:T(8,128)(2,1)} async-done(((bf16[8,192,384]{2,1,0:T(8,128)(2,1)}), bf16[8,192,384]{2,1,0:T(8,128)(2,1)}, u32[]{:S(2)}, u32[]{:S(2)}) %all-to-all-start.1) | async-done | bytes 1179680 | tf_op jit(solution)/shard_map/all_to_all | solution.py:174
  212.5 5.2 %collective-permute-start.26 = (f32[96,768]{1,0:T(8,128)S(1)}, f32[96,768]{1,0:T(8,128)S(1)}, u32[]{:S(2)}, u32[]{:S(2)}) collective-permute-start(f32[96,768]{1,0:T(8,128)S(1)} %get-tuple-element.16), channel_id=1, source_target_pairs={{0,0},{8,128},{128,8},{136,136},{16,16},{24,144},{144,24},{152,152... | collective-permute-start | bytes 884744 | tf_op jit(solution)/shard_map/ppermute | solution.py:210
  221.5 5.4 %collective-permute-done.20 = f32[8,128]{1,0:T(8,128)S(1)} collective-permute-done((f32[8,128]{1,0:T(8,128)S(1)}, f32[8,128]{1,0:T(8,128)S(1)}, u32[]{:S(2)}, u32[]{:S(2)}) %collective-permute-start.20) | collective-permute-done | bytes 4128 | tf_op jit(solution)/shard_map/ppermute | solution.py:25
  226.9 4.8 %collective-permute-done.21 = f32[8,128]{1,0:T(8,128)S(1)} collective-permute-done((f32[8,128]{1,0:T(8,128)S(1)}, f32[8,128]{1,0:T(8,128)S(1)}, u32[]{:S(2)}, u32[]{:S(2)}) %collective-permute-start.21) | collective-permute-done | bytes 4128 | tf_op jit(solution)/shard_map/ppermute | solution.py:25
  239.4 4.4 %collective-permute-done.24 = f32[8,128]{1,0:T(8,128)S(1)} collective-permute-done((f32[8,128]{1,0:T(8,128)S(1)}, f32[8,128]{1,0:T(8,128)S(1)}, u32[]{:S(2)}, u32[]{:S(2)}) %collective-permute-start.24) | collective-permute-done | bytes 4128 | tf_op jit(solution)/shard_map/ppermute | solution.py:25
  245.3 3.6 %collective-permute-done.25 = f32[8,128]{1,0:T(8,128)S(1)} collective-permute-done((f32[8,128]{1,0:T(8,128)S(1)}, f32[8,128]{1,0:T(8,128)S(1)}, u32[]{:S(2)}, u32[]{:S(2)}) %collective-permute-start.25) | collective-permute-done | bytes 4128 | tf_op jit(solution)/shard_map/ppermute | solution.py:25
  (141 shorter events, 79.8 us)
Async XLA Ops:
  6.0 8.2 %collective-permute-start.4 = (bf16[128,768]{1,0:T(8,128)(2,1)S(1)}, bf16[128,768]{1,0:T(8,128)(2,1)S(1)}, u32[]{:S(2)}, u32[]{:S(2)}) collective-permute-start(bf16[128,768]{1,0:T(8,128)(2,1)S(1)} %get-tuple-element.19), channel_id=1, source_target_pairs={{0,128},{128,0},{1,129},{129,1},{2,130},{130,2},{3,131},{131,3},{4... | collective-permute-start | bytes 589832 | tf_op jit(solution)/shard_map/ppermute | solution.py:25
  14.3 14.2 %collective-permute-start.5 = (bf16[256,768]{1,0:T(8,128)(2,1)S(1)}, bf16[256,768]{1,0:T(8,128)(2,1)S(1)}, u32[]{:S(2)}, u32[]{:S(2)}) collective-permute-start(bf16[256,768]{1,0:T(8,128)(2,1)S(1)} %pad_maximum_fusion.4.refs_1_.refs_4_), channel_id=1, source_target_pairs={{0,16},{16,32},{32,48},{48,64},{64,80},{80,96},{96,112},{112,0},{1... | collective-permute-start | bytes 1179656 | tf_op jit(solution)/shard_map/ppermute | solution.py:21
  16.3 12.2 %collective-permute-start.6 = (bf16[256,768]{1,0:T(8,128)(2,1)S(1)}, bf16[256,768]{1,0:T(8,128)(2,1)S(1)}, u32[]{:S(2)}, u32[]{:S(2)}) collective-permute-start(bf16[256,768]{1,0:T(8,128)(2,1)S(1)} %pad_maximum_fusion.4.refs_1_.refs_4_), channel_id=1, source_target_pairs={{0,112},{16,0},{32,16},{48,32},{64,48},{80,64},{96,80},{112,96},{1... | collective-permute-start | bytes 1179656 | tf_op jit(solution)/shard_map/ppermute | solution.py:21
  21.4 10.3 %collective-permute-start.2 = (bf16[128,768]{1,0:T(8,128)(2,1)S(1)}, bf16[128,768]{1,0:T(8,128)(2,1)S(1)}, u32[]{:S(2)}, u32[]{:S(2)}) collective-permute-start(bf16[128,768]{1,0:T(8,128)(2,1)S(1)} %get-tuple-element.21), channel_id=1, source_target_pairs={{0,128},{128,0},{1,129},{129,1},{2,130},{130,2},{3,131},{131,3},{4... | collective-permute-start | bytes 589832 | tf_op jit(solution)/shard_map/ppermute | solution.py:25
  28.5 10.7 %collective-permute-start.7 = (bf16[256,768]{1,0:T(8,128)(2,1)S(1)}, bf16[256,768]{1,0:T(8,128)(2,1)}, u32[]{:S(2)}, u32[]{:S(2)}) collective-permute-start(bf16[256,768]{1,0:T(8,128)(2,1)S(1)} %collective-permute-done.5.refs_2_.refs_5_), channel_id=1, source_target_pairs={{0,16},{16,32},{32,48},{48,64},{64,80},{80,96},{96,112},{112,0},{1... | collective-permute-start | bytes 1179656 | tf_op jit(solution)/shard_map/ppermute | solution.py:21
  28.5 10.7 %collective-permute-start.8 = (bf16[256,768]{1,0:T(8,128)(2,1)S(1)}, bf16[256,768]{1,0:T(8,128)(2,1)}, u32[]{:S(2)}, u32[]{:S(2)}) collective-permute-start(bf16[256,768]{1,0:T(8,128)(2,1)S(1)} %collective-permute-done.6.refs_3_.refs_6_), channel_id=1, source_target_pairs={{0,112},{16,0},{32,16},{48,32},{64,48},{80,64},{96,80},{112,96},{1... | collective-permute-start | bytes 1179656 | tf_op jit(solution)/shard_map/ppermute | solution.py:21
  32.6 9.9 %collective-permute-start.3 = (bf16[256,768]{1,0:T(8,128)(2,1)}, bf16[256,768]{1,0:T(8,128)(2,1)}, u32[]{:S(2)}, u32[]{:S(2)}) collective-permute-start(bf16[256,768]{1,0:T(8,128)(2,1)} %pad_maximum_fusion.2), channel_id=1, source_target_pairs={{0,8},{8,0},{1,9},{9,1},{2,10},{10,2},{3,11},{11,3},{4,12},{12,4},... | collective-permute-start | bytes 1179656 | tf_op jit(solution)/shard_map/ppermute | solution.py:25
  39.1 9.8 %collective-permute-start.9 = (bf16[256,768]{1,0:T(8,128)(2,1)}, bf16[256,768]{1,0:T(8,128)(2,1)S(1)}, u32[]{:S(2)}, u32[]{:S(2)}) collective-permute-start(bf16[256,768]{1,0:T(8,128)(2,1)} %collective-permute-done.7.refs_4_.refs_7_), channel_id=1, source_target_pairs={{0,16},{16,32},{32,48},{48,64},{64,80},{80,96},{96,112},{112,0},{1... | collective-permute-start | bytes 1179656 | tf_op jit(solution)/shard_map/ppermute | solution.py:21
  39.2 9.9 %collective-permute-start.10 = (bf16[256,768]{1,0:T(8,128)(2,1)}, bf16[256,768]{1,0:T(8,128)(2,1)S(1)}, u32[]{:S(2)}, u32[]{:S(2)}) collective-permute-start(bf16[256,768]{1,0:T(8,128)(2,1)} %collective-permute-done.8.refs_5_.refs_8_), channel_id=1, source_target_pairs={{0,112},{16,0},{32,16},{48,32},{64,48},{80,64},{96,80},{112,96},{1... | collective-permute-start | bytes 1179656 | tf_op jit(solution)/shard_map/ppermute | solution.py:21
  49.0 7.0 %collective-permute-start.11 = (bf16[128,768]{1,0:T(8,128)(2,1)S(1)}, bf16[128,768]{1,0:T(8,128)(2,1)S(1)}, u32[]{:S(2)}, u32[]{:S(2)}) collective-permute-start(bf16[128,768]{1,0:T(8,128)(2,1)S(1)} %slice.34), channel_id=1, source_target_pairs={{0,16},{16,32},{32,48},{48,64},{64,80},{80,96},{96,112},{112,0},{1... | collective-permute-start | bytes 589832 | tf_op jit(solution)/shard_map/ppermute | solution.py:21
  49.9 6.6 %collective-permute-start.12 = (bf16[128,768]{1,0:T(8,128)(2,1)S(1)}, bf16[128,768]{1,0:T(8,128)(2,1)S(1)}, u32[]{:S(2)}, u32[]{:S(2)}) collective-permute-start(bf16[128,768]{1,0:T(8,128)(2,1)S(1)} %slice.35), channel_id=1, source_target_pairs={{0,112},{16,0},{32,16},{48,32},{64,48},{80,64},{96,80},{112,96},{1... | collective-permute-start | bytes 589832 | tf_op jit(solution)/shard_map/ppermute | solution.py:21
  79.3 54.7 %all-to-all-start = ((bf16[8,256,384]{2,1,0:T(8,128)(2,1)}), bf16[8,256,384]{2,1,0:T(8,128)(2,1)}, u32[]{:S(2)}, u32[]{:S(2)}) async-start(bf16[8,256,384]{2,1,0:T(8,128)(2,1)} %copy-done.10), calls=%async_computation | async-start | bytes 3145728 | tf_op jit(solution)/shard_map/all_to_all | solution.py:174
  90.9 21.2 %collective-permute-start.15 = (bf16[128,3072]{0,1:T(8,128)(2,1)}, bf16[128,3072]{0,1:T(8,128)(2,1)}, u32[]{:S(2)}, u32[]{:S(2)}) collective-permute-start(bf16[128,3072]{0,1:T(8,128)(2,1)} %bitcast.58), channel_id=1, source_target_pairs={{0,128},{128,0},{1,129},{129,1},{2,130},{130,2},{3,131},{131,3},{4... | collective-permute-start | bytes 2359304 | tf_op jit(solution)/shard_map/ppermute | solution.py:25
  116.8 13.0 %collective-permute-start.16 = (bf16[256,1536]{1,0:T(8,128)(2,1)}, bf16[256,1536]{1,0:T(8,128)(2,1)}, u32[]{:S(2)}, u32[]{:S(2)}) collective-permute-start(bf16[256,1536]{1,0:T(8,128)(2,1)} %bitcast.59), channel_id=1, source_target_pairs={{0,8},{8,0},{1,9},{9,1},{2,10},{10,2},{3,11},{11,3},{4,12},{12,4},... | collective-permute-start | bytes 2359304 | tf_op jit(solution)/shard_map/ppermute | solution.py:25
  116.8 13.0 %collective-permute-start.17 = (bf16[384,512]{1,0:T(8,128)(2,1)S(1)}, bf16[384,512]{1,0:T(8,128)(2,1)}, u32[]{:S(2)}, u32[]{:S(2)}) collective-permute-start(bf16[384,512]{1,0:T(8,128)(2,1)S(1)} %copy-done.17), channel_id=1, source_target_pairs={{0,8},{8,0},{1,9},{9,1},{2,10},{10,2},{3,11},{11,3},{4,12},{12,4},... | collective-permute-start | bytes 1179656 | tf_op jit(solution)/shard_map/ppermute | solution.py:25
  128.3 21.3 %collective-permute-start = (bf16[128,3072]{0,1:T(8,128)(2,1)}, bf16[128,3072]{0,1:T(8,128)(2,1)}, u32[]{:S(2)}, u32[]{:S(2)}) collective-permute-start(bf16[128,3072]{0,1:T(8,128)(2,1)} %bitcast.57), channel_id=1, source_target_pairs={{0,128},{128,0},{1,129},{129,1},{2,130},{130,2},{3,131},{131,3},{4... | collective-permute-start | bytes 2359304 | tf_op jit(solution)/shard_map/ppermute | solution.py:25
  134.0 38.5 %all-to-all-start.2 = ((bf16[8,192,384]{2,1,0:T(8,128)(2,1)}), bf16[8,192,384]{2,1,0:T(8,128)(2,1)S(1)}, u32[]{:S(2)}, u32[]{:S(2)}) async-start(bf16[8,192,384]{2,1,0:T(8,128)(2,1)} %bitcast.55), calls=%async_computation.2 | async-start | bytes 2359296 | tf_op jit(solution)/shard_map/all_to_all | solution.py:174
  154.6 5.2 %collective-permute-start.1 = (bf16[256,1536]{1,0:T(8,128)(2,1)}, bf16[256,1536]{1,0:T(8,128)(2,1)}, u32[]{:S(2)}, u32[]{:S(2)}) collective-permute-start(bf16[256,1536]{1,0:T(8,128)(2,1)} %bitcast.60), channel_id=1, source_target_pairs={{0,8},{8,0},{1,9},{9,1},{2,10},{10,2},{3,11},{11,3},{4,12},{12,4},... | collective-permute-start | bytes 2359304 | tf_op jit(solution)/shard_map/ppermute | solution.py:25
  172.5 36.3 %all-to-all-start.1 = ((bf16[8,192,384]{2,1,0:T(8,128)(2,1)}), bf16[8,192,384]{2,1,0:T(8,128)(2,1)}, u32[]{:S(2)}, u32[]{:S(2)}) async-start(bf16[8,192,384]{2,1,0:T(8,128)(2,1)} %bitcast.56), calls=%async_computation.1 | async-start | bytes 2359296 | tf_op jit(solution)/shard_map/all_to_all | solution.py:174
  212.3 5.5 %collective-permute-start.18 = (f32[8,128]{1,0:T(8,128)S(1)}, f32[8,128]{1,0:T(8,128)S(1)}, u32[]{:S(2)}, u32[]{:S(2)}) collective-permute-start(f32[8,128]{1,0:T(8,128)S(1)} %broadcast_in_dim.3), channel_id=1, source_target_pairs={{0,8},{8,0},{1,9},{9,1},{2,10},{10,2},{3,11},{11,3},{4,12},{12,4},... | collective-permute-start | bytes 12296 | tf_op jit(solution)/shard_map/ppermute | solution.py:25
  212.5 37.7 %collective-permute-start.26 = (f32[96,768]{1,0:T(8,128)S(1)}, f32[96,768]{1,0:T(8,128)S(1)}, u32[]{:S(2)}, u32[]{:S(2)}) collective-permute-start(f32[96,768]{1,0:T(8,128)S(1)} %get-tuple-element.16), channel_id=1, source_target_pairs={{0,0},{8,128},{128,8},{136,136},{16,16},{24,144},{144,24},{152,152... | collective-permute-start | bytes 884744 | tf_op jit(solution)/shard_map/ppermute | solution.py:210
  217.7 32.5 %collective-permute-start.27 = (f32[96,768]{1,0:T(8,128)S(1)}, f32[96,768]{1,0:T(8,128)S(1)}, u32[]{:S(2)}, u32[]{:S(2)}) collective-permute-start(f32[96,768]{1,0:T(8,128)S(1)} %get-tuple-element.17), channel_id=1, source_target_pairs={{0,8},{8,136},{128,0},{136,128},{16,24},{24,152},{144,16},{152,144... | collective-permute-start | bytes 884744 | tf_op jit(solution)/shard_map/ppermute | solution.py:211
  221.5 5.4 %collective-permute-start.20 = (f32[8,128]{1,0:T(8,128)S(1)}, f32[8,128]{1,0:T(8,128)S(1)}, u32[]{:S(2)}, u32[]{:S(2)}) collective-permute-start(f32[8,128]{1,0:T(8,128)S(1)} %fusion.36), channel_id=1, source_target_pairs={{0,48},{16,32},{32,16},{48,0},{64,112},{80,96},{96,80},{112,64},{1... | collective-permute-start | bytes 12296 | tf_op jit(solution)/shard_map/ppermute | solution.py:25
  243.8 5.1 %collective-permute-start.25 = (f32[8,128]{1,0:T(8,128)S(1)}, f32[8,128]{1,0:T(8,128)S(1)}, u32[]{:S(2)}, u32[]{:S(2)}) collective-permute-start(f32[8,128]{1,0:T(8,128)S(1)} %add.84), channel_id=1, source_target_pairs={{0,128},{128,0},{1,129},{129,1},{2,130},{130,2},{3,131},{131,3},{4... | collective-permute-start | bytes 12296 | tf_op jit(solution)/shard_map/ppermute | solution.py:25
  (34 other events, 192.1 us)

commit v2 on v0

v2 whole, which is shorter than its diff:
```python
import functools
import math

import jax
import jax.numpy as jnp
from jax import lax
from jax.experimental import pallas as pl
from jax.experimental.pallas import tpu as pltpu
from jax.sharding import Mesh, PartitionSpec as P

D = 3072
HEADS = 24
HEAD_DIM = 128
F32 = jnp.float32
BF16 = jnp.bfloat16
YH, Z, CORE = 2, 8, 2
SMALL, LARGE = 24 * 2**20, 60 * 2**20
SCALE = 1.0 / math.sqrt(HEAD_DIM)


def shift(x, axis, size, by):
    return lax.ppermute(x, axis, [(i, (i + by) % size) for i in range(size)])


def swap(x, axis, size, mask=1):
    return lax.ppermute(x, axis, [(i, i ^ mask) for i in range(size)])


def head_cols(head):
    return slice(head * HEAD_DIM, (head + 1) * HEAD_DIM)


def log_add(left, right):
    top = jnp.maximum(left, right)
    return top + jnp.log(jnp.exp(left - top) + jnp.exp(right - top))


class Arriving:
    def __init__(self, source, target, sem):
        self.copy = pltpu.make_async_copy(source, target, sem)
        self.target, self.here = target, False
        self.copy.start()

    def ref(self):
        if not self.here:
            self.copy.wait()
            self.here = True
        return self.target

    def __getitem__(self, at):
        return self.ref()[at]


class Leaving:
    def __init__(self, source, target, sem):
        self.copy = pltpu.make_async_copy(source, target, sem)
        self.ref, self.sent = source, False

    def send(self):
        if not self.sent:
            self.copy.start()
            self.sent = True


def call(body, name, scalars, inputs, outputs, views=None, vmem=SMALL):
    views = views or {}
    n_scalars, n_inputs, n_outputs = len(scalars), len(inputs), len(outputs)
    shapes = [views[at][0] if at in views else x.shape for at, x in enumerate(inputs)]

    def kernel(*refs):
        numbers, refs = refs[:n_scalars], refs[n_scalars:]
        sources, refs = refs[:n_inputs], refs[n_inputs:]
        targets, refs = refs[:n_outputs], refs[n_outputs:]
        in_sems, out_sems = refs[-2:]
        numbers = [ref[0] for ref in numbers]
        arriving = []
        for at, source in enumerate(sources):
            if at in views:
                source = source.at[views[at][1](*numbers)]
            arriving.append(Arriving(source, refs[at], in_sems.at[at]))
        leaving = [
            Leaving(refs[n_inputs + at], target, out_sems.at[at])
            for at, target in enumerate(targets)
        ]
        body(numbers, arriving, leaving)
        for one in arriving:
            one.ref()
        for one in leaving:
            one.send()
        for one in leaving:
            one.copy.wait()

    hbm = pl.BlockSpec(memory_space=pltpu.HBM)
    smem = pl.BlockSpec(memory_space=pltpu.SMEM)
    return pl.pallas_call(
        kernel,
        out_shape=tuple(outputs),
        in_specs=[smem] * n_scalars + [hbm] * n_inputs,
        out_specs=(hbm,) * n_outputs,
        scratch_shapes=[pltpu.VMEM(size, x.dtype) for size, x in zip(shapes, inputs)]
        + [pltpu.VMEM(x.shape, x.dtype) for x in outputs]
        + [pltpu.SemaphoreType.DMA((n_inputs,)), pltpu.SemaphoreType.DMA((n_outputs,))],
        compiler_params=pltpu.CompilerParams(vmem_limit_bytes=vmem),
        cost_estimate=pl.CostEstimate(flops=1000, bytes_accessed=0, transcendentals=0),
        name=name,
    )(*scalars, *inputs)


def score_block(key_block, query_block):
    last = (((1,), (1,)), ((), ()))
    return lax.dot_general(key_block, query_block, last, preferred_element_type=F32) * SCALE


def stats_body(heads, pieces, numbers, arriving, leaving):
    query, keys, carried = arriving[0], arriving[1 : 1 + pieces], arriving[1 + pieces :]
    rows = []
    for head in range(heads):
        cols = head_cols(head)
        blocks = [score_block(key[:, cols], query[:, cols]) for key in keys]
        tops = [jnp.max(scores, axis=0, keepdims=True) for scores in blocks]
        top = functools.reduce(jnp.maximum, tops)
        total = sum(jnp.sum(jnp.exp(scores - top), axis=0, keepdims=True) for scores in blocks)
        rows.append(top + jnp.log(total))
    rows.append(jnp.zeros((8 - heads, rows[0].shape[1]), F32))
    found = jnp.concatenate(rows, axis=0)
    for one in carried:
        found = log_add(found, one[...])
    leaving[0].ref[...] = found


def both_totals(mine, other):
    other = other[...]
    half = other.shape[1] // 2
    other = jnp.concatenate([other[:, half:], other[:, :half]], axis=1)
    return log_add(mine[...], other)


def d_value_body(heads, slots, numbers, arriving, leaving):
    (here,) = numbers
    query, d_attn, mine, other = arriving[:4]
    keys, pieces = arriving[4:], len(slots)
    out, kept = leaving[0], leaving[1:]
    totals = both_totals(mine, other)

    def scores(head, piece):
        cols = head_cols(head)
        return score_block(keys[piece][:, cols], query[:, cols])

    order = [(head, piece) for head in range(heads) for piece in range(pieces)]
    ahead = scores(*order[0])
    for at, (head, piece) in enumerate(order):
        block = ahead
        if at + 1 < len(order):
            ahead = scores(*order[at + 1])
        cols = head_cols(head)
        probs = jnp.exp(block - totals[head : head + 1, :]).astype(BF16)
        kept[piece].ref[head] = probs
        d_value = jnp.dot(probs, d_attn[:, cols], preferred_element_type=F32)
        distance, start = slots[piece]
        owner = lax.rem(here + (Z - distance), Z)
        out.ref[owner, start : start + probs.shape[0], cols] = d_value.astype(BF16)
        if head == heads - 1:
            kept[piece].send()


def attend_body(heads, numbers, arriving, leaving):
    pieces = len(arriving) // 2
    probs, values, (out,) = arriving[:pieces], arriving[pieces:], leaving
    half = out.ref.shape[2]
    first = (((0,), (0,)), ((), ()))
    for head in range(heads):
        cols = head_cols(head)
        attended = jnp.zeros((HEAD_DIM, 2 * half), F32)
        for prob, value in zip(probs, values):
            attended += lax.dot_general(
                value[:, cols], prob[head], first, preferred_element_type=F32
            )
        out.ref[0, cols, :] = attended[:, :half].astype(BF16)
        out.ref[1, cols, :] = attended[:, half:].astype(BF16)


def turn_body(numbers, arriving, leaving):
    core, _ = numbers
    keep, send = leaving
    for at, one in enumerate(arriving):
        array = one[...]
        rows, width = array.shape
        low, high = array[:, : width // 2].T, array[:, width // 2 :].T
        to = slice(at * rows, (at + 1) * rows)
        keep.ref[:, to] = jnp.where(core == 0, low, high)
        send.ref[:, to] = jnp.where(core == 0, high, low)


def value_grad_body(numbers, arriving, leaving):
    (here,) = numbers
    mine, other, dv_mine, dv_other = [one.ref() for one in arriving]
    rows = leaving[0].ref.shape[1]
    for output, part, ahead, start, count in (
        (2, 0, 4, 0, rows // 2),
        (3, 0, 4, rows // 2, rows // 2),
        (0, 0, 1, 0, rows),
        (0, 1, 3, 0, rows),
        (1, 0, 7, 0, rows),
        (1, 1, 5, 0, rows),
        (4, 0, 2, 0, rows),
        (5, 0, 6, 0, rows),
        (6, 0, 0, 0, rows),
    ):
        first = lax.rem(here + ahead, Z) * rows + start
        at = pl.ds(pl.multiple_of(first, rows // 2), count)
        product = jnp.dot(mine[at, :], dv_mine[...], preferred_element_type=F32)
        product += jnp.dot(other[at, :], dv_other[...], preferred_element_type=F32)
        leaving[output].ref[part] = product.astype(BF16)
        if part == leaving[output].ref.shape[0] - 1:
            leaving[output].send()


def out_grad_body(numbers, arriving, leaving):
    mine, other, att, att_other = arriving
    (out,) = leaving
    att_mine = (att[0].astype(F32) + att_other[1].astype(F32)).astype(BF16)
    att_rest = (att[1].astype(F32) + att_other[0].astype(F32)).astype(BF16)
    last = (((1,), (1,)), ((), ()))
    rows = out.ref.shape[0] // Z
    for part in range(Z):
        at = slice(part * rows, (part + 1) * rows)
        product = lax.dot_general(mine[at, :], att_mine, last, preferred_element_type=F32)
        product += lax.dot_general(other[at, :], att_rest, last, preferred_element_type=F32)
        out.ref[at, :] = product.astype(BF16)


def relay_body(numbers, arriving, leaving):
    near_f, near_b, far_f, far_b, keep_f, keep_b = arriving
    half = far_f.ref().shape[1]
    for near, far, keep, send, low in (
        (near_f, far_f, keep_f, leaving[0], 0),
        (near_b, far_b, keep_b, leaving[1], half),
    ):
        at, rest = slice(low, low + half), slice(half - low, 2 * half - low)
        through = near[1, at, :].astype(F32) + far[0].astype(F32)
        send.ref[0, at, :] = (keep[0, at, :].astype(F32) + through).astype(BF16)
        through = near[1, rest, :].astype(F32)
        send.ref[0, rest, :] = (keep[0, rest, :].astype(F32) + through).astype(BF16)
        send.send()


def total_of(own, near_f, near_b, last_f, last_b):
    near = near_f[0].astype(F32) + near_b[0].astype(F32)
    return own[0].astype(F32) + near + (last_f[0].astype(F32) + last_b[0].astype(F32))


def sum_body(numbers, arriving, leaving):
    total = sum(arriving[0][part].astype(F32) for part in range(Z))
    leaving[0].ref[...] = total.astype(BF16)


def shard_body(numbers, arriving, leaving):
    out, *terms = arriving
    shard, square_out = leaving
    columns = shard.ref.shape[1] // 2
    square = jnp.zeros((1, 1), F32)
    for total, at in ((out[...].astype(F32), columns), (total_of(*terms), 0)):
        shard.ref[:, at : at + columns] = total.astype(BF16)
        column_sums = jnp.sum(total * total, axis=0, keepdims=True)
        square += jnp.sum(column_sums, axis=1, keepdims=True)
    square_out.ref[...] = jnp.broadcast_to(square.reshape(1, 1, 1), square_out.ref.shape)


def sum_parts(parts, first, count):
    return functools.reduce(jnp.add, [parts[first + at] for at in range(count)])


def square_body(numbers, arriving, leaving):
    total = sum_parts(arriving[0], 0, Z * CORE)
    leaving[0].ref[...] = jnp.broadcast_to(total[None], leaving[0].ref.shape)


def final_body(numbers, arriving, leaving):
    (core,) = numbers
    squares, near, far, noise_value, noise_out = arriving
    value, out = leaving
    columns = value.ref.shape[1]
    clip_bound = math.sqrt(2.0 * D * HEADS * HEAD_DIM)
    factors = []
    for image in range(YH):
        total = sum_parts(squares, image * 8, 8)[0:1, 0:1]
        factors.append(clip_bound / (jnp.sqrt(total) + 0.01))
    near_factor = jnp.where(core == 0, factors[0], factors[1])
    far_factor = jnp.where(core == 0, factors[1], factors[0])
    weighted = near_factor * near[...].astype(F32) + far_factor * far[...].astype(F32)
    value.ref[...] = (weighted[:, :columns] + noise_value[...]) * 0.5
    out.ref[...] = (weighted[:, columns:].T + noise_out[...]) * 0.5


def local(tokens, w_query, w_key, w_value, w_out, cotangent, noise_value, noise_out):
    images, rows, width = tokens.shape
    columns = w_query.shape[1]
    heads = columns // HEAD_DIM
    image = lax.axis_index("yh")
    z = lax.axis_index("z")
    core = lax.axis_index("core")
    flat_tokens = tokens.reshape(images * rows, width)
    flat_cotangent = cotangent.reshape(images * rows, width)
    shape = jax.ShapeDtypeStruct
    here, this_core, this_image = z.reshape(1), core.reshape(1), image.reshape(1)

    def project(weight):
        return jnp.dot(flat_tokens, weight, preferred_element_type=F32).astype(BF16)

    def pick(array, index):
        return lax.dynamic_index_in_dim(array, index, 0, keepdims=False)

    def image_rows(array):
        array = array.reshape(images, rows, array.shape[1])
        partner = swap(pick(array, 1 - image), "yh", YH)
        return jnp.concatenate([pick(array, image), partner], axis=0)

    def from_partner(array):
        return lax.all_gather(pick(array, 1 - image), "yh", axis=0)

    keys_values = jnp.concatenate([project(w_key), project(w_value)], axis=1)
    cotangent_pair = cotangent, from_partner(cotangent)
    chunk = image_rows(keys_values)
    d_attn = jnp.einsum("rd,cd->rc", flat_cotangent, w_out, preferred_element_type=F32)
    queries_d = jnp.concatenate([project(w_query), d_attn.astype(BF16)], axis=1)
    chunk, queries_d, late_tokens = lax.optimization_barrier((chunk, queries_d, tokens))
    queries_d = image_rows(queries_d)
    tokens_pair = tokens, from_partner(late_tokens)
    queries_d = jnp.concatenate([queries_d, swap(queries_d, "core", CORE)], axis=0)
    chip_rows = queries_d.shape[0]

    def stats_of(chosen, *carried):
        (found,) = call(
            functools.partial(stats_body, heads, len(chosen)),
            "stats",
            (),
            (queries_d, *chosen, *carried),
            (shape((8, chip_rows), F32),),
            {at: left_part(x) for at, x in enumerate((queries_d, *chosen))},
        )
        return found

    def left_part(x):
        return (x.shape[0], columns), lambda *_: (slice(None), slice(0, columns))

    def right_part(x):
        return (x.shape[0], columns), lambda *_: (slice(None), slice(columns, 2 * columns))

    forward = backward = chunk
    pieces = [chunk]
    for step in range(1, 4):
        forward = shift(forward, "z", Z, 1)
        backward = shift(backward, "z", Z, -1)
        pieces += [forward, backward]
        if step == 3:
            stats = stats_of(pieces[:3])
            forward, backward, stats = lax.optimization_barrier((forward, backward, stats))
    half = chunk.shape[0] // 2
    pieces += [shift(forward[:half], "z", Z, 1), shift(backward[half:], "z", Z, -1)]
    stats = stats_of(pieces[3:7], stats)
    stats = stats_of(pieces[7:], stats)
    other_stats = swap(stats, "core", CORE)

    def block(parts, count):
        return shape((parts, count, columns), BF16)

    def start_scatter(near_f, near_b, far_f, far_b):
        return (
            shift(near_f, "z", Z, 1),
            shift(near_b, "z", Z, -1),
            shift(far_f, "z", Z, 2),
            shift(far_b, "z", Z, -2),
        )

    def relay(arrived, keep_f, keep_b):
        like = shape(keep_f.shape, BF16)
        return call(relay_body, "relay", (), (*arrived, keep_f, keep_b), (like, like))

    def end_scatter(arrived, sums, own):
        return own, arrived[0], arrived[1], shift(sums[0], "z", Z, 2), shift(sums[1], "z", Z, -2)

    slots = ((0, 0), (1, 0), (7, 0), (2, 0), (6, 0), (3, 0), (5, 0), (4, 0), (4, half))
    inputs = (queries_d, queries_d, stats, other_stats, *pieces)
    views = {at: left_part(inputs[at]) for at in (0, *range(4, len(inputs)))}
    d_value, *probs = call(
        functools.partial(d_value_body, heads, slots),
        "d_value",
        (here,),
        inputs,
        (block(Z, 2 * rows),) + tuple(shape((heads, x.shape[0], chip_rows), BF16) for x in pieces),
        {**views, 1: right_part(queries_d)},
        LARGE,
    )
    d_value, probs, cotangent_pair = lax.optimization_barrier((d_value, probs, cotangent_pair))
    terms = lax.all_to_all(d_value, "z", 0, 0, tiled=True)
    (attended,) = call(
        functools.partial(attend_body, heads),
        "attend",
        (),
        (*probs, *pieces),
        (shape((2, columns, chip_rows // 2), BF16),),
        {len(pieces) + at: right_part(x) for at, x in enumerate(pieces)},
        LARGE,
    )
    attended_other = swap(attended, "core", CORE)
    attended, tokens_pair = lax.optimization_barrier((attended, tokens_pair))

    def half_width(pair):
        turned = shape((width // 2, 2 * rows), BF16)
        keep, send = call(
            turn_body,
            "turn",
            (this_core, this_image),
            pair,
            (turned, turned),
            {
                0: ((rows, width), lambda core, image: image),
                1: ((rows, width), lambda core, image: 1 - image),
            },
            LARGE,
        )
        return keep, swap(send, "core", CORE)

    cotangent_half = half_width(cotangent_pair)
    tokens_half = half_width(tokens_pair)
    (per_out,) = call(
        out_grad_body,
        "per_out",
        (),
        (*cotangent_half, attended, attended_other),
        (shape((width // 2, columns), BF16),),
        vmem=LARGE,
    )
    out_shard = lax.psum_scatter(per_out, "z", scatter_dimension=0, tiled=True)

    (d_value,) = call(sum_body, "d_value_sum", (), (terms,), (shape((2 * rows, columns), BF16),))
    count = width // 2 // Z
    parts = call(
        value_grad_body,
        "per_value",
        (here,),
        (*tokens_half, d_value, swap(d_value, "core", CORE)),
        (block(2, count), block(2, count), block(1, count // 2), block(1, count // 2)) + (block(1, count),) * 3,
        vmem=LARGE,
    )
    arrived = start_scatter(*parts[:4])
    terms = end_scatter(arrived, relay(arrived, *parts[4:6]), parts[6])
    small = shape((Z * CORE, 8, 128), F32)
    shard, square = call(
        shard_body,
        "shards",
        (),
        (out_shard, *terms),
        (shape((count, 2 * columns), BF16), small),
        vmem=LARGE,
    )

    halves = shard.reshape(2, count // 2, 2 * columns)
    pairs = ([(0, 0), (1, 2), (2, 1), (3, 3)], [(0, 1), (1, 3), (2, 0), (3, 2)])
    along = [
        [((s // 2 * Z + k) * 2 + s % 2, (t // 2 * Z + k) * 2 + t % 2) for k in range(Z) for s, t in pair]
        for pair in pairs
    ]
    axes = ("yh", "z", "core")
    near = lax.ppermute(pick(halves, image), axes, along[0])
    far = lax.ppermute(pick(halves, 1 - image), axes, along[1])

    squares = lax.all_to_all(square, ("z", "core"), 0, 0, tiled=True)
    (squares,) = call(square_body, "squares", (), (squares,), (small,))
    squares = lax.all_to_all(squares, ("yh", "yl", "x"), 0, 0, tiled=True)
    return call(
        final_body,
        "final",
        (this_core,),
        (squares, near, far, noise_value, noise_out),
        (shape(noise_value.shape, F32), shape(noise_out.shape, F32)),
    )


def solution(mesh):
    fine = Mesh(mesh.devices.reshape(YH, Z, CORE, 2, 4), ("yh", "z", "core", "yl", "x"))
    seq, tensor = ("yh", "z", "core"), ("yl", "x")
    placed = (
        P(None, seq, None),
        P(None, tensor),
        P(None, tensor),
        P(None, tensor),
        P(tensor, None),
        P(None, seq, None),
        P(seq, tensor),
        P(tensor, seq),
    )
    return jax.shard_map(
        local,
        mesh=fine,
        in_specs=placed,
        out_specs=(P(seq, tensor), P(tensor, seq)),
        check_vma=False,
    )
```

time: 700 us -> 214 us (0.31)
  waiting for transfers between devices: 529 us -> 77 us
  blocking collectives: 78.7 us -> 0 us
  starting transfers between devices: 0.39 us -> 57 us
  Pallas kernels: 0 us -> 42.6 us
  matrix products: 37.2 us -> 7.78 us
  local copies, waits for them, and re-layouts: 29.8 us -> 12.7 us
  other arithmetic: 10 us -> 2.19 us
    reduce_scatter x2 -> x1, waiting for transfers between devices: 253 us -> 0.01 us  [local(): out_shard = lax.psum_scatter(per_out, 'z', scatter_dimension=0, tiled=True)]
    all_gather x2, waiting for transfers between devices: 163 us -> 0.03 us  [from_partner(): return lax.all_gather(pick(array, 1 - image), 'yh', axis=0)]
    unnamed x6 -> x3, waiting for transfers between devices: 114 us -> 0.05 us
    psum x1 -> x0, blocking collectives: 78.7 us -> none  [local(): squares_all = lax.psum(partial_value, ('seq', 'tensor'))]
    ppermute x0 -> x24, waiting for transfers between devices: none -> 44.9 us  [the longest x14 30.4 us: shift(): return lax.ppermute(x, axis, [(i, (i + by) % size) for i in range(size)])]
    pallas_call x0 -> x14, Pallas kernels: none -> 42.6 us  [call(): pl.pallas_call(kernel, out_shape=tuple(outputs), in_specs=[smem] * n_scal...]
    ppermute x0 -> x24, starting transfers between devices: none -> 40 us  [the longest x14 24.1 us: shift(): return lax.ppermute(x, axis, [(i, (i + by) % size) for i in range(size)])]
    all_to_all x0 -> x3, waiting for transfers between devices: none -> 32.1 us  [the longest x1 22.3 us: local(): terms = lax.all_to_all(d_value, 'z', 0, 0, tiled=True)]
  transfers between devices with their start and end apart: 5 -> 30, of which waited for: 5 -> 13; matrix products, arithmetic and copies ran while one was open for 9% -> 5% of each run, Pallas kernels for 0% -> 18%
where the time goes in v2:
time: 214 us
  waiting for transfers between devices  77 us (36%)
  starting transfers between devices  57 us (27%)
  Pallas kernels  42.6 us (20%)
  between operations  14.3 us (7%)
  local copies, waits for them, and re-layouts  12.7 us (6%)
  matrix products  7.78 us (4%)
  other arithmetic  2.19 us (1%)
    pallas_call x14, Pallas kernels, call(): pl.pallas_call(kernel, out_shape=tuple(outputs), in_specs=[smem] * n_scal...  42.6 us
    ppermute x14, waiting for transfers between devices, shift(): return lax.ppermute(x, axis, [(i, (i + by) % size) for i in range(size)])  30.4 us
    ppermute x14, starting transfers between devices, shift(): return lax.ppermute(x, axis, [(i, (i + by) % size) for i in range(size)])  24.1 us
    all_to_all x1, waiting for transfers between devices, local(): terms = lax.all_to_all(d_value, 'z', 0, 0, tiled=True)  22.3 us
    ppermute x8, waiting for transfers between devices, swap(): return lax.ppermute(x, axis, [(i, i ^ mask) for i in range(size)])  14.5 us
    ppermute x8, starting transfers between devices, swap(): return lax.ppermute(x, axis, [(i, i ^ mask) for i in range(size)])  12.5 us
    unnamed x63, local copies, waits for them, and re-layouts  7 us
    dot_general x3, matrix products, project(): return jnp.dot(flat_tokens, weight, preferred_element_type=F32).astype(BF16)  6.78 us
  transfers between devices with their start and end apart: 30, of which 13 were waited for; matrix products, arithmetic and copies ran while one was open for 5% of the time, Pallas kernels for 18%

profile of v2, /device:TPU:1, one launch (start us, length us, event | category | flops | bytes accessed | tf_op | source)
XLA Modules:
  0.0 213.6 jit_solution(4522109025837428994)
XLA Ops:
  12.5 3.8 %collective-permute-start = (bf16[128,768]{1,0:T(8,128)(2,1)S(1)}, bf16[128,768]{1,0:T(8,128)(2,1)S(1)}, u32[]{:S(2)}, u32[]{:S(2)}) collective-permute-start(bf16[128,768]{1,0:T(8,128)(2,1)S(1)} %get-tuple-element.101), channel_id=1, source_target_pairs={{0,128},{128,0},{1,129},{129,1},{2,130},{130,2},{3,131},{131,3},{4... | collective-permute-start | bytes 589832 | tf_op jit(solution)/shard_map/ppermute | solution.py:26
  17.4 3.3 %convolution_convert_fusion.1 = bf16[256,384]{1,0:T(8,128)(2,1)S(1)} fusion(bf16[256,3072]{1,0:T(8,128)(2,1)} %bitcast.30, bf16[3072,384]{1,0:T(8,128)(2,1)} %param.9), kind=kOutput, calls=%fused_computation.1 | convolution fusion | flops 604078080 | bytes 4128768 | tf_op jit(solution)/shard_map/dot_general | solution.py:308
  23.6 4.0 %collective-permute-start.6 = (bf16[256,768]{1,0:T(8,128)(2,1)S(1)}, bf16[256,768]{1,0:T(8,128)(2,1)S(1)}, u32[]{:S(2)}, u32[]{:S(2)}) collective-permute-start(bf16[256,768]{1,0:T(8,128)(2,1)S(1)} %pad_maximum_fusion.2.refs_1_.refs_5_.refs_9_), channel_id=1, source_target_pairs={{0,112},{16,0},{32,16},{48,32},{64,48},{80,64},{96,80},{112,96},{1... | collective-permute-start | bytes 1179656 | tf_op jit(solution)/shard_map/ppermute | solution.py:22
  27.6 8.4 %collective-permute-done.3.refs_2_.refs_6_.refs_10_ = bf16[256,768]{1,0:T(8,128)(2,1)S(1)} collective-permute-done((bf16[256,768]{1,0:T(8,128)(2,1)S(1)}, bf16[256,768]{1,0:T(8,128)(2,1)S(1)}, u32[]{:S(2)}, u32[]{:S(2)}) %collective-permute-start.3) | collective-permute-done | bytes 393248 | tf_op jit(solution)/shard_map/ppermute | solution.py:22
  40.0 10.7 %collective-permute-done.1 = bf16[128,768]{1,0:T(8,128)(2,1)S(1)} collective-permute-done((bf16[128,768]{1,0:T(8,128)(2,1)S(1)}, bf16[128,768]{1,0:T(8,128)(2,1)S(1)}, u32[]{:S(2)}, u32[]{:S(2)}) %collective-permute-start.1) | collective-permute-done | bytes 196640 | tf_op jit(solution)/shard_map/ppermute | solution.py:26
  54.4 2.9 %collective-permute-start.8 = (bf16[256,768]{1,0:T(8,128)(2,1)}, bf16[256,768]{1,0:T(8,128)(2,1)}, u32[]{:S(2)}, u32[]{:S(2)}) collective-permute-start(bf16[256,768]{1,0:T(8,128)(2,1)} %collective-permute-done.7.refs_2_.refs_9_.refs_13_), channel_id=1, source_target_pairs={{0,112},{16,0},{32,16},{48,32},{64,48},{80,64},{96,80},{112,96},{1... | collective-permute-start | bytes 1179656 | tf_op jit(solution)/shard_map/ppermute | solution.py:22
  61.8 4.8 %collective-permute-done.5.refs_3_.refs_10_.refs_14_ = bf16[256,768]{1,0:T(8,128)(2,1)} collective-permute-done((bf16[256,768]{1,0:T(8,128)(2,1)}, bf16[256,768]{1,0:T(8,128)(2,1)}, u32[]{:S(2)}, u32[]{:S(2)}) %collective-permute-start.5) | collective-permute-done | bytes 393248 | tf_op jit(solution)/shard_map/ppermute | solution.py:22
  71.4 3.8 %stats.4.refs_3_ = f32[8,512]{1,0:T(8,128)S(1)} custom-call(bf16[512,768]{1,0:T(8,128)(2,1)S(1)} %pad_maximum_fusion.refs_0_.refs_1_.refs_2_, bf16[256,768]{1,0:T(8,128)(2,1)} %collective-permute-done.4.refs_1_.refs_8_.refs_12_, bf16[256,768]{1,0:T(8,128)(2,1)} %collective-permute-done.7.refs_2_.refs_9_.refs_13_, ...), custom_call_target="tpu_custom_call" | custom-call | flops 1000 | tf_op jit(solution)/shard_map/stats/pallas_call | solution.py:95
  82.4 9.3 %d_value.1 = (bf16[8,256,384]{2,1,0:T(8,128)(2,1)}, bf16[3,256,512]{2,1,0:T(8,128)(2,1)}, bf16[3,256,512]{2,1,0:T(8,128)(2,1)}, bf16[3,256,512]{2,1,0:T(8,128)(2...) custom-call(s32[1]{0:T(128)} %bitcast.2.refs_0_, ...), custom_call_target="tpu_custom_call" | custom-call | flops 1000 | tf_op jit(solution)/shard_map/d_value/pallas_call | solution.py:95
  91.7 5.2 %all-to-all-start = ((bf16[8,256,384]{2,1,0:T(8,128)(2,1)}), bf16[8,256,384]{2,1,0:T(8,128)(2,1)}, u32[]{:S(2)}, u32[]{:S(2)}) async-start(bf16[8,256,384]{2,1,0:T(8,128)(2,1)} %get-tuple-element.82), calls=%async_computation.1 | async-start | bytes 3145728 | tf_op jit(solution)/shard_map/all_to_all | solution.py:395
  100.8 5.5 %attend.1.refs_2_ = bf16[2,384,256]{2,1,0:T(8,128)(2,1)} custom-call(bf16[3,256,512]{2,1,0:T(8,128)(2,1)} %get-tuple-element.67.refs_0_, bf16[3,256,512]{2,1,0:T(8,128)(2,1)} %get-tuple-element.68.refs_1_, bf16[3,256,512]{2,1,0:T(8,128)(2,1)} %get-tuple-element.69.refs_2_, bf16[3,256,512]{2,1,0:T(8,128)(2,1)} %get-tuple-element.70.refs_3_, ...), custom_call_target="tpu_custom_call" | custom-call | flops 1000 | tf_op jit(solution)/shard_map/attend/pallas_call | solution.py:95
  109.4 3.9 %per_out.1 = bf16[1536,384]{1,0:T(8,128)(2,1)} custom-call(bf16[1536,256]{1,0:T(8,128)(2,1)} %get-tuple-element.65.refs_0_, bf16[1536,256]{1,0:T(8,128)(2,1)} %copy-done.21, bf16[2,384,256]{2,1,0:T(8,128)(2,1)} %attend.1.refs_2_, bf16[2,384,256]{2,1,0:T(8,128)(2,1)} %copy-done.24), custom_call_target="tpu_custom_call" | custom-call | flops 1000 | tf_op jit(solution)/shard_map/per_out/pallas_call | solution.py:95
  113.4 2.9 %turn.3 = (bf16[1536,256]{1,0:T(8,128)(2,1)}, bf16[1536,256]{1,0:T(8,128)(2,1)}) custom-call(s32[1]{0:T(128)} %bitcast.refs_0_, s32[1]{0:T(128)} %bitcast.1.refs_1_, bf16[2,128,3072]{2,1,0:T(8,128)(2,1)} %refs_2_.1, bf16[2,128,3072]{2,1,0:T(8,128)(2,1)} %all-gather.5.cloned.1.call-done.refs_3_), custom_call_target="tpu_custom_call" | custom-call | flops 1000 | tf_op jit(solution)/shard_map/turn/pallas_call | solution.py:95
  116.5 22.3 %all-to-all-done.refs_0_ = bf16[8,256,384]{2,1,0:T(8,128)(2,1)} async-done(((bf16[8,256,384]{2,1,0:T(8,128)(2,1)}), bf16[8,256,384]{2,1,0:T(8,128)(2,1)}, u32[]{:S(2)}, u32[]{:S(2)}) %all-to-all-start) | async-done | bytes 1572896 | tf_op jit(solution)/shard_map/all_to_all | solution.py:395
  143.7 3.3 %per_value.1 = (bf16[2,192,384]{2,1,0:T(8,128)(2,1)}, bf16[2,192,384]{2,1,0:T(8,128)(2,1)}, bf16[1,96,384]{2,1,0:T(8,128)(2,1)}, bf16[1,96,384]{2,1,0:T(8,128)(2...) custom-call(s32[1]{0:T(128)} %bitcast.2.refs_0_, ...), custom_call_target="tpu_custom_call" | custom-call | flops 1000 | tf_op jit(solution)/shard_map/per_value/pallas_call | solution.py:95
  150.4 3.0 %collective-permute-start.19 = (bf16[1,96,384]{2,1,0:T(8,128)(2,1)}, bf16[1,96,384]{2,1,0:T(8,128)(2,1)S(1)}, u32[]{:S(2)}, u32[]{:S(2)}) collective-permute-start(bf16[1,96,384]{2,1,0:T(8,128)(2,1)} %get-tuple-element.87), channel_id=1, source_target_pairs={{0,96},{16,112},{32,0},{48,16},{64,32},{80,48},{96,64},{112,80},{1... | collective-permute-start | bytes 221192 | tf_op jit(solution)/shard_map/ppermute | solution.py:22
  153.4 7.3 %collective-permute-done.18.refs_2_ = bf16[1,96,384]{2,1,0:T(8,128)(2,1)S(1)} collective-permute-done((bf16[1,96,384]{2,1,0:T(8,128)(2,1)}, bf16[1,96,384]{2,1,0:T(8,128)(2,1)S(1)}, u32[]{:S(2)}, u32[]{:S(2)}) %collective-permute-start.18) | collective-permute-done | bytes 73760 | tf_op jit(solution)/shard_map/ppermute | solution.py:22
  165.3 3.4 %collective-permute-start.21 = (bf16[1,192,384]{2,1,0:T(8,128)(2,1)S(1)}, bf16[1,192,384]{2,1,0:T(8,128)(2,1)}, u32[]{:S(2)}, u32[]{:S(2)}) collective-permute-start(bf16[1,192,384]{2,1,0:T(8,128)(2,1)S(1)} %get-tuple-element.91), channel_id=1, source_target_pairs={{0,96},{16,112},{32,0},{48,16},{64,32},{80,48},{96,64},{112,80},{1... | collective-permute-start | bytes 442376 | tf_op jit(solution)/shard_map/ppermute | solution.py:22
  168.7 6.2 %collective-permute-done.20.refs_4_ = bf16[1,192,384]{2,1,0:T(8,128)(2,1)S(1)} collective-permute-done((bf16[1,192,384]{2,1,0:T(8,128)(2,1)S(1)}, bf16[1,192,384]{2,1,0:T(8,128)(2,1)S(1)}, u32[]{:S(2)}, u32[]{:S(2)}) %collective-permute-start.20) | collective-permute-done | bytes 147488 | tf_op jit(solution)/shard_map/ppermute | solution.py:22
  177.8 5.9 %all-to-all-start.1 = ((f32[16,8,128]{2,1,0:T(8,128)}), f32[16,8,128]{2,1,0:T(8,128)S(1)}, u32[]{:S(2)}, u32[]{:S(2)}) async-start(f32[16,8,128]{2,1,0:T(8,128)} %get-tuple-element.92), calls=%async_computation.2 | async-start | bytes 131072 | tf_op jit(solution)/shard_map/all_to_all | solution.py:468
  184.7 3.3 %collective-permute-start.22 = (bf16[96,768]{1,0:T(8,128)(2,1)S(1)}, bf16[96,768]{1,0:T(8,128)(2,1)S(1)}, u32[]{:S(2)}, u32[]{:S(2)}) collective-permute-start(bf16[96,768]{1,0:T(8,128)(2,1)S(1)} %get-tuple-element.103), channel_id=1, source_target_pairs={{0,0},{8,128},{128,8},{136,136},{16,16},{24,144},{144,24},{152,152... | collective-permute-start | bytes 442376 | tf_op jit(solution)/shard_map/ppermute | solution.py:465
  188.1 3.4 %all-to-all-done.1.refs_0_ = f32[16,8,128]{2,1,0:T(8,128)S(1)} async-done(((f32[16,8,128]{2,1,0:T(8,128)}), f32[16,8,128]{2,1,0:T(8,128)S(1)}, u32[]{:S(2)}, u32[]{:S(2)}) %all-to-all-start.1) | async-done | bytes 65568 | tf_op jit(solution)/shard_map/all_to_all | solution.py:468
  192.2 5.7 %all-to-all-start.2 = ((f32[16,8,128]{2,1,0:T(8,128)}), f32[16,8,128]{2,1,0:T(8,128)S(1)}, u32[]{:S(2)}, u32[]{:S(2)}) async-start(f32[16,8,128]{2,1,0:T(8,128)} %squares.1), calls=%async_computation.3 | async-start | bytes 131072 | tf_op jit(solution)/shard_map/all_to_all | solution.py:470
  198.0 6.4 %all-to-all-done.2.refs_1_ = f32[16,8,128]{2,1,0:T(8,128)S(1)} async-done(((f32[16,8,128]{2,1,0:T(8,128)}), f32[16,8,128]{2,1,0:T(8,128)S(1)}, u32[]{:S(2)}, u32[]{:S(2)}) %all-to-all-start.2) | async-done | bytes 65568 | tf_op jit(solution)/shard_map/all_to_all | solution.py:470
  (133 shorter events, 60.6 us)
Async XLA Ops:
  7.2 84.5 %all-gather.3.cloned.1.call-start = ((), (), s32[]{:S(2)}) async-start(), calls=%async_computation.4 | async-start | bytes 2359296 | tf_op jit(solution)/shard_map/all_gather | solution.py:319
  12.5 9.3 %collective-permute-start = (bf16[128,768]{1,0:T(8,128)(2,1)S(1)}, bf16[128,768]{1,0:T(8,128)(2,1)S(1)}, u32[]{:S(2)}, u32[]{:S(2)}) collective-permute-start(bf16[128,768]{1,0:T(8,128)(2,1)S(1)} %get-tuple-element.101), channel_id=1, source_target_pairs={{0,128},{128,0},{1,129},{129,1},{2,130},{130,2},{3,131},{131,3},{4... | collective-permute-start | bytes 589832 | tf_op jit(solution)/shard_map/ppermute | solution.py:26
  17.4 89.0 %all-gather.5.cloned.1.call-start = ((), (), s32[]{:S(2)}) async-start(), calls=%async_computation.5 | async-start | bytes 2359296 | tf_op jit(solution)/shard_map/all_gather | solution.py:319
  21.8 14.2 %collective-permute-start.3 = (bf16[256,768]{1,0:T(8,128)(2,1)S(1)}, bf16[256,768]{1,0:T(8,128)(2,1)S(1)}, u32[]{:S(2)}, u32[]{:S(2)}) collective-permute-start(bf16[256,768]{1,0:T(8,128)(2,1)S(1)} %pad_maximum_fusion.2.refs_1_.refs_5_.refs_9_), channel_id=1, source_target_pairs={{0,16},{16,32},{32,48},{48,64},{64,80},{80,96},{96,112},{112,0},{1... | collective-permute-start | bytes 1179656 | tf_op jit(solution)/shard_map/ppermute | solution.py:22
  23.6 12.5 %collective-permute-start.6 = (bf16[256,768]{1,0:T(8,128)(2,1)S(1)}, bf16[256,768]{1,0:T(8,128)(2,1)S(1)}, u32[]{:S(2)}, u32[]{:S(2)}) collective-permute-start(bf16[256,768]{1,0:T(8,128)(2,1)S(1)} %pad_maximum_fusion.2.refs_1_.refs_5_.refs_9_), channel_id=1, source_target_pairs={{0,112},{16,0},{32,16},{48,32},{64,48},{80,64},{96,80},{112,96},{1... | collective-permute-start | bytes 1179656 | tf_op jit(solution)/shard_map/ppermute | solution.py:22
  36.0 18.4 %collective-permute-start.4 = (bf16[256,768]{1,0:T(8,128)(2,1)S(1)}, bf16[256,768]{1,0:T(8,128)(2,1)}, u32[]{:S(2)}, u32[]{:S(2)}) collective-permute-start(bf16[256,768]{1,0:T(8,128)(2,1)S(1)} %collective-permute-done.3.refs_2_.refs_6_.refs_10_), channel_id=1, source_target_pairs={{0,16},{16,32},{32,48},{48,64},{64,80},{80,96},{96,112},{112,0},{1... | collective-permute-start | bytes 1179656 | tf_op jit(solution)/shard_map/ppermute | solution.py:22
  36.0 18.3 %collective-permute-start.7 = (bf16[256,768]{1,0:T(8,128)(2,1)S(1)}, bf16[256,768]{1,0:T(8,128)(2,1)}, u32[]{:S(2)}, u32[]{:S(2)}) collective-permute-start(bf16[256,768]{1,0:T(8,128)(2,1)S(1)} %collective-permute-done.6.refs_3_.refs_7_.refs_11_), channel_id=1, source_target_pairs={{0,112},{16,0},{32,16},{48,32},{64,48},{80,64},{96,80},{112,96},{1... | collective-permute-start | bytes 1179656 | tf_op jit(solution)/shard_map/ppermute | solution.py:22
  38.7 11.9 %collective-permute-start.1 = (bf16[128,768]{1,0:T(8,128)(2,1)S(1)}, bf16[128,768]{1,0:T(8,128)(2,1)S(1)}, u32[]{:S(2)}, u32[]{:S(2)}) collective-permute-start(bf16[128,768]{1,0:T(8,128)(2,1)S(1)} %get-tuple-element.99), channel_id=1, source_target_pairs={{0,128},{128,0},{1,129},{129,1},{2,130},{130,2},{3,131},{131,3},{4... | collective-permute-start | bytes 589832 | tf_op jit(solution)/shard_map/ppermute | solution.py:26
  54.4 12.3 %collective-permute-start.5 = (bf16[256,768]{1,0:T(8,128)(2,1)}, bf16[256,768]{1,0:T(8,128)(2,1)}, u32[]{:S(2)}, u32[]{:S(2)}) collective-permute-start(bf16[256,768]{1,0:T(8,128)(2,1)} %collective-permute-done.4.refs_1_.refs_8_.refs_12_), channel_id=1, source_target_pairs={{0,16},{16,32},{32,48},{48,64},{64,80},{80,96},{96,112},{112,0},{1... | collective-permute-start | bytes 1179656 | tf_op jit(solution)/shard_map/ppermute | solution.py:22
  54.4 12.2 %collective-permute-start.8 = (bf16[256,768]{1,0:T(8,128)(2,1)}, bf16[256,768]{1,0:T(8,128)(2,1)}, u32[]{:S(2)}, u32[]{:S(2)}) collective-permute-start(bf16[256,768]{1,0:T(8,128)(2,1)} %collective-permute-done.7.refs_2_.refs_9_.refs_13_), channel_id=1, source_target_pairs={{0,112},{16,0},{32,16},{48,32},{64,48},{80,64},{96,80},{112,96},{1... | collective-permute-start | bytes 1179656 | tf_op jit(solution)/shard_map/ppermute | solution.py:22
  91.7 47.1 %all-to-all-start = ((bf16[8,256,384]{2,1,0:T(8,128)(2,1)}), bf16[8,256,384]{2,1,0:T(8,128)(2,1)}, u32[]{:S(2)}, u32[]{:S(2)}) async-start(bf16[8,256,384]{2,1,0:T(8,128)(2,1)} %get-tuple-element.82), calls=%async_computation.1 | async-start | bytes 3145728 | tf_op jit(solution)/shard_map/all_to_all | solution.py:395
  96.9 71.8 %reduce-scatter.2.cloned.1.call-start = ((), (), s32[]{:S(2)}) async-start(), calls=%async_computation.6 | async-start | bytes 1327104 | tf_op jit(solution)/shard_map/reduce_scatter | solution.py:434
  100.1 8.2 %collective-permute-start.12 = (bf16[1536,256]{1,0:T(8,128)(2,1)}, bf16[1536,256]{1,0:T(8,128)(2,1)S(1)}, u32[]{:S(2)}, u32[]{:S(2)}) collective-permute-start(bf16[1536,256]{1,0:T(8,128)(2,1)} %get-tuple-element.66), channel_id=1, source_target_pairs={{0,8},{8,0},{1,9},{9,1},{2,10},{10,2},{3,11},{11,3},{4,12},{12,4},... | collective-permute-start | bytes 2359304 | tf_op jit(solution)/shard_map/ppermute | solution.py:26
  116.3 25.7 %collective-permute-start.14 = (bf16[1536,256]{1,0:T(8,128)(2,1)}, bf16[1536,256]{1,0:T(8,128)(2,1)S(1)}, u32[]{:S(2)}, u32[]{:S(2)}) collective-permute-start(bf16[1536,256]{1,0:T(8,128)(2,1)} %get-tuple-element.81), channel_id=1, source_target_pairs={{0,8},{8,0},{1,9},{9,1},{2,10},{10,2},{3,11},{11,3},{4,12},{12,4},... | collective-permute-start | bytes 2359304 | tf_op jit(solution)/shard_map/ppermute | solution.py:26
  147.0 14.7 %collective-permute-start.16 = (bf16[2,192,384]{2,1,0:T(8,128)(2,1)}, bf16[2,192,384]{2,1,0:T(8,128)(2,1)S(1)}, u32[]{:S(2)}, u32[]{:S(2)}) collective-permute-start(bf16[2,192,384]{2,1,0:T(8,128)(2,1)} %get-tuple-element.84), channel_id=1, source_target_pairs={{0,16},{16,32},{32,48},{48,64},{64,80},{80,96},{96,112},{112,0},{1... | collective-permute-start | bytes 884744 | tf_op jit(solution)/shard_map/ppermute | solution.py:22
  149.1 12.7 %collective-permute-start.17 = (bf16[2,192,384]{2,1,0:T(8,128)(2,1)}, bf16[2,192,384]{2,1,0:T(8,128)(2,1)S(1)}, u32[]{:S(2)}, u32[]{:S(2)}) collective-permute-start(bf16[2,192,384]{2,1,0:T(8,128)(2,1)} %get-tuple-element.85), channel_id=1, source_target_pairs={{0,112},{16,0},{32,16},{48,32},{64,48},{80,64},{96,80},{112,96},{1... | collective-permute-start | bytes 884744 | tf_op jit(solution)/shard_map/ppermute | solution.py:22
  149.8 10.9 %collective-permute-start.18 = (bf16[1,96,384]{2,1,0:T(8,128)(2,1)}, bf16[1,96,384]{2,1,0:T(8,128)(2,1)S(1)}, u32[]{:S(2)}, u32[]{:S(2)}) collective-permute-start(bf16[1,96,384]{2,1,0:T(8,128)(2,1)} %get-tuple-element.86), channel_id=1, source_target_pairs={{0,32},{16,48},{32,64},{48,80},{64,96},{80,112},{96,0},{112,16},{1... | collective-permute-start | bytes 221192 | tf_op jit(solution)/shard_map/ppermute | solution.py:22
  150.4 11.4 %collective-permute-start.19 = (bf16[1,96,384]{2,1,0:T(8,128)(2,1)}, bf16[1,96,384]{2,1,0:T(8,128)(2,1)S(1)}, u32[]{:S(2)}, u32[]{:S(2)}) collective-permute-start(bf16[1,96,384]{2,1,0:T(8,128)(2,1)} %get-tuple-element.87), channel_id=1, source_target_pairs={{0,96},{16,112},{32,0},{48,16},{64,32},{80,48},{96,64},{112,80},{1... | collective-permute-start | bytes 221192 | tf_op jit(solution)/shard_map/ppermute | solution.py:22
  165.0 9.9 %collective-permute-start.20 = (bf16[1,192,384]{2,1,0:T(8,128)(2,1)S(1)}, bf16[1,192,384]{2,1,0:T(8,128)(2,1)S(1)}, u32[]{:S(2)}, u32[]{:S(2)}) collective-permute-start(bf16[1,192,384]{2,1,0:T(8,128)(2,1)S(1)} %get-tuple-element.90), channel_id=1, source_target_pairs={{0,32},{16,48},{32,64},{48,80},{64,96},{80,112},{96,0},{112,16},{1... | collective-permute-start | bytes 442376 | tf_op jit(solution)/shard_map/ppermute | solution.py:22
  165.3 9.7 %collective-permute-start.21 = (bf16[1,192,384]{2,1,0:T(8,128)(2,1)S(1)}, bf16[1,192,384]{2,1,0:T(8,128)(2,1)}, u32[]{:S(2)}, u32[]{:S(2)}) collective-permute-start(bf16[1,192,384]{2,1,0:T(8,128)(2,1)S(1)} %get-tuple-element.91), channel_id=1, source_target_pairs={{0,96},{16,112},{32,0},{48,16},{64,32},{80,48},{96,64},{112,80},{1... | collective-permute-start | bytes 442376 | tf_op jit(solution)/shard_map/ppermute | solution.py:22
  177.8 13.7 %all-to-all-start.1 = ((f32[16,8,128]{2,1,0:T(8,128)}), f32[16,8,128]{2,1,0:T(8,128)S(1)}, u32[]{:S(2)}, u32[]{:S(2)}) async-start(f32[16,8,128]{2,1,0:T(8,128)} %get-tuple-element.92), calls=%async_computation.2 | async-start | bytes 131072 | tf_op jit(solution)/shard_map/all_to_all | solution.py:468
  184.7 13.3 %collective-permute-start.22 = (bf16[96,768]{1,0:T(8,128)(2,1)S(1)}, bf16[96,768]{1,0:T(8,128)(2,1)S(1)}, u32[]{:S(2)}, u32[]{:S(2)}) collective-permute-start(bf16[96,768]{1,0:T(8,128)(2,1)S(1)} %get-tuple-element.103), channel_id=1, source_target_pairs={{0,0},{8,128},{128,8},{136,136},{16,16},{24,144},{144,24},{152,152... | collective-permute-start | bytes 442376 | tf_op jit(solution)/shard_map/ppermute | solution.py:465
  188.0 10.0 %collective-permute-start.23 = (bf16[96,768]{1,0:T(8,128)(2,1)S(1)}, bf16[96,768]{1,0:T(8,128)(2,1)S(1)}, u32[]{:S(2)}, u32[]{:S(2)}) collective-permute-start(bf16[96,768]{1,0:T(8,128)(2,1)S(1)} %get-tuple-element.102), channel_id=1, source_target_pairs={{0,8},{8,136},{128,0},{136,128},{16,24},{24,152},{144,16},{152,144... | collective-permute-start | bytes 442376 | tf_op jit(solution)/shard_map/ppermute | solution.py:466
  192.2 12.2 %all-to-all-start.2 = ((f32[16,8,128]{2,1,0:T(8,128)}), f32[16,8,128]{2,1,0:T(8,128)S(1)}, u32[]{:S(2)}, u32[]{:S(2)}) async-start(f32[16,8,128]{2,1,0:T(8,128)} %squares.1), calls=%async_computation.3 | async-start | bytes 131072 | tf_op jit(solution)/shard_map/all_to_all | solution.py:470
  (37 other events, 316.4 us)
Sparse Core Ops, SparseCore 0:
  17.5 39.3 all-gather.2
  58.6 33.2 all-gather.4
  113.5 39.9 reduce-scatter.1

commit v3 on v2

--- a/solution.py
+++ b/solution.py
@@ -77,14 +77,15 @@
         for at, source in enumerate(sources):
             if at in views:
                 source = source.at[views[at][1](*numbers)]
-            arriving.append(Arriving(source, refs[at], in_sems.at[at]))
+            arriving.append(source if small[at] else Arriving(source, refs[at], in_sems.at[at]))
         leaving = [
             Leaving(refs[n_inputs + at], target, out_sems.at[at])
             for at, target in enumerate(targets)
         ]
         body(numbers, arriving, leaving)
-        for one in arriving:
-            one.ref()
+        for at, one in enumerate(arriving):
+            if not small[at]:
+                one.ref()
         for one in leaving:
             one.send()
         for one in leaving:
@@ -92,10 +93,12 @@
 
     hbm = pl.BlockSpec(memory_space=pltpu.HBM)
     smem = pl.BlockSpec(memory_space=pltpu.SMEM)
+    in_vmem = pl.BlockSpec(memory_space=pltpu.VMEM)
+    small = [x.dtype == F32 and x.size <= 2**15 for x in inputs]
     return pl.pallas_call(
         kernel,
         out_shape=tuple(outputs),
-        in_specs=[smem] * n_scalars + [hbm] * n_inputs,
+        in_specs=[smem] * n_scalars + [in_vmem if one else hbm for one in small],
         out_specs=(hbm,) * n_outputs,
         scratch_shapes=[pltpu.VMEM(size, x.dtype) for size, x in zip(shapes, inputs)]
         + [pltpu.VMEM(x.shape, x.dtype) for x in outputs]
@@ -139,7 +142,8 @@
     (here,) = numbers
     query, d_attn, mine, other = arriving[:4]
     keys, pieces = arriving[4:], len(slots)
-    out, kept = leaving[0], leaving[1:]
+    out, att = leaving
+    half = att.ref.shape[2]
     totals = both_totals(mine, other)
 
     def scores(head, piece):
@@ -154,29 +158,17 @@
             ahead = scores(*order[at + 1])
         cols = head_cols(head)
         probs = jnp.exp(block - totals[head : head + 1, :]).astype(BF16)
-        kept[piece].ref[head] = probs
         d_value = jnp.dot(probs, d_attn[:, cols], preferred_element_type=F32)
         distance, start = slots[piece]
         owner = lax.rem(here + (Z - distance), Z)
         out.ref[owner, start : start + probs.shape[0], cols] = d_value.astype(BF16)
-        if head == heads - 1:
-            kept[piece].send()
-
-
-def attend_body(heads, numbers, arriving, leaving):
-    pieces = len(arriving) // 2
-    probs, values, (out,) = arriving[:pieces], arriving[pieces:], leaving
-    half = out.ref.shape[2]
-    first = (((0,), (0,)), ((), ()))
-    for head in range(heads):
-        cols = head_cols(head)
-        attended = jnp.zeros((HEAD_DIM, 2 * half), F32)
-        for prob, value in zip(probs, values):
-            attended += lax.dot_general(
-                value[:, cols], prob[head], first, preferred_element_type=F32
-            )
-        out.ref[0, cols, :] = attended[:, :half].astype(BF16)
-        out.ref[1, cols, :] = attended[:, half:].astype(BF16)
+        first = (((0,), (0,)), ((), ()))
+        value = keys[piece][:, head_cols(heads + head)]
+        term = lax.dot_general(value, probs, first, preferred_element_type=F32)
+        attended = term if piece == 0 else attended + term
+        if piece == pieces - 1:
+            att.ref[0, cols, :] = attended[:, :half].astype(BF16)
+            att.ref[1, cols, :] = attended[:, half:].astype(BF16)
 
 
 def turn_body(numbers, arriving, leaving):
@@ -289,7 +281,7 @@
     far_factor = jnp.where(core == 0, factors[1], factors[0])
     weighted = near_factor * near[...].astype(F32) + far_factor * far[...].astype(F32)
     value.ref[...] = (weighted[:, :columns] + noise_value[...]) * 0.5
-    out.ref[...] = (weighted[:, columns:].T + noise_out[...]) * 0.5
+    out.ref[...] = (weighted[:, columns:] + noise_out[...]) * 0.5
 
 
 def local(tokens, w_query, w_key, w_value, w_out, cotangent, noise_value, noise_out):
@@ -319,15 +311,12 @@
         return lax.all_gather(pick(array, 1 - image), "yh", axis=0)
 
     keys_values = jnp.concatenate([project(w_key), project(w_value)], axis=1)
-    cotangent_pair = cotangent, from_partner(cotangent)
     chunk = image_rows(keys_values)
     d_attn = jnp.einsum("rd,cd->rc", flat_cotangent, w_out, preferred_element_type=F32)
     queries_d = jnp.concatenate([project(w_query), d_attn.astype(BF16)], axis=1)
-    chunk, queries_d, late_tokens = lax.optimization_barrier((chunk, queries_d, tokens))
+    chunk, queries_d = lax.optimization_barrier((chunk, queries_d))
     queries_d = image_rows(queries_d)
-    tokens_pair = tokens, from_partner(late_tokens)
-    queries_d = jnp.concatenate([queries_d, swap(queries_d, "core", CORE)], axis=0)
-    chip_rows = queries_d.shape[0]
+    chip_rows = CORE * images * rows
 
     def stats_of(chosen, *carried):
         (found,) = call(
@@ -352,6 +341,13 @@
         forward = shift(forward, "z", Z, 1)
         backward = shift(backward, "z", Z, -1)
         pieces += [forward, backward]
+        if step == 1:
+            forward, backward, queries_d, late_tokens, late_cotangent = lax.optimization_barrier(
+                (forward, backward, queries_d, tokens, cotangent)
+            )
+            queries_d = jnp.concatenate([queries_d, swap(queries_d, "core", CORE)], axis=0)
+            cotangent_pair = cotangent, from_partner(late_cotangent)
+            tokens_pair = tokens, from_partner(late_tokens)
         if step == 3:
             stats = stats_of(pieces[:3])
             forward, backward, stats = lax.optimization_barrier((forward, backward, stats))
@@ -374,36 +370,26 @@
 
     def relay(arrived, keep_f, keep_b):
         like = shape(keep_f.shape, BF16)
-        return call(relay_body, "relay", (), (*arrived, keep_f, keep_b), (like, like))
+        return call(
+            relay_body, "relay", (), (*arrived, keep_f, keep_b), (like, like), vmem=LARGE
+        )
 
     def end_scatter(arrived, sums, own):
         return own, arrived[0], arrived[1], shift(sums[0], "z", Z, 2), shift(sums[1], "z", Z, -2)
 
     slots = ((0, 0), (1, 0), (7, 0), (2, 0), (6, 0), (3, 0), (5, 0), (4, 0), (4, half))
-    inputs = (queries_d, queries_d, stats, other_stats, *pieces)
-    views = {at: left_part(inputs[at]) for at in (0, *range(4, len(inputs)))}
-    d_value, *probs = call(
+    d_value, attended = call(
         functools.partial(d_value_body, heads, slots),
         "d_value",
         (here,),
-        inputs,
-        (block(Z, 2 * rows),) + tuple(shape((heads, x.shape[0], chip_rows), BF16) for x in pieces),
-        {**views, 1: right_part(queries_d)},
+        (queries_d, queries_d, stats, other_stats, *pieces),
+        (block(Z, 2 * rows), shape((2, columns, chip_rows // 2), BF16)),
+        {0: left_part(queries_d), 1: right_part(queries_d)},
         LARGE,
     )
-    d_value, probs, cotangent_pair = lax.optimization_barrier((d_value, probs, cotangent_pair))
+    attended, cotangent_pair = lax.optimization_barrier((attended, cotangent_pair))
     terms = lax.all_to_all(d_value, "z", 0, 0, tiled=True)
-    (attended,) = call(
-        functools.partial(attend_body, heads),
-        "attend",
-        (),
-        (*probs, *pieces),
-        (shape((2, columns, chip_rows // 2), BF16),),
-        {len(pieces) + at: right_part(x) for at, x in enumerate(pieces)},
-        LARGE,
-    )
     attended_other = swap(attended, "core", CORE)
-    attended, tokens_pair = lax.optimization_barrier((attended, tokens_pair))
 
     def half_width(pair):
         turned = shape((width // 2, 2 * rows), BF16)
@@ -422,7 +408,6 @@
         return keep, swap(send, "core", CORE)
 
     cotangent_half = half_width(cotangent_pair)
-    tokens_half = half_width(tokens_pair)
     (per_out,) = call(
         out_grad_body,
         "per_out",
@@ -431,7 +416,9 @@
         (shape((width // 2, columns), BF16),),
         vmem=LARGE,
     )
+    per_out, tokens_pair = lax.optimization_barrier((per_out, tokens_pair))
     out_shard = lax.psum_scatter(per_out, "z", scatter_dimension=0, tiled=True)
+    tokens_half = half_width(tokens_pair)
 
     (d_value,) = call(sum_body, "d_value_sum", (), (terms,), (shape((2 * rows, columns), BF16),))
     count = width // 2 // Z
@@ -468,13 +455,15 @@
     squares = lax.all_to_all(square, ("z", "core"), 0, 0, tiled=True)
     (squares,) = call(square_body, "squares", (), (squares,), (small,))
     squares = lax.all_to_all(squares, ("yh", "yl", "x"), 0, 0, tiled=True)
-    return call(
+    rows_of_both = shape(noise_value.shape, F32)
+    grad_value, grad_out = call(
         final_body,
         "final",
         (this_core,),
-        (squares, near, far, noise_value, noise_out),
-        (shape(noise_value.shape, F32), shape(noise_out.shape, F32)),
-    )
+        (squares, near, far, noise_value, noise_out.T),
+        (rows_of_both, rows_of_both),
+    )
+    return grad_value, grad_out.T
 
 
 def solution(mesh):

time: 214 us -> 205 us (0.958)
  waiting for transfers between devices: 77 us -> 64.9 us
  starting transfers between devices: 57 us -> 65.4 us
  Pallas kernels: 42.6 us -> 37.8 us
    all_gather x2, waiting for transfers between devices: 0.03 us -> 8.12 us  [from_partner(): return lax.all_gather(pick(array, 1 - image), 'yh', axis=0)]
    all_to_all x1, waiting for transfers between devices: 22.3 us -> 15.2 us  [local(): terms = lax.all_to_all(d_value, 'z', 0, 0, tiled=True)]
    ppermute x8, waiting for transfers between devices: 14.5 us -> 7.39 us  [swap(): return lax.ppermute(x, axis, [(i, i ^ mask) for i in range(size)])]
    ppermute x8, starting transfers between devices: 12.5 us -> 18.6 us  [swap(): return lax.ppermute(x, axis, [(i, i ^ mask) for i in range(size)])]
    ppermute x14, waiting for transfers between devices: 30.4 us -> 25.5 us  [shift(): return lax.ppermute(x, axis, [(i, (i + by) % size) for i in range(size)])]
    pallas_call x14 -> x13, Pallas kernels: 42.6 us -> 37.8 us  [call(): pl.pallas_call(kernel, out_shape=tuple(outputs), in_specs=[smem] * n_scal...]
    unnamed x63 -> x61, local copies, waits for them, and re-layouts: 7 us -> 6.72 us
  transfers between devices with their start and end apart: 30 -> 30, of which waited for: 13 -> 15; matrix products, arithmetic and copies ran while one was open for 5% -> 6% of each run, Pallas kernels for 18% -> 17%
where the time goes in v3:
time: 205 us; the launch traced here: 204 us
  starting transfers between devices  65.4 us (32%)
  waiting for transfers between devices  64.9 us (32%)
  Pallas kernels  37.8 us (18%)
  between operations  14.2 us (7%)
  local copies, waits for them, and re-layouts  13.9 us (7%)
  matrix products  7.15 us (3%)
    pallas_call x13, Pallas kernels, call(): pl.pallas_call(kernel, out_shape=tuple(outputs), in_specs=[smem] * n_scal...  37.8 us
    ppermute x14, waiting for transfers between devices, shift(): return lax.ppermute(x, axis, [(i, (i + by) % size) for i in range(size)])  25.5 us
    ppermute x14, starting transfers between devices, shift(): return lax.ppermute(x, axis, [(i, (i + by) % size) for i in range(size)])  24.3 us
    ppermute x8, starting transfers between devices, swap(): return lax.ppermute(x, axis, [(i, i ^ mask) for i in range(size)])  18.6 us
    all_to_all x1, waiting for transfers between devices, local(): terms = lax.all_to_all(d_value, 'z', 0, 0, tiled=True)  15.2 us
    all_gather x2, waiting for transfers between devices, from_partner(): return lax.all_gather(pick(array, 1 - image), 'yh', axis=0)  8.12 us
    ppermute x8, waiting for transfers between devices, swap(): return lax.ppermute(x, axis, [(i, i ^ mask) for i in range(size)])  7.39 us
    unnamed x61, local copies, waits for them, and re-layouts  6.72 us
  transfers between devices with their start and end apart: 30, of which 15 were waited for; matrix products, arithmetic and copies ran while one was open for 6% of the time, Pallas kernels for 17%

profile of v3, /device:TPU:1, one launch (start us, length us, event | category | flops | bytes accessed | tf_op | source)
XLA Modules:
  0.0 204.3 jit_solution(2082603540403119558)
XLA Ops:
  12.6 3.8 %collective-permute-start = (bf16[128,768]{1,0:T(8,128)(2,1)S(1)}, bf16[128,768]{1,0:T(8,128)(2,1)S(1)}, u32[]{:S(2)}, u32[]{:S(2)}) collective-permute-start(bf16[128,768]{1,0:T(8,128)(2,1)S(1)} %get-tuple-element.75), channel_id=1, source_target_pairs={{0,128},{128,0},{1,129},{129,1},{2,130},{130,2},{3,131},{131,3},{4... | collective-permute-start | bytes 589832 | tf_op jit(solution)/shard_map/ppermute | solution.py:26
  22.5 4.0 %collective-permute-start.2 = (bf16[256,768]{1,0:T(8,128)(2,1)S(1)}, bf16[256,768]{1,0:T(8,128)(2,1)S(1)}, u32[]{:S(2)}, u32[]{:S(2)}) collective-permute-start(bf16[256,768]{1,0:T(8,128)(2,1)S(1)} %pad_maximum_fusion.1.refs_1_.refs_5_), channel_id=1, source_target_pairs={{0,112},{16,0},{32,16},{48,32},{64,48},{80,64},{96,80},{112,96},{1... | collective-permute-start | bytes 1179656 | tf_op jit(solution)/shard_map/ppermute | solution.py:22
  26.6 3.0 %collective-permute-start.3 = (bf16[128,768]{1,0:T(8,128)(2,1)S(1)}, bf16[128,768]{1,0:T(8,128)(2,1)S(1)}, u32[]{:S(2)}, u32[]{:S(2)}) collective-permute-start(bf16[128,768]{1,0:T(8,128)(2,1)S(1)} %get-tuple-element.73), channel_id=1, source_target_pairs={{0,128},{128,0},{1,129},{129,1},{2,130},{130,2},{3,131},{131,3},{4... | collective-permute-start | bytes 589832 | tf_op jit(solution)/shard_map/ppermute | solution.py:26
  29.6 3.1 %collective-permute-done.3 = bf16[128,768]{1,0:T(8,128)(2,1)S(1)} collective-permute-done((bf16[128,768]{1,0:T(8,128)(2,1)S(1)}, bf16[128,768]{1,0:T(8,128)(2,1)S(1)}, u32[]{:S(2)}, u32[]{:S(2)}) %collective-permute-start.3) | collective-permute-done | bytes 196640 | tf_op jit(solution)/shard_map/ppermute | solution.py:26
  38.2 2.7 %collective-permute-start.4 = (bf16[256,768]{1,0:T(8,128)(2,1)}, bf16[256,768]{1,0:T(8,128)(2,1)}, u32[]{:S(2)}, u32[]{:S(2)}) collective-permute-start(bf16[256,768]{1,0:T(8,128)(2,1)} %pad_maximum_fusion.3), channel_id=1, source_target_pairs={{0,8},{8,0},{1,9},{9,1},{2,10},{10,2},{3,11},{11,3},{4,12},{12,4},... | collective-permute-start | bytes 1179656 | tf_op jit(solution)/shard_map/ppermute | solution.py:26
  41.0 4.3 %collective-permute-done.5.refs_1_.refs_8_ = bf16[256,768]{1,0:T(8,128)(2,1)} collective-permute-done((bf16[256,768]{1,0:T(8,128)(2,1)S(1)}, bf16[256,768]{1,0:T(8,128)(2,1)}, u32[]{:S(2)}, u32[]{:S(2)}) %collective-permute-start.5) | collective-permute-done | bytes 393248 | tf_op jit(solution)/shard_map/ppermute | solution.py:22
  58.8 3.8 %stats.4.refs_3_ = f32[8,512]{1,0:T(8,128)S(1)} custom-call(bf16[512,768]{1,0:T(8,128)(2,1)S(1)} %constant_dynamic-update-slice_fusion.refs_0_.refs_1_.refs_2_, bf16[256,768]{1,0:T(8,128)(2,1)} %collective-permute-done.5.refs_1_.refs_8_, bf16[256,768]{1,0:T(8,128)(2,1)} %collective-permute-done.7.refs_2_.refs_9_, ...), custom_call_target="tpu_custom_call" | custom-call | flops 1000 | tf_op jit(solution)/shard_map/stats/pallas_call | solution.py:98
  65.8 5.6 %collective-permute-start.11 = (f32[8,512]{1,0:T(8,128)S(1)}, f32[8,512]{1,0:T(8,128)S(1)}, u32[]{:S(2)}, u32[]{:S(2)}) collective-permute-start(f32[8,512]{1,0:T(8,128)S(1)} %stats.5.refs_3_), channel_id=1, source_target_pairs={{0,8},{8,0},{1,9},{9,1},{2,10},{10,2},{3,11},{11,3},{4,12},{12,4},... | collective-permute-start | bytes 49160 | tf_op jit(solution)/shard_map/ppermute | solution.py:26
  72.9 9.4 %d_value.1 = (bf16[8,256,384]{2,1,0:T(8,128)(2,1)}, bf16[2,384,256]{2,1,0:T(8,128)(2,1)}) custom-call(s32[1]{0:T(128)} %bitcast.2.refs_0_, bf16[512,768]{1,0:T(8,128)(2,1)} %copy-done.1, bf16[512,768]{1,0:T(8,128)(2,1)} %copy-done.1, f32[8,512]{1,0:T(8,128)} %copy-done.12, f32[8,512]{1,0:T(8,128)} %copy-done.27, bf16[256,768]{1,0:T(8,128)(2,1)} %copy-done.2, ...), custom_call_target="tpu_custom_call" | custom-call | flops 1000 | tf_op jit(solution)/shard_map/d_value/pallas_call | solution.py:98
  82.3 4.6 %all-to-all-start = ((bf16[8,256,384]{2,1,0:T(8,128)(2,1)}), bf16[8,256,384]{2,1,0:T(8,128)(2,1)}, u32[]{:S(2)}, u32[]{:S(2)}) async-start(bf16[8,256,384]{2,1,0:T(8,128)(2,1)} %get-tuple-element.58), calls=%async_computation.1 | async-start | bytes 3145728 | tf_op jit(solution)/shard_map/all_to_all | solution.py:391
  87.1 3.0 %turn.2 = (bf16[1536,256]{1,0:T(8,128)(2,1)}, bf16[1536,256]{1,0:T(8,128)(2,1)}) custom-call(s32[1]{0:T(128)} %bitcast.refs_0_, s32[1]{0:T(128)} %bitcast.1.refs_1_, bf16[2,128,3072]{2,1,0:T(8,128)(2,1)} %refs_2_, bf16[2,128,3072]{2,1,0:T(8,128)(2,1)} %all-gather.3.cloned.1.call-done.refs_3_), custom_call_target="tpu_custom_call" | custom-call | flops 1000 | tf_op jit(solution)/shard_map/turn/pallas_call | solution.py:98
  94.3 3.9 %per_out.1 = bf16[1536,384]{1,0:T(8,128)(2,1)} custom-call(bf16[1536,256]{1,0:T(8,128)(2,1)} %get-tuple-element.49.refs_0_, bf16[1536,256]{1,0:T(8,128)(2,1)} %copy-done.18, bf16[2,384,256]{2,1,0:T(8,128)(2,1)} %get-tuple-element.51.refs_2_, bf16[2,384,256]{2,1,0:T(8,128)(2,1)} %copy-done.21), custom_call_target="tpu_custom_call" | custom-call | flops 1000 | tf_op jit(solution)/shard_map/per_out/pallas_call | solution.py:98
  98.3 8.1 %all-gather.5.cloned.1.call-done.refs_3_ = bf16[2,128,3072]{2,1,0:T(8,128)(2,1)} async-done(((bf16[1,128,3072]{2,1,0:T(8,128)(2,1)}), bf16[2,128,3072]{2,1,0:T(8,128)(2,1)}) %all-gather.5.cloned.1.call-update) | async-done | bytes 1572880 | tf_op jit(solution)/shard_map/all_gather | solution.py:311
  106.4 2.9 %turn.3 = (bf16[1536,256]{1,0:T(8,128)(2,1)}, bf16[1536,256]{1,0:T(8,128)(2,1)}) custom-call(s32[1]{0:T(128)} %bitcast.refs_0_, s32[1]{0:T(128)} %bitcast.1.refs_1_, bf16[2,128,3072]{2,1,0:T(8,128)(2,1)} %refs_2_.1, bf16[2,128,3072]{2,1,0:T(8,128)(2,1)} %all-gather.5.cloned.1.call-done.refs_3_), custom_call_target="tpu_custom_call" | custom-call | flops 1000 | tf_op jit(solution)/shard_map/turn/pallas_call | solution.py:98
  110.1 15.2 %all-to-all-done.refs_0_ = bf16[8,256,384]{2,1,0:T(8,128)(2,1)} async-done(((bf16[8,256,384]{2,1,0:T(8,128)(2,1)}), bf16[8,256,384]{2,1,0:T(8,128)(2,1)}, u32[]{:S(2)}, u32[]{:S(2)}) %all-to-all-start) | async-done | bytes 1572896 | tf_op jit(solution)/shard_map/all_to_all | solution.py:391
  130.8 3.3 %per_value.1 = (bf16[2,192,384]{2,1,0:T(8,128)(2,1)}, bf16[2,192,384]{2,1,0:T(8,128)(2,1)}, bf16[1,96,384]{2,1,0:T(8,128)(2,1)}, bf16[1,96,384]{2,1,0:T(8,128)(2...) custom-call(s32[1]{0:T(128)} %bitcast.2.refs_0_, ...), custom_call_target="tpu_custom_call" | custom-call | flops 1000 | tf_op jit(solution)/shard_map/per_value/pallas_call | solution.py:98
  134.1 3.0 %collective-permute-start.16 = (bf16[2,192,384]{2,1,0:T(8,128)(2,1)}, bf16[2,192,384]{2,1,0:T(8,128)(2,1)S(1)}, u32[]{:S(2)}, u32[]{:S(2)}) collective-permute-start(bf16[2,192,384]{2,1,0:T(8,128)(2,1)} %get-tuple-element.60), channel_id=1, source_target_pairs={{0,16},{16,32},{32,48},{48,64},{64,80},{80,96},{96,112},{112,0},{1... | collective-permute-start | bytes 884744 | tf_op jit(solution)/shard_map/ppermute | solution.py:22
  140.6 9.2 %collective-permute-done.18.refs_2_ = bf16[1,96,384]{2,1,0:T(8,128)(2,1)S(1)} collective-permute-done((bf16[1,96,384]{2,1,0:T(8,128)(2,1)}, bf16[1,96,384]{2,1,0:T(8,128)(2,1)S(1)}, u32[]{:S(2)}, u32[]{:S(2)}) %collective-permute-start.18) | collective-permute-done | bytes 73760 | tf_op jit(solution)/shard_map/ppermute | solution.py:22
  155.7 3.1 %collective-permute-start.21 = (bf16[1,192,384]{2,1,0:T(8,128)(2,1)}, bf16[1,192,384]{2,1,0:T(8,128)(2,1)S(1)}, u32[]{:S(2)}, u32[]{:S(2)}) collective-permute-start(bf16[1,192,384]{2,1,0:T(8,128)(2,1)} %get-tuple-element.67), channel_id=1, source_target_pairs={{0,96},{16,112},{32,0},{48,16},{64,32},{80,48},{96,64},{112,80},{1... | collective-permute-start | bytes 442376 | tf_op jit(solution)/shard_map/ppermute | solution.py:22
  158.8 5.3 %collective-permute-done.20.refs_4_ = bf16[1,192,384]{2,1,0:T(8,128)(2,1)S(1)} collective-permute-done((bf16[1,192,384]{2,1,0:T(8,128)(2,1)}, bf16[1,192,384]{2,1,0:T(8,128)(2,1)S(1)}, u32[]{:S(2)}, u32[]{:S(2)}) %collective-permute-start.20) | collective-permute-done | bytes 147488 | tf_op jit(solution)/shard_map/ppermute | solution.py:22
  168.0 6.6 %all-to-all-start.1 = ((f32[16,8,128]{2,1,0:T(8,128)}), f32[16,8,128]{2,1,0:T(8,128)S(1)}, u32[]{:S(2)}, u32[]{:S(2)}) async-start(f32[16,8,128]{2,1,0:T(8,128)} %get-tuple-element.68), calls=%async_computation.2 | async-start | bytes 131072 | tf_op jit(solution)/shard_map/all_to_all | solution.py:455
  175.6 4.6 %collective-permute-start.22 = (bf16[96,768]{1,0:T(8,128)(2,1)S(1)}, bf16[96,768]{1,0:T(8,128)(2,1)S(1)}, u32[]{:S(2)}, u32[]{:S(2)}) collective-permute-start(bf16[96,768]{1,0:T(8,128)(2,1)S(1)} %get-tuple-element.77), channel_id=1, source_target_pairs={{0,0},{8,128},{128,8},{136,136},{16,16},{24,144},{144,24},{152,152... | collective-permute-start | bytes 442376 | tf_op jit(solution)/shard_map/ppermute | solution.py:452
  183.1 6.4 %all-to-all-start.2 = ((f32[16,8,128]{2,1,0:T(8,128)}), f32[16,8,128]{2,1,0:T(8,128)S(1)}, u32[]{:S(2)}, u32[]{:S(2)}) async-start(f32[16,8,128]{2,1,0:T(8,128)} %squares.1), calls=%async_computation.3 | async-start | bytes 131072 | tf_op jit(solution)/shard_map/all_to_all | solution.py:457
  189.6 6.5 %all-to-all-done.2.refs_1_ = f32[16,8,128]{2,1,0:T(8,128)S(1)} async-done(((f32[16,8,128]{2,1,0:T(8,128)}), f32[16,8,128]{2,1,0:T(8,128)S(1)}, u32[]{:S(2)}, u32[]{:S(2)}) %all-to-all-start.2) | async-done | bytes 65568 | tf_op jit(solution)/shard_map/all_to_all | solution.py:457
  (129 shorter events, 64.3 us)
Async XLA Ops:
  7.2 79.9 %all-gather.3.cloned.1.call-start = ((), (), s32[]{:S(2)}) async-start(), calls=%async_computation.4 | async-start | bytes 2359296 | tf_op jit(solution)/shard_map/all_gather | solution.py:311
  12.6 7.5 %collective-permute-start = (bf16[128,768]{1,0:T(8,128)(2,1)S(1)}, bf16[128,768]{1,0:T(8,128)(2,1)S(1)}, u32[]{:S(2)}, u32[]{:S(2)}) collective-permute-start(bf16[128,768]{1,0:T(8,128)(2,1)S(1)} %get-tuple-element.75), channel_id=1, source_target_pairs={{0,128},{128,0},{1,129},{129,1},{2,130},{130,2},{3,131},{131,3},{4... | collective-permute-start | bytes 589832 | tf_op jit(solution)/shard_map/ppermute | solution.py:26
  20.2 14.2 %collective-permute-start.1 = (bf16[256,768]{1,0:T(8,128)(2,1)S(1)}, bf16[256,768]{1,0:T(8,128)(2,1)S(1)}, u32[]{:S(2)}, u32[]{:S(2)}) collective-permute-start(bf16[256,768]{1,0:T(8,128)(2,1)S(1)} %pad_maximum_fusion.1.refs_1_.refs_5_), channel_id=1, source_target_pairs={{0,16},{16,32},{32,48},{48,64},{64,80},{80,96},{96,112},{112,0},{1... | collective-permute-start | bytes 1179656 | tf_op jit(solution)/shard_map/ppermute | solution.py:22
  22.5 11.8 %collective-permute-start.2 = (bf16[256,768]{1,0:T(8,128)(2,1)S(1)}, bf16[256,768]{1,0:T(8,128)(2,1)S(1)}, u32[]{:S(2)}, u32[]{:S(2)}) collective-permute-start(bf16[256,768]{1,0:T(8,128)(2,1)S(1)} %pad_maximum_fusion.1.refs_1_.refs_5_), channel_id=1, source_target_pairs={{0,112},{16,0},{32,16},{48,32},{64,48},{80,64},{96,80},{112,96},{1... | collective-permute-start | bytes 1179656 | tf_op jit(solution)/shard_map/ppermute | solution.py:22
  35.4 71.0 %all-gather.5.cloned.1.call-start = ((), (), s32[]{:S(2)}) async-start(), calls=%async_computation.5 | async-start | bytes 2359296 | tf_op jit(solution)/shard_map/all_gather | solution.py:311
  35.5 9.8 %collective-permute-start.5 = (bf16[256,768]{1,0:T(8,128)(2,1)S(1)}, bf16[256,768]{1,0:T(8,128)(2,1)}, u32[]{:S(2)}, u32[]{:S(2)}) collective-permute-start(bf16[256,768]{1,0:T(8,128)(2,1)S(1)} %collective-permute-done.1.refs_2_.refs_6_), channel_id=1, source_target_pairs={{0,16},{16,32},{32,48},{48,64},{64,80},{80,96},{96,112},{112,0},{1... | collective-permute-start | bytes 1179656 | tf_op jit(solution)/shard_map/ppermute | solution.py:22
  35.6 9.7 %collective-permute-start.7 = (bf16[256,768]{1,0:T(8,128)(2,1)S(1)}, bf16[256,768]{1,0:T(8,128)(2,1)}, u32[]{:S(2)}, u32[]{:S(2)}) collective-permute-start(bf16[256,768]{1,0:T(8,128)(2,1)S(1)} %collective-permute-done.2.refs_3_.refs_7_), channel_id=1, source_target_pairs={{0,112},{16,0},{32,16},{48,32},{64,48},{80,64},{96,80},{112,96},{1... | collective-permute-start | bytes 1179656 | tf_op jit(solution)/shard_map/ppermute | solution.py:22
  38.2 13.1 %collective-permute-start.4 = (bf16[256,768]{1,0:T(8,128)(2,1)}, bf16[256,768]{1,0:T(8,128)(2,1)}, u32[]{:S(2)}, u32[]{:S(2)}) collective-permute-start(bf16[256,768]{1,0:T(8,128)(2,1)} %pad_maximum_fusion.3), channel_id=1, source_target_pairs={{0,8},{8,0},{1,9},{9,1},{2,10},{10,2},{3,11},{11,3},{4,12},{12,4},... | collective-permute-start | bytes 1179656 | tf_op jit(solution)/shard_map/ppermute | solution.py:26
  45.3 9.3 %collective-permute-start.6 = (bf16[256,768]{1,0:T(8,128)(2,1)}, bf16[256,768]{1,0:T(8,128)(2,1)}, u32[]{:S(2)}, u32[]{:S(2)}) collective-permute-start(bf16[256,768]{1,0:T(8,128)(2,1)} %collective-permute-done.5.refs_1_.refs_8_), channel_id=1, source_target_pairs={{0,16},{16,32},{32,48},{48,64},{64,80},{80,96},{96,112},{112,0},{1... | collective-permute-start | bytes 1179656 | tf_op jit(solution)/shard_map/ppermute | solution.py:22
  45.3 9.3 %collective-permute-start.8 = (bf16[256,768]{1,0:T(8,128)(2,1)}, bf16[256,768]{1,0:T(8,128)(2,1)}, u32[]{:S(2)}, u32[]{:S(2)}) collective-permute-start(bf16[256,768]{1,0:T(8,128)(2,1)} %collective-permute-done.7.refs_2_.refs_9_), channel_id=1, source_target_pairs={{0,112},{16,0},{32,16},{48,32},{64,48},{80,64},{96,80},{112,96},{1... | collective-permute-start | bytes 1179656 | tf_op jit(solution)/shard_map/ppermute | solution.py:22
  55.5 7.0 %collective-permute-start.10 = (bf16[128,768]{1,0:T(8,128)(2,1)S(1)}, bf16[128,768]{1,0:T(8,128)(2,1)S(1)}, u32[]{:S(2)}, u32[]{:S(2)}) collective-permute-start(bf16[128,768]{1,0:T(8,128)(2,1)S(1)} %slice.7), channel_id=1, source_target_pairs={{0,112},{16,0},{32,16},{48,32},{64,48},{80,64},{96,80},{112,96},{1... | collective-permute-start | bytes 589832 | tf_op jit(solution)/shard_map/ppermute | solution.py:22
  82.3 43.0 %all-to-all-start = ((bf16[8,256,384]{2,1,0:T(8,128)(2,1)}), bf16[8,256,384]{2,1,0:T(8,128)(2,1)}, u32[]{:S(2)}, u32[]{:S(2)}) async-start(bf16[8,256,384]{2,1,0:T(8,128)(2,1)} %get-tuple-element.58), calls=%async_computation.1 | async-start | bytes 3145728 | tf_op jit(solution)/shard_map/all_to_all | solution.py:391
  87.0 78.1 %reduce-scatter.2.cloned.1.call-start = ((), (), s32[]{:S(2)}) async-start(), calls=%async_computation.6 | async-start | bytes 1327104 | tf_op jit(solution)/shard_map/reduce_scatter | solution.py:420
  109.4 19.7 %collective-permute-start.14 = (bf16[1536,256]{1,0:T(8,128)(2,1)}, bf16[1536,256]{1,0:T(8,128)(2,1)S(1)}, u32[]{:S(2)}, u32[]{:S(2)}) collective-permute-start(bf16[1536,256]{1,0:T(8,128)(2,1)} %get-tuple-element.57), channel_id=1, source_target_pairs={{0,8},{8,0},{1,9},{9,1},{2,10},{10,2},{3,11},{11,3},{4,12},{12,4},... | collective-permute-start | bytes 2359304 | tf_op jit(solution)/shard_map/ppermute | solution.py:26
  134.1 18.2 %collective-permute-start.16 = (bf16[2,192,384]{2,1,0:T(8,128)(2,1)}, bf16[2,192,384]{2,1,0:T(8,128)(2,1)S(1)}, u32[]{:S(2)}, u32[]{:S(2)}) collective-permute-start(bf16[2,192,384]{2,1,0:T(8,128)(2,1)} %get-tuple-element.60), channel_id=1, source_target_pairs={{0,16},{16,32},{32,48},{48,64},{64,80},{80,96},{96,112},{112,0},{1... | collective-permute-start | bytes 884744 | tf_op jit(solution)/shard_map/ppermute | solution.py:22
  137.0 15.2 %collective-permute-start.17 = (bf16[2,192,384]{2,1,0:T(8,128)(2,1)}, bf16[2,192,384]{2,1,0:T(8,128)(2,1)S(1)}, u32[]{:S(2)}, u32[]{:S(2)}) collective-permute-start(bf16[2,192,384]{2,1,0:T(8,128)(2,1)} %get-tuple-element.61), channel_id=1, source_target_pairs={{0,112},{16,0},{32,16},{48,32},{64,48},{80,64},{96,80},{112,96},{1... | collective-permute-start | bytes 884744 | tf_op jit(solution)/shard_map/ppermute | solution.py:22
  137.0 12.8 %collective-permute-start.18 = (bf16[1,96,384]{2,1,0:T(8,128)(2,1)}, bf16[1,96,384]{2,1,0:T(8,128)(2,1)S(1)}, u32[]{:S(2)}, u32[]{:S(2)}) collective-permute-start(bf16[1,96,384]{2,1,0:T(8,128)(2,1)} %get-tuple-element.62), channel_id=1, source_target_pairs={{0,32},{16,48},{32,64},{48,80},{64,96},{80,112},{96,0},{112,16},{1... | collective-permute-start | bytes 221192 | tf_op jit(solution)/shard_map/ppermute | solution.py:22
  138.6 13.7 %collective-permute-start.19 = (bf16[1,96,384]{2,1,0:T(8,128)(2,1)}, bf16[1,96,384]{2,1,0:T(8,128)(2,1)S(1)}, u32[]{:S(2)}, u32[]{:S(2)}) collective-permute-start(bf16[1,96,384]{2,1,0:T(8,128)(2,1)} %get-tuple-element.63), channel_id=1, source_target_pairs={{0,96},{16,112},{32,0},{48,16},{64,32},{80,48},{96,64},{112,80},{1... | collective-permute-start | bytes 221192 | tf_op jit(solution)/shard_map/ppermute | solution.py:22
  155.1 8.9 %collective-permute-start.20 = (bf16[1,192,384]{2,1,0:T(8,128)(2,1)}, bf16[1,192,384]{2,1,0:T(8,128)(2,1)S(1)}, u32[]{:S(2)}, u32[]{:S(2)}) collective-permute-start(bf16[1,192,384]{2,1,0:T(8,128)(2,1)} %get-tuple-element.66), channel_id=1, source_target_pairs={{0,32},{16,48},{32,64},{48,80},{64,96},{80,112},{96,0},{112,16},{1... | collective-permute-start | bytes 442376 | tf_op jit(solution)/shard_map/ppermute | solution.py:22
  155.7 9.4 %collective-permute-start.21 = (bf16[1,192,384]{2,1,0:T(8,128)(2,1)}, bf16[1,192,384]{2,1,0:T(8,128)(2,1)S(1)}, u32[]{:S(2)}, u32[]{:S(2)}) collective-permute-start(bf16[1,192,384]{2,1,0:T(8,128)(2,1)} %get-tuple-element.67), channel_id=1, source_target_pairs={{0,96},{16,112},{32,0},{48,16},{64,32},{80,48},{96,64},{112,80},{1... | collective-permute-start | bytes 442376 | tf_op jit(solution)/shard_map/ppermute | solution.py:22
  168.0 14.4 %all-to-all-start.1 = ((f32[16,8,128]{2,1,0:T(8,128)}), f32[16,8,128]{2,1,0:T(8,128)S(1)}, u32[]{:S(2)}, u32[]{:S(2)}) async-start(f32[16,8,128]{2,1,0:T(8,128)} %get-tuple-element.68), calls=%async_computation.2 | async-start | bytes 131072 | tf_op jit(solution)/shard_map/all_to_all | solution.py:455
  175.6 13.9 %collective-permute-start.22 = (bf16[96,768]{1,0:T(8,128)(2,1)S(1)}, bf16[96,768]{1,0:T(8,128)(2,1)S(1)}, u32[]{:S(2)}, u32[]{:S(2)}) collective-permute-start(bf16[96,768]{1,0:T(8,128)(2,1)S(1)} %get-tuple-element.77), channel_id=1, source_target_pairs={{0,0},{8,128},{128,8},{136,136},{16,16},{24,144},{144,24},{152,152... | collective-permute-start | bytes 442376 | tf_op jit(solution)/shard_map/ppermute | solution.py:452
  180.2 9.3 %collective-permute-start.23 = (bf16[96,768]{1,0:T(8,128)(2,1)S(1)}, bf16[96,768]{1,0:T(8,128)(2,1)S(1)}, u32[]{:S(2)}, u32[]{:S(2)}) collective-permute-start(bf16[96,768]{1,0:T(8,128)(2,1)S(1)} %get-tuple-element.76), channel_id=1, source_target_pairs={{0,8},{8,136},{128,0},{136,128},{16,24},{24,152},{144,16},{152,144... | collective-permute-start | bytes 442376 | tf_op jit(solution)/shard_map/ppermute | solution.py:453
  183.1 13.0 %all-to-all-start.2 = ((f32[16,8,128]{2,1,0:T(8,128)}), f32[16,8,128]{2,1,0:T(8,128)S(1)}, u32[]{:S(2)}, u32[]{:S(2)}) async-start(f32[16,8,128]{2,1,0:T(8,128)} %squares.1), calls=%async_computation.3 | async-start | bytes 131072 | tf_op jit(solution)/shard_map/all_to_all | solution.py:457
  (36 other events, 258.6 us)
Sparse Core Ops, SparseCore 0:
  35.5 35.7 all-gather.2
  73.1 33.2 all-gather.4
  108.9 37.8 reduce-scatter.1

commit v4 on v3

--- a/solution.py
+++ b/solution.py
@@ -20,6 +20,14 @@
 
 def shift(x, axis, size, by):
     return lax.ppermute(x, axis, [(i, (i + by) % size) for i in range(size)])
+
+
+def shift_by_core(x, by):
+    pairs = []
+    for place in range(Z):
+        pairs.append((place * CORE, (place + by) % Z * CORE))
+        pairs.append((place * CORE + 1, (place - by) % Z * CORE + 1))
+    return lax.ppermute(x, ("z", "core"), pairs)
 
 
 def swap(x, axis, size, mask=1):
@@ -138,10 +146,10 @@
     return log_add(mine[...], other)
 
 
-def d_value_body(heads, slots, numbers, arriving, leaving):
+def d_value_body(heads, distances, numbers, arriving, leaving):
     (here,) = numbers
     query, d_attn, mine, other = arriving[:4]
-    keys, pieces = arriving[4:], len(slots)
+    keys, pieces = arriving[4:], len(distances)
     out, att = leaving
     half = att.ref.shape[2]
     totals = both_totals(mine, other)
@@ -159,9 +167,8 @@
         cols = head_cols(head)
         probs = jnp.exp(block - totals[head : head + 1, :]).astype(BF16)
         d_value = jnp.dot(probs, d_attn[:, cols], preferred_element_type=F32)
-        distance, start = slots[piece]
-        owner = lax.rem(here + (Z - distance), Z)
-        out.ref[owner, start : start + probs.shape[0], cols] = d_value.astype(BF16)
+        owner = lax.rem(here + (Z - distances[piece]), Z)
+        out.ref[owner, :, cols] = d_value.astype(BF16)
         first = (((0,), (0,)), ((), ()))
         value = keys[piece][:, head_cols(heads + head)]
         term = lax.dot_general(value, probs, first, preferred_element_type=F32)
@@ -187,19 +194,17 @@
     (here,) = numbers
     mine, other, dv_mine, dv_other = [one.ref() for one in arriving]
     rows = leaving[0].ref.shape[1]
-    for output, part, ahead, start, count in (
-        (2, 0, 4, 0, rows // 2),
-        (3, 0, 4, rows // 2, rows // 2),
-        (0, 0, 1, 0, rows),
-        (0, 1, 3, 0, rows),
-        (1, 0, 7, 0, rows),
-        (1, 1, 5, 0, rows),
-        (4, 0, 2, 0, rows),
-        (5, 0, 6, 0, rows),
-        (6, 0, 0, 0, rows),
+    for output, part, ahead in (
+        (2, 0, 4),
+        (0, 0, 1),
+        (0, 1, 3),
+        (1, 0, 7),
+        (1, 1, 5),
+        (3, 0, 2),
+        (4, 0, 6),
+        (5, 0, 0),
     ):
-        first = lax.rem(here + ahead, Z) * rows + start
-        at = pl.ds(pl.multiple_of(first, rows // 2), count)
+        at = pl.ds(pl.multiple_of(lax.rem(here + ahead, Z) * rows, rows), rows)
         product = jnp.dot(mine[at, :], dv_mine[...], preferred_element_type=F32)
         product += jnp.dot(other[at, :], dv_other[...], preferred_element_type=F32)
         leaving[output].ref[part] = product.astype(BF16)
@@ -222,17 +227,14 @@
 
 
 def relay_body(numbers, arriving, leaving):
-    near_f, near_b, far_f, far_b, keep_f, keep_b = arriving
-    half = far_f.ref().shape[1]
-    for near, far, keep, send, low in (
-        (near_f, far_f, keep_f, leaving[0], 0),
-        (near_b, far_b, keep_b, leaving[1], half),
+    (core,) = numbers
+    near_f, near_b, far, keep_f, keep_b = arriving
+    for near, keep, send, takes in (
+        (near_f, keep_f, leaving[0], core == 0),
+        (near_b, keep_b, leaving[1], core == 1),
     ):
-        at, rest = slice(low, low + half), slice(half - low, 2 * half - low)
-        through = near[1, at, :].astype(F32) + far[0].astype(F32)
-        send.ref[0, at, :] = (keep[0, at, :].astype(F32) + through).astype(BF16)
-        through = near[1, rest, :].astype(F32)
-        send.ref[0, rest, :] = (keep[0, rest, :].astype(F32) + through).astype(BF16)
+        through = near[1].astype(F32) + jnp.where(takes, far[0].astype(F32), 0.0)
+        send.ref[0] = (keep[0].astype(F32) + through).astype(BF16)
         send.send()
 
 
@@ -351,8 +353,7 @@
         if step == 3:
             stats = stats_of(pieces[:3])
             forward, backward, stats = lax.optimization_barrier((forward, backward, stats))
-    half = chunk.shape[0] // 2
-    pieces += [shift(forward[:half], "z", Z, 1), shift(backward[half:], "z", Z, -1)]
+    pieces.append(shift_by_core(jnp.where(core == 0, forward, backward), 1))
     stats = stats_of(pieces[3:7], stats)
     stats = stats_of(pieces[7:], stats)
     other_stats = swap(stats, "core", CORE)
@@ -360,26 +361,26 @@
     def block(parts, count):
         return shape((parts, count, columns), BF16)
 
-    def start_scatter(near_f, near_b, far_f, far_b):
-        return (
-            shift(near_f, "z", Z, 1),
-            shift(near_b, "z", Z, -1),
-            shift(far_f, "z", Z, 2),
-            shift(far_b, "z", Z, -2),
-        )
+    def start_scatter(near_f, near_b, far):
+        return shift(near_f, "z", Z, 1), shift(near_b, "z", Z, -1), shift_by_core(far, 2)
 
     def relay(arrived, keep_f, keep_b):
         like = shape(keep_f.shape, BF16)
         return call(
-            relay_body, "relay", (), (*arrived, keep_f, keep_b), (like, like), vmem=LARGE
+            relay_body,
+            "relay",
+            (this_core,),
+            (*arrived, keep_f, keep_b),
+            (like, like),
+            vmem=LARGE,
         )
 
     def end_scatter(arrived, sums, own):
         return own, arrived[0], arrived[1], shift(sums[0], "z", Z, 2), shift(sums[1], "z", Z, -2)
 
-    slots = ((0, 0), (1, 0), (7, 0), (2, 0), (6, 0), (3, 0), (5, 0), (4, 0), (4, half))
+    distances = (0, 1, 7, 2, 6, 3, 5, 4)
     d_value, attended = call(
-        functools.partial(d_value_body, heads, slots),
+        functools.partial(d_value_body, heads, distances),
         "d_value",
         (here,),
         (queries_d, queries_d, stats, other_stats, *pieces),
@@ -427,11 +428,11 @@
         "per_value",
         (here,),
         (*tokens_half, d_value, swap(d_value, "core", CORE)),
-        (block(2, count), block(2, count), block(1, count // 2), block(1, count // 2)) + (block(1, count),) * 3,
+        (block(2, count), block(2, count)) + (block(1, count),) * 4,
         vmem=LARGE,
     )
-    arrived = start_scatter(*parts[:4])
-    terms = end_scatter(arrived, relay(arrived, *parts[4:6]), parts[6])
+    arrived = start_scatter(*parts[:3])
+    terms = end_scatter(arrived, relay(arrived, *parts[3:5]), parts[5])
     small = shape((Z * CORE, 8, 128), F32)
     shard, square = call(
         shard_body,

time: 205 us -> 204 us (level)
  starting transfers between devices: 65.4 us -> 62.5 us
    ppermute x0 -> x2, waiting for transfers between devices: none -> 16.5 us  [shift_by_core(): return lax.ppermute(x, ('z', 'core'), pairs)]
    ppermute x14 -> x10, waiting for transfers between devices: 25.5 us -> 9.58 us  [shift(): return lax.ppermute(x, axis, [(i, (i + by) % size) for i in range(size)])]
    ppermute x14 -> x10, starting transfers between devices: 24.3 us -> 18.6 us  [shift(): return lax.ppermute(x, axis, [(i, (i + by) % size) for i in range(size)])]
    unnamed x61 -> x57, local copies, waits for them, and re-layouts: 6.72 us -> 9.73 us
    all_to_all x1, waiting for transfers between devices: 15.2 us -> 13.1 us  [local(): terms = lax.all_to_all(d_value, 'z', 0, 0, tiled=True)]
  transfers between devices with their start and end apart: 30 -> 28, of which waited for: 15 -> 13; matrix products, arithmetic and copies ran while one was open for 6% -> 5% of each run, Pallas kernels for 17% -> 17%
where the time goes in v4:
time: 204 us; the launch traced here: 203 us
  waiting for transfers between devices  64.6 us (32%)
  starting transfers between devices  62.5 us (31%)
  Pallas kernels  37.7 us (18%)
  local copies, waits for them, and re-layouts  15 us (7%)
  between operations  14.2 us (7%)
  matrix products  7.15 us (4%)
  other arithmetic  2.06 us (1%)
    pallas_call x13, Pallas kernels, call(): pl.pallas_call(kernel, out_shape=tuple(outputs), in_specs=[smem] * n_scal...  37.7 us
    ppermute x8, starting transfers between devices, swap(): return lax.ppermute(x, axis, [(i, i ^ mask) for i in range(size)])  20 us
    ppermute x10, starting transfers between devices, shift(): return lax.ppermute(x, axis, [(i, (i + by) % size) for i in range(size)])  18.6 us
    ppermute x2, waiting for transfers between devices, shift_by_core(): return lax.ppermute(x, ('z', 'core'), pairs)  16.5 us
    all_to_all x1, waiting for transfers between devices, local(): terms = lax.all_to_all(d_value, 'z', 0, 0, tiled=True)  13.1 us
    all_gather x2, waiting for transfers between devices, from_partner(): return lax.all_gather(pick(array, 1 - image), 'yh', axis=0)  9.96 us
    unnamed x57, local copies, waits for them, and re-layouts  9.73 us
    ppermute x10, waiting for transfers between devices, shift(): return lax.ppermute(x, axis, [(i, (i + by) % size) for i in range(size)])  9.58 us
  transfers between devices with their start and end apart: 28, of which 13 were waited for; matrix products, arithmetic and copies ran while one was open for 5% of the time, Pallas kernels for 17%

profile of v4, /device:TPU:1, one launch (start us, length us, event | category | flops | bytes accessed | tf_op | source)
XLA Modules:
  0.0 203.2 jit_solution(15109905462066686712)
XLA Ops:
  12.6 3.8 %collective-permute-start = (bf16[128,768]{1,0:T(8,128)(2,1)S(1)}, bf16[128,768]{1,0:T(8,128)(2,1)S(1)}, u32[]{:S(2)}, u32[]{:S(2)}) collective-permute-start(bf16[128,768]{1,0:T(8,128)(2,1)S(1)} %get-tuple-element.73), channel_id=1, source_target_pairs={{0,128},{128,0},{1,129},{129,1},{2,130},{130,2},{3,131},{131,3},{4... | collective-permute-start | bytes 589832 | tf_op jit(solution)/shard_map/ppermute | solution.py:34
  22.5 4.0 %collective-permute-start.2 = (bf16[256,768]{1,0:T(8,128)(2,1)S(1)}, bf16[256,768]{1,0:T(8,128)(2,1)}, u32[]{:S(2)}, u32[]{:S(2)}) collective-permute-start(bf16[256,768]{1,0:T(8,128)(2,1)S(1)} %pad_maximum_fusion.1.refs_1_.refs_5_), channel_id=1, source_target_pairs={{0,112},{16,0},{32,16},{48,32},{64,48},{80,64},{96,80},{112,96},{1... | collective-permute-start | bytes 1179656 | tf_op jit(solution)/shard_map/ppermute | solution.py:22
  27.3 3.0 %collective-permute-start.3 = (bf16[128,768]{1,0:T(8,128)(2,1)S(1)}, bf16[128,768]{1,0:T(8,128)(2,1)S(1)}, u32[]{:S(2)}, u32[]{:S(2)}) collective-permute-start(bf16[128,768]{1,0:T(8,128)(2,1)S(1)} %get-tuple-element.71), channel_id=1, source_target_pairs={{0,128},{128,0},{1,129},{129,1},{2,130},{130,2},{3,131},{131,3},{4... | collective-permute-start | bytes 589832 | tf_op jit(solution)/shard_map/ppermute | solution.py:34
  30.3 3.1 %collective-permute-done.3 = bf16[128,768]{1,0:T(8,128)(2,1)S(1)} collective-permute-done((bf16[128,768]{1,0:T(8,128)(2,1)S(1)}, bf16[128,768]{1,0:T(8,128)(2,1)S(1)}, u32[]{:S(2)}, u32[]{:S(2)}) %collective-permute-start.3) | collective-permute-done | bytes 196640 | tf_op jit(solution)/shard_map/ppermute | solution.py:34
  38.2 3.4 %collective-permute-start.4 = (bf16[256,768]{1,0:T(8,128)(2,1)}, bf16[256,768]{1,0:T(8,128)(2,1)}, u32[]{:S(2)}, u32[]{:S(2)}) collective-permute-start(bf16[256,768]{1,0:T(8,128)(2,1)} %pad_maximum_fusion.3), channel_id=1, source_target_pairs={{0,8},{8,0},{1,9},{9,1},{2,10},{10,2},{3,11},{11,3},{4,12},{12,4},... | collective-permute-start | bytes 1179656 | tf_op jit(solution)/shard_map/ppermute | solution.py:34
  57.1 3.8 %stats.4.refs_2_ = f32[8,512]{1,0:T(8,128)S(1)} custom-call(bf16[512,768]{1,0:T(8,128)(2,1)S(1)} %constant_dynamic-update-slice_fusion.refs_0_.refs_1_.refs_2_, bf16[256,768]{1,0:T(8,128)(2,1)} %collective-permute-done.5.refs_1_.refs_8_, bf16[256,768]{1,0:T(8,128)(2,1)} %collective-permute-done.7.refs_2_.refs_9_, ...), custom_call_target="tpu_custom_call" | custom-call | flops 1000 | tf_op jit(solution)/shard_map/stats/pallas_call | solution.py:106
  60.9 2.8 %collective-permute-done.9.refs_1_.refs_12_ = bf16[256,768]{1,0:T(8,128)(2,1)S(1)} collective-permute-done((bf16[256,768]{1,0:T(8,128)(2,1)S(1)}, bf16[256,768]{1,0:T(8,128)(2,1)S(1)}, u32[]{:S(2)}, u32[]{:S(2)}) %collective-permute-start.9) | collective-permute-done | bytes 393248 | tf_op jit(solution)/shard_map/ppermute | solution.py:30
  64.4 5.2 %collective-permute-start.10 = (f32[8,512]{1,0:T(8,128)S(1)}, f32[8,512]{1,0:T(8,128)S(1)}, u32[]{:S(2)}, u32[]{:S(2)}) collective-permute-start(f32[8,512]{1,0:T(8,128)S(1)} %stats.5.refs_3_), channel_id=1, source_target_pairs={{0,8},{8,0},{1,9},{9,1},{2,10},{10,2},{3,11},{11,3},{4,12},{12,4},... | collective-permute-start | bytes 49160 | tf_op jit(solution)/shard_map/ppermute | solution.py:34
  71.1 9.1 %d_value.1 = (bf16[8,256,384]{2,1,0:T(8,128)(2,1)}, bf16[2,384,256]{2,1,0:T(8,128)(2,1)}) custom-call(s32[1]{0:T(128)} %bitcast.2.refs_0_, bf16[512,768]{1,0:T(8,128)(2,1)} %copy-done.1, bf16[512,768]{1,0:T(8,128)(2,1)} %copy-done.1, f32[8,512]{1,0:T(8,128)} %copy-done.11, f32[8,512]{1,0:T(8,128)} %copy-done.25, bf16[256,768]{1,0:T(8,128)(2,1)} %copy-done.3, ...), custom_call_target="tpu_custom_call" | custom-call | flops 1000 | tf_op jit(solution)/shard_map/d_value/pallas_call | solution.py:106
  80.2 5.2 %all-to-all-start = ((bf16[8,256,384]{2,1,0:T(8,128)(2,1)}), bf16[8,256,384]{2,1,0:T(8,128)(2,1)}, u32[]{:S(2)}, u32[]{:S(2)}) async-start(bf16[8,256,384]{2,1,0:T(8,128)(2,1)} %get-tuple-element.57), calls=%async_computation.1 | async-start | bytes 3145728 | tf_op jit(solution)/shard_map/all_to_all | solution.py:392
  85.7 3.0 %turn.2 = (bf16[1536,256]{1,0:T(8,128)(2,1)}, bf16[1536,256]{1,0:T(8,128)(2,1)}) custom-call(s32[1]{0:T(128)} %bitcast.refs_0_, s32[1]{0:T(128)} %bitcast.1.refs_1_, bf16[2,128,3072]{2,1,0:T(8,128)(2,1)} %refs_2_, bf16[2,128,3072]{2,1,0:T(8,128)(2,1)} %all-gather.3.cloned.1.call-done.refs_3_), custom_call_target="tpu_custom_call" | custom-call | flops 1000 | tf_op jit(solution)/shard_map/turn/pallas_call | solution.py:106
  93.0 4.0 %per_out.1 = bf16[1536,384]{1,0:T(8,128)(2,1)} custom-call(bf16[1536,256]{1,0:T(8,128)(2,1)} %get-tuple-element.48.refs_0_, bf16[1536,256]{1,0:T(8,128)(2,1)} %copy-done.17, bf16[2,384,256]{2,1,0:T(8,128)(2,1)} %get-tuple-element.50.refs_2_, bf16[2,384,256]{2,1,0:T(8,128)(2,1)} %copy-done.20), custom_call_target="tpu_custom_call" | custom-call | flops 1000 | tf_op jit(solution)/shard_map/per_out/pallas_call | solution.py:106
  97.0 9.9 %all-gather.5.cloned.1.call-done.refs_3_ = bf16[2,128,3072]{2,1,0:T(8,128)(2,1)} async-done(((bf16[1,128,3072]{2,1,0:T(8,128)(2,1)}), bf16[2,128,3072]{2,1,0:T(8,128)(2,1)}) %all-gather.5.cloned.1.call-update) | async-done | bytes 1572880 | tf_op jit(solution)/shard_map/all_gather | solution.py:313
  107.0 2.9 %turn.3 = (bf16[1536,256]{1,0:T(8,128)(2,1)}, bf16[1536,256]{1,0:T(8,128)(2,1)}) custom-call(s32[1]{0:T(128)} %bitcast.refs_0_, s32[1]{0:T(128)} %bitcast.1.refs_1_, bf16[2,128,3072]{2,1,0:T(8,128)(2,1)} %refs_2_.1, bf16[2,128,3072]{2,1,0:T(8,128)(2,1)} %all-gather.5.cloned.1.call-done.refs_3_), custom_call_target="tpu_custom_call" | custom-call | flops 1000 | tf_op jit(solution)/shard_map/turn/pallas_call | solution.py:106
  110.7 13.1 %all-to-all-done.refs_0_ = bf16[8,256,384]{2,1,0:T(8,128)(2,1)} async-done(((bf16[8,256,384]{2,1,0:T(8,128)(2,1)}), bf16[8,256,384]{2,1,0:T(8,128)(2,1)}, u32[]{:S(2)}, u32[]{:S(2)}) %all-to-all-start) | async-done | bytes 1572896 | tf_op jit(solution)/shard_map/all_to_all | solution.py:392
  125.7 2.9 %collective-permute-start.14 = (bf16[256,384]{1,0:T(8,128)(2,1)S(1)}, bf16[256,384]{1,0:T(8,128)(2,1)S(1)}, u32[]{:S(2)}, u32[]{:S(2)}) collective-permute-start(bf16[256,384]{1,0:T(8,128)(2,1)S(1)} %d_value_sum.1.refs_3_), channel_id=1, source_target_pairs={{0,8},{8,0},{1,9},{9,1},{2,10},{10,2},{3,11},{11,3},{4,12},{12,4},... | collective-permute-start | bytes 589832 | tf_op jit(solution)/shard_map/ppermute | solution.py:34
  130.3 3.2 %per_value.1 = (bf16[2,192,384]{2,1,0:T(8,128)(2,1)}, bf16[2,192,384]{2,1,0:T(8,128)(2,1)}, bf16[1,192,384]{2,1,0:T(8,128)(2,1)}, bf16[1,192,384]{2,1,0:T(8,128)...) custom-call(s32[1]{0:T(128)} %bitcast.2.refs_0_, bf16[1536,256]{1,0:T(8,128)(2,1)} %get-tuple-element.55.refs_1_, ...), custom_call_target="tpu_custom_call" | custom-call | flops 1000 | tf_op jit(solution)/shard_map/per_value/pallas_call | solution.py:106
  136.3 13.7 %collective-permute-done.17.refs_3_ = bf16[1,192,384]{2,1,0:T(8,128)(2,1)S(1)} collective-permute-done((bf16[1,192,384]{2,1,0:T(8,128)(2,1)}, bf16[1,192,384]{2,1,0:T(8,128)(2,1)S(1)}, u32[]{:S(2)}, u32[]{:S(2)}) %collective-permute-start.17) | collective-permute-done | bytes 147488 | tf_op jit(solution)/shard_map/ppermute | solution.py:30
  153.0 3.8 %collective-permute-start.19 = (bf16[1,192,384]{2,1,0:T(8,128)(2,1)}, bf16[1,192,384]{2,1,0:T(8,128)(2,1)S(1)}, u32[]{:S(2)}, u32[]{:S(2)}) collective-permute-start(bf16[1,192,384]{2,1,0:T(8,128)(2,1)} %get-tuple-element.65), channel_id=1, source_target_pairs={{0,96},{16,112},{32,0},{48,16},{64,32},{80,48},{96,64},{112,80},{1... | collective-permute-start | bytes 442376 | tf_op jit(solution)/shard_map/ppermute | solution.py:22
  156.9 7.6 %collective-permute-done.18.refs_4_ = bf16[1,192,384]{2,1,0:T(8,128)(2,1)S(1)} collective-permute-done((bf16[1,192,384]{2,1,0:T(8,128)(2,1)}, bf16[1,192,384]{2,1,0:T(8,128)(2,1)S(1)}, u32[]{:S(2)}, u32[]{:S(2)}) %collective-permute-start.18) | collective-permute-done | bytes 147488 | tf_op jit(solution)/shard_map/ppermute | solution.py:22
  167.4 5.7 %all-to-all-start.1 = ((f32[16,8,128]{2,1,0:T(8,128)}), f32[16,8,128]{2,1,0:T(8,128)S(1)}, u32[]{:S(2)}, u32[]{:S(2)}) async-start(f32[16,8,128]{2,1,0:T(8,128)} %get-tuple-element.66), calls=%async_computation.2 | async-start | bytes 131072 | tf_op jit(solution)/shard_map/all_to_all | solution.py:456
  174.1 5.1 %collective-permute-start.20 = (bf16[96,768]{1,0:T(8,128)(2,1)S(1)}, bf16[96,768]{1,0:T(8,128)(2,1)S(1)}, u32[]{:S(2)}, u32[]{:S(2)}) collective-permute-start(bf16[96,768]{1,0:T(8,128)(2,1)S(1)} %get-tuple-element.75), channel_id=1, source_target_pairs={{0,0},{8,128},{128,8},{136,136},{16,16},{24,144},{144,24},{152,152... | collective-permute-start | bytes 442376 | tf_op jit(solution)/shard_map/ppermute | solution.py:453
  181.6 6.9 %all-to-all-start.2 = ((f32[16,8,128]{2,1,0:T(8,128)}), f32[16,8,128]{2,1,0:T(8,128)S(1)}, u32[]{:S(2)}, u32[]{:S(2)}) async-start(f32[16,8,128]{2,1,0:T(8,128)} %squares.1), calls=%async_computation.3 | async-start | bytes 131072 | tf_op jit(solution)/shard_map/all_to_all | solution.py:458
  188.5 6.5 %all-to-all-done.2.refs_1_ = f32[16,8,128]{2,1,0:T(8,128)S(1)} async-done(((f32[16,8,128]{2,1,0:T(8,128)}), f32[16,8,128]{2,1,0:T(8,128)S(1)}, u32[]{:S(2)}, u32[]{:S(2)}) %all-to-all-start.2) | async-done | bytes 65568 | tf_op jit(solution)/shard_map/all_to_all | solution.py:458
  (120 shorter events, 57.1 us)
Async XLA Ops:
  7.2 78.5 %all-gather.3.cloned.1.call-start = ((), (), s32[]{:S(2)}) async-start(), calls=%async_computation.4 | async-start | bytes 2359296 | tf_op jit(solution)/shard_map/all_gather | solution.py:313
  12.6 7.5 %collective-permute-start = (bf16[128,768]{1,0:T(8,128)(2,1)S(1)}, bf16[128,768]{1,0:T(8,128)(2,1)S(1)}, u32[]{:S(2)}, u32[]{:S(2)}) collective-permute-start(bf16[128,768]{1,0:T(8,128)(2,1)S(1)} %get-tuple-element.73), channel_id=1, source_target_pairs={{0,128},{128,0},{1,129},{129,1},{2,130},{130,2},{3,131},{131,3},{4... | collective-permute-start | bytes 589832 | tf_op jit(solution)/shard_map/ppermute | solution.py:34
  20.1 14.2 %collective-permute-start.1 = (bf16[256,768]{1,0:T(8,128)(2,1)S(1)}, bf16[256,768]{1,0:T(8,128)(2,1)S(1)}, u32[]{:S(2)}, u32[]{:S(2)}) collective-permute-start(bf16[256,768]{1,0:T(8,128)(2,1)S(1)} %pad_maximum_fusion.1.refs_1_.refs_5_), channel_id=1, source_target_pairs={{0,16},{16,32},{32,48},{48,64},{64,80},{80,96},{96,112},{112,0},{1... | collective-permute-start | bytes 1179656 | tf_op jit(solution)/shard_map/ppermute | solution.py:22
  22.5 11.8 %collective-permute-start.2 = (bf16[256,768]{1,0:T(8,128)(2,1)S(1)}, bf16[256,768]{1,0:T(8,128)(2,1)}, u32[]{:S(2)}, u32[]{:S(2)}) collective-permute-start(bf16[256,768]{1,0:T(8,128)(2,1)S(1)} %pad_maximum_fusion.1.refs_1_.refs_5_), channel_id=1, source_target_pairs={{0,112},{16,0},{32,16},{48,32},{64,48},{80,64},{96,80},{112,96},{1... | collective-permute-start | bytes 1179656 | tf_op jit(solution)/shard_map/ppermute | solution.py:22
  27.3 6.1 %collective-permute-start.3 = (bf16[128,768]{1,0:T(8,128)(2,1)S(1)}, bf16[128,768]{1,0:T(8,128)(2,1)S(1)}, u32[]{:S(2)}, u32[]{:S(2)}) collective-permute-start(bf16[128,768]{1,0:T(8,128)(2,1)S(1)} %get-tuple-element.71), channel_id=1, source_target_pairs={{0,128},{128,0},{1,129},{129,1},{2,130},{130,2},{3,131},{131,3},{4... | collective-permute-start | bytes 589832 | tf_op jit(solution)/shard_map/ppermute | solution.py:34
  35.4 71.5 %all-gather.5.cloned.1.call-start = ((), (), s32[]{:S(2)}) async-start(), calls=%async_computation.5 | async-start | bytes 2359296 | tf_op jit(solution)/shard_map/all_gather | solution.py:313
  35.5 9.1 %collective-permute-start.5 = (bf16[256,768]{1,0:T(8,128)(2,1)S(1)}, bf16[256,768]{1,0:T(8,128)(2,1)}, u32[]{:S(2)}, u32[]{:S(2)}) collective-permute-start(bf16[256,768]{1,0:T(8,128)(2,1)S(1)} %collective-permute-done.1.refs_2_.refs_6_), channel_id=1, source_target_pairs={{0,16},{16,32},{32,48},{48,64},{64,80},{80,96},{96,112},{112,0},{1... | collective-permute-start | bytes 1179656 | tf_op jit(solution)/shard_map/ppermute | solution.py:22
  35.6 9.0 %collective-permute-start.7 = (bf16[256,768]{1,0:T(8,128)(2,1)}, bf16[256,768]{1,0:T(8,128)(2,1)}, u32[]{:S(2)}, u32[]{:S(2)}) collective-permute-start(bf16[256,768]{1,0:T(8,128)(2,1)} %collective-permute-done.2.refs_3_.refs_7_), channel_id=1, source_target_pairs={{0,112},{16,0},{32,16},{48,32},{64,48},{80,64},{96,80},{112,96},{1... | collective-permute-start | bytes 1179656 | tf_op jit(solution)/shard_map/ppermute | solution.py:22
  38.2 11.1 %collective-permute-start.4 = (bf16[256,768]{1,0:T(8,128)(2,1)}, bf16[256,768]{1,0:T(8,128)(2,1)}, u32[]{:S(2)}, u32[]{:S(2)}) collective-permute-start(bf16[256,768]{1,0:T(8,128)(2,1)} %pad_maximum_fusion.3), channel_id=1, source_target_pairs={{0,8},{8,0},{1,9},{9,1},{2,10},{10,2},{3,11},{11,3},{4,12},{12,4},... | collective-permute-start | bytes 1179656 | tf_op jit(solution)/shard_map/ppermute | solution.py:34
  44.6 10.8 %collective-permute-start.6 = (bf16[256,768]{1,0:T(8,128)(2,1)}, bf16[256,768]{1,0:T(8,128)(2,1)S(1)}, u32[]{:S(2)}, u32[]{:S(2)}) collective-permute-start(bf16[256,768]{1,0:T(8,128)(2,1)} %collective-permute-done.5.refs_1_.refs_8_), channel_id=1, source_target_pairs={{0,16},{16,32},{32,48},{48,64},{64,80},{80,96},{96,112},{112,0},{1... | collective-permute-start | bytes 1179656 | tf_op jit(solution)/shard_map/ppermute | solution.py:22
  44.6 10.8 %collective-permute-start.8 = (bf16[256,768]{1,0:T(8,128)(2,1)}, bf16[256,768]{1,0:T(8,128)(2,1)}, u32[]{:S(2)}, u32[]{:S(2)}) collective-permute-start(bf16[256,768]{1,0:T(8,128)(2,1)} %collective-permute-done.7.refs_2_.refs_9_), channel_id=1, source_target_pairs={{0,112},{16,0},{32,16},{48,32},{64,48},{80,64},{96,80},{112,96},{1... | collective-permute-start | bytes 1179656 | tf_op jit(solution)/shard_map/ppermute | solution.py:22
  56.5 7.1 %collective-permute-start.9 = (bf16[256,768]{1,0:T(8,128)(2,1)S(1)}, bf16[256,768]{1,0:T(8,128)(2,1)S(1)}, u32[]{:S(2)}, u32[]{:S(2)}) collective-permute-start(bf16[256,768]{1,0:T(8,128)(2,1)S(1)} %broadcast_select_fusion), channel_id=1, source_target_pairs={{0,16},{8,120},{16,32},{24,8},{32,48},{40,24},{48,64},{56,40},{64,... | collective-permute-start | bytes 1179656 | tf_op jit(solution)/shard_map/ppermute | solution.py:30
  80.2 43.6 %all-to-all-start = ((bf16[8,256,384]{2,1,0:T(8,128)(2,1)}), bf16[8,256,384]{2,1,0:T(8,128)(2,1)}, u32[]{:S(2)}, u32[]{:S(2)}) async-start(bf16[8,256,384]{2,1,0:T(8,128)(2,1)} %get-tuple-element.57), calls=%async_computation.1 | async-start | bytes 3145728 | tf_op jit(solution)/shard_map/all_to_all | solution.py:392
  85.4 79.1 %reduce-scatter.2.cloned.1.call-start = ((), (), s32[]{:S(2)}) async-start(), calls=%async_computation.6 | async-start | bytes 1327104 | tf_op jit(solution)/shard_map/reduce_scatter | solution.py:421
  109.9 18.6 %collective-permute-start.13 = (bf16[1536,256]{1,0:T(8,128)(2,1)}, bf16[1536,256]{1,0:T(8,128)(2,1)S(1)}, u32[]{:S(2)}, u32[]{:S(2)}) collective-permute-start(bf16[1536,256]{1,0:T(8,128)(2,1)} %get-tuple-element.56), channel_id=1, source_target_pairs={{0,8},{8,0},{1,9},{9,1},{2,10},{10,2},{3,11},{11,3},{4,12},{12,4},... | collective-permute-start | bytes 2359304 | tf_op jit(solution)/shard_map/ppermute | solution.py:34
  133.5 16.5 %collective-permute-start.15 = (bf16[2,192,384]{2,1,0:T(8,128)(2,1)}, bf16[2,192,384]{2,1,0:T(8,128)(2,1)S(1)}, u32[]{:S(2)}, u32[]{:S(2)}) collective-permute-start(bf16[2,192,384]{2,1,0:T(8,128)(2,1)} %get-tuple-element.59), channel_id=1, source_target_pairs={{0,16},{16,32},{32,48},{48,64},{64,80},{80,96},{96,112},{112,0},{1... | collective-permute-start | bytes 884744 | tf_op jit(solution)/shard_map/ppermute | solution.py:22
  133.9 16.1 %collective-permute-start.16 = (bf16[2,192,384]{2,1,0:T(8,128)(2,1)}, bf16[2,192,384]{2,1,0:T(8,128)(2,1)S(1)}, u32[]{:S(2)}, u32[]{:S(2)}) collective-permute-start(bf16[2,192,384]{2,1,0:T(8,128)(2,1)} %get-tuple-element.60), channel_id=1, source_target_pairs={{0,112},{16,0},{32,16},{48,32},{64,48},{80,64},{96,80},{112,96},{1... | collective-permute-start | bytes 884744 | tf_op jit(solution)/shard_map/ppermute | solution.py:22
  136.3 13.7 %collective-permute-start.17 = (bf16[1,192,384]{2,1,0:T(8,128)(2,1)}, bf16[1,192,384]{2,1,0:T(8,128)(2,1)S(1)}, u32[]{:S(2)}, u32[]{:S(2)}) collective-permute-start(bf16[1,192,384]{2,1,0:T(8,128)(2,1)} %get-tuple-element.61), channel_id=1, source_target_pairs={{0,32},{8,104},{16,48},{24,120},{32,64},{40,8},{48,80},{56,24},{64... | collective-permute-start | bytes 442376 | tf_op jit(solution)/shard_map/ppermute | solution.py:30
  152.8 11.6 %collective-permute-start.18 = (bf16[1,192,384]{2,1,0:T(8,128)(2,1)}, bf16[1,192,384]{2,1,0:T(8,128)(2,1)S(1)}, u32[]{:S(2)}, u32[]{:S(2)}) collective-permute-start(bf16[1,192,384]{2,1,0:T(8,128)(2,1)} %get-tuple-element.64), channel_id=1, source_target_pairs={{0,32},{16,48},{32,64},{48,80},{64,96},{80,112},{96,0},{112,16},{1... | collective-permute-start | bytes 442376 | tf_op jit(solution)/shard_map/ppermute | solution.py:22
  153.0 11.4 %collective-permute-start.19 = (bf16[1,192,384]{2,1,0:T(8,128)(2,1)}, bf16[1,192,384]{2,1,0:T(8,128)(2,1)S(1)}, u32[]{:S(2)}, u32[]{:S(2)}) collective-permute-start(bf16[1,192,384]{2,1,0:T(8,128)(2,1)} %get-tuple-element.65), channel_id=1, source_target_pairs={{0,96},{16,112},{32,0},{48,16},{64,32},{80,48},{96,64},{112,80},{1... | collective-permute-start | bytes 442376 | tf_op jit(solution)/shard_map/ppermute | solution.py:22
  167.4 13.5 %all-to-all-start.1 = ((f32[16,8,128]{2,1,0:T(8,128)}), f32[16,8,128]{2,1,0:T(8,128)S(1)}, u32[]{:S(2)}, u32[]{:S(2)}) async-start(f32[16,8,128]{2,1,0:T(8,128)} %get-tuple-element.66), calls=%async_computation.2 | async-start | bytes 131072 | tf_op jit(solution)/shard_map/all_to_all | solution.py:456
  174.1 14.4 %collective-permute-start.20 = (bf16[96,768]{1,0:T(8,128)(2,1)S(1)}, bf16[96,768]{1,0:T(8,128)(2,1)S(1)}, u32[]{:S(2)}, u32[]{:S(2)}) collective-permute-start(bf16[96,768]{1,0:T(8,128)(2,1)S(1)} %get-tuple-element.75), channel_id=1, source_target_pairs={{0,0},{8,128},{128,8},{136,136},{16,16},{24,144},{144,24},{152,152... | collective-permute-start | bytes 442376 | tf_op jit(solution)/shard_map/ppermute | solution.py:453
  179.2 9.3 %collective-permute-start.21 = (bf16[96,768]{1,0:T(8,128)(2,1)S(1)}, bf16[96,768]{1,0:T(8,128)(2,1)S(1)}, u32[]{:S(2)}, u32[]{:S(2)}) collective-permute-start(bf16[96,768]{1,0:T(8,128)(2,1)S(1)} %get-tuple-element.74), channel_id=1, source_target_pairs={{0,8},{8,136},{128,0},{136,128},{16,24},{24,152},{144,16},{152,144... | collective-permute-start | bytes 442376 | tf_op jit(solution)/shard_map/ppermute | solution.py:454
  181.6 13.4 %all-to-all-start.2 = ((f32[16,8,128]{2,1,0:T(8,128)}), f32[16,8,128]{2,1,0:T(8,128)S(1)}, u32[]{:S(2)}, u32[]{:S(2)}) async-start(f32[16,8,128]{2,1,0:T(8,128)} %squares.1), calls=%async_computation.3 | async-start | bytes 131072 | tf_op jit(solution)/shard_map/all_to_all | solution.py:458
  (32 other events, 180.6 us)
Sparse Core Ops, SparseCore 0:
  35.5 36.2 all-gather.2
  73.7 33.2 all-gather.4
  109.5 35.9 reduce-scatter.1

commit v5 on v4

--- a/solution.py
+++ b/solution.py
@@ -249,14 +249,19 @@
 
 
 def shard_body(numbers, arriving, leaving):
+    (image,) = numbers
     out, *terms = arriving
-    shard, square_out = leaving
-    columns = shard.ref.shape[1] // 2
+    first, second, square_out = leaving
+    rows, columns = first.ref.shape[0], first.ref.shape[1] // 2
     square = jnp.zeros((1, 1), F32)
     for total, at in ((out[...].astype(F32), columns), (total_of(*terms), 0)):
-        shard.ref[:, at : at + columns] = total.astype(BF16)
+        top, bottom = total[:rows].astype(BF16), total[rows:].astype(BF16)
+        first.ref[:, at : at + columns] = jnp.where(image == 0, top, bottom)
+        second.ref[:, at : at + columns] = jnp.where(image == 0, bottom, top)
         column_sums = jnp.sum(total * total, axis=0, keepdims=True)
         square += jnp.sum(column_sums, axis=1, keepdims=True)
+    first.send()
+    second.send()
     square_out.ref[...] = jnp.broadcast_to(square.reshape(1, 1, 1), square_out.ref.shape)
 
 
@@ -434,24 +439,24 @@
     arrived = start_scatter(*parts[:3])
     terms = end_scatter(arrived, relay(arrived, *parts[3:5]), parts[5])
     small = shape((Z * CORE, 8, 128), F32)
-    shard, square = call(
+    half = shape((count // 2, 2 * columns), BF16)
+    first, second, square = call(
         shard_body,
         "shards",
-        (),
+        (this_image,),
         (out_shard, *terms),
-        (shape((count, 2 * columns), BF16), small),
+        (half, half, small),
         vmem=LARGE,
     )
 
-    halves = shard.reshape(2, count // 2, 2 * columns)
     pairs = ([(0, 0), (1, 2), (2, 1), (3, 3)], [(0, 1), (1, 3), (2, 0), (3, 2)])
     along = [
         [((s // 2 * Z + k) * 2 + s % 2, (t // 2 * Z + k) * 2 + t % 2) for k in range(Z) for s, t in pair]
         for pair in pairs
     ]
     axes = ("yh", "z", "core")
-    near = lax.ppermute(pick(halves, image), axes, along[0])
-    far = lax.ppermute(pick(halves, 1 - image), axes, along[1])
+    near = lax.ppermute(first, axes, along[0])
+    far = lax.ppermute(second, axes, along[1])
 
     squares = lax.all_to_all(square, ("z", "core"), 0, 0, tiled=True)
     (squares,) = call(square_body, "squares", (), (squares,), (small,))

time: 204 us -> 204 us (level)
  no operation moved by 1% of the time
where the time goes in v5:
time: 204 us; the launch traced here: 203 us
  waiting for transfers between devices  65.7 us (32%)
  starting transfers between devices  62.5 us (31%)
  Pallas kernels  37.7 us (18%)
  between operations  14.2 us (7%)
  local copies, waits for them, and re-layouts  13.9 us (7%)
  matrix products  7.15 us (4%)
  other arithmetic  2.06 us (1%)
    pallas_call x13, Pallas kernels, call(): pl.pallas_call(kernel, out_shape=tuple(outputs), in_specs=[smem] * n_scal...  37.7 us
    ppermute x8, starting transfers between devices, swap(): return lax.ppermute(x, axis, [(i, i ^ mask) for i in range(size)])  20 us
    ppermute x10, starting transfers between devices, shift(): return lax.ppermute(x, axis, [(i, (i + by) % size) for i in range(size)])  18.6 us
    ppermute x2, waiting for transfers between devices, shift_by_core(): return lax.ppermute(x, ('z', 'core'), pairs)  16.4 us
    all_to_all x1, waiting for transfers between devices, local(): terms = lax.all_to_all(d_value, 'z', 0, 0, tiled=True)  13.1 us
    all_gather x2, waiting for transfers between devices, from_partner(): return lax.all_gather(pick(array, 1 - image), 'yh', axis=0)  9.96 us
    unnamed x57, local copies, waits for them, and re-layouts  9.69 us
    ppermute x10, waiting for transfers between devices, shift(): return lax.ppermute(x, axis, [(i, (i + by) % size) for i in range(size)])  9.58 us
  transfers between devices with their start and end apart: 28, of which 13 were waited for; matrix products, arithmetic and copies ran while one was open for 5% of the time, Pallas kernels for 17%

profile of v5, /device:TPU:1, one launch (start us, length us, event | category | flops | bytes accessed | tf_op | source)
XLA Modules:
  0.0 203.3 jit_solution(845753357822962174)
XLA Ops:
  12.6 3.8 %collective-permute-start = (bf16[128,768]{1,0:T(8,128)(2,1)S(1)}, bf16[128,768]{1,0:T(8,128)(2,1)S(1)}, u32[]{:S(2)}, u32[]{:S(2)}) collective-permute-start(bf16[128,768]{1,0:T(8,128)(2,1)S(1)} %get-tuple-element.75), channel_id=1, source_target_pairs={{0,128},{128,0},{1,129},{129,1},{2,130},{130,2},{3,131},{131,3},{4... | collective-permute-start | bytes 589832 | tf_op jit(solution)/shard_map/ppermute | solution.py:34
  22.5 4.0 %collective-permute-start.2 = (bf16[256,768]{1,0:T(8,128)(2,1)S(1)}, bf16[256,768]{1,0:T(8,128)(2,1)}, u32[]{:S(2)}, u32[]{:S(2)}) collective-permute-start(bf16[256,768]{1,0:T(8,128)(2,1)S(1)} %pad_maximum_fusion.1.refs_1_.refs_5_), channel_id=1, source_target_pairs={{0,112},{16,0},{32,16},{48,32},{64,48},{80,64},{96,80},{112,96},{1... | collective-permute-start | bytes 1179656 | tf_op jit(solution)/shard_map/ppermute | solution.py:22
  27.3 3.0 %collective-permute-start.3 = (bf16[128,768]{1,0:T(8,128)(2,1)S(1)}, bf16[128,768]{1,0:T(8,128)(2,1)S(1)}, u32[]{:S(2)}, u32[]{:S(2)}) collective-permute-start(bf16[128,768]{1,0:T(8,128)(2,1)S(1)} %get-tuple-element.73), channel_id=1, source_target_pairs={{0,128},{128,0},{1,129},{129,1},{2,130},{130,2},{3,131},{131,3},{4... | collective-permute-start | bytes 589832 | tf_op jit(solution)/shard_map/ppermute | solution.py:34
  30.3 3.1 %collective-permute-done.3 = bf16[128,768]{1,0:T(8,128)(2,1)S(1)} collective-permute-done((bf16[128,768]{1,0:T(8,128)(2,1)S(1)}, bf16[128,768]{1,0:T(8,128)(2,1)S(1)}, u32[]{:S(2)}, u32[]{:S(2)}) %collective-permute-start.3) | collective-permute-done | bytes 196640 | tf_op jit(solution)/shard_map/ppermute | solution.py:34
  38.2 3.4 %collective-permute-start.4 = (bf16[256,768]{1,0:T(8,128)(2,1)}, bf16[256,768]{1,0:T(8,128)(2,1)}, u32[]{:S(2)}, u32[]{:S(2)}) collective-permute-start(bf16[256,768]{1,0:T(8,128)(2,1)} %pad_maximum_fusion.3), channel_id=1, source_target_pairs={{0,8},{8,0},{1,9},{9,1},{2,10},{10,2},{3,11},{11,3},{4,12},{12,4},... | collective-permute-start | bytes 1179656 | tf_op jit(solution)/shard_map/ppermute | solution.py:34
  57.1 3.8 %stats.4.refs_2_ = f32[8,512]{1,0:T(8,128)S(1)} custom-call(bf16[512,768]{1,0:T(8,128)(2,1)S(1)} %constant_dynamic-update-slice_fusion.refs_0_.refs_1_.refs_2_, bf16[256,768]{1,0:T(8,128)(2,1)} %collective-permute-done.5.refs_1_.refs_8_, bf16[256,768]{1,0:T(8,128)(2,1)} %collective-permute-done.7.refs_2_.refs_9_, ...), custom_call_target="tpu_custom_call" | custom-call | flops 1000 | tf_op jit(solution)/shard_map/stats/pallas_call | solution.py:106
  60.9 2.8 %collective-permute-done.9.refs_1_.refs_12_ = bf16[256,768]{1,0:T(8,128)(2,1)S(1)} collective-permute-done((bf16[256,768]{1,0:T(8,128)(2,1)S(1)}, bf16[256,768]{1,0:T(8,128)(2,1)S(1)}, u32[]{:S(2)}, u32[]{:S(2)}) %collective-permute-start.9) | collective-permute-done | bytes 393248 | tf_op jit(solution)/shard_map/ppermute | solution.py:30
  64.4 5.2 %collective-permute-start.10 = (f32[8,512]{1,0:T(8,128)S(1)}, f32[8,512]{1,0:T(8,128)S(1)}, u32[]{:S(2)}, u32[]{:S(2)}) collective-permute-start(f32[8,512]{1,0:T(8,128)S(1)} %stats.5.refs_3_), channel_id=1, source_target_pairs={{0,8},{8,0},{1,9},{9,1},{2,10},{10,2},{3,11},{11,3},{4,12},{12,4},... | collective-permute-start | bytes 49160 | tf_op jit(solution)/shard_map/ppermute | solution.py:34
  71.1 9.1 %d_value.1 = (bf16[8,256,384]{2,1,0:T(8,128)(2,1)}, bf16[2,384,256]{2,1,0:T(8,128)(2,1)}) custom-call(s32[1]{0:T(128)} %bitcast.2.refs_0_, bf16[512,768]{1,0:T(8,128)(2,1)} %copy-done.1, bf16[512,768]{1,0:T(8,128)(2,1)} %copy-done.1, f32[8,512]{1,0:T(8,128)} %copy-done.11, f32[8,512]{1,0:T(8,128)} %copy-done.25, bf16[256,768]{1,0:T(8,128)(2,1)} %copy-done.3, ...), custom_call_target="tpu_custom_call" | custom-call | flops 1000 | tf_op jit(solution)/shard_map/d_value/pallas_call | solution.py:106
  80.2 5.2 %all-to-all-start = ((bf16[8,256,384]{2,1,0:T(8,128)(2,1)}), bf16[8,256,384]{2,1,0:T(8,128)(2,1)}, u32[]{:S(2)}, u32[]{:S(2)}) async-start(bf16[8,256,384]{2,1,0:T(8,128)(2,1)} %get-tuple-element.58), calls=%async_computation.1 | async-start | bytes 3145728 | tf_op jit(solution)/shard_map/all_to_all | solution.py:397
  85.7 3.0 %turn.2 = (bf16[1536,256]{1,0:T(8,128)(2,1)}, bf16[1536,256]{1,0:T(8,128)(2,1)}) custom-call(s32[1]{0:T(128)} %bitcast.refs_0_, s32[1]{0:T(128)} %bitcast.1.refs_1_.refs_0_, bf16[2,128,3072]{2,1,0:T(8,128)(2,1)} %refs_2_, bf16[2,128,3072]{2,1,0:T(8,128)(2,1)} %all-gather.3.cloned.1.call-done.refs_3_), custom_call_target="tpu_custom_call" | custom-call | flops 1000 | tf_op jit(solution)/shard_map/turn/pallas_call | solution.py:106
  93.0 4.0 %per_out.1 = bf16[1536,384]{1,0:T(8,128)(2,1)} custom-call(bf16[1536,256]{1,0:T(8,128)(2,1)} %get-tuple-element.49.refs_0_, bf16[1536,256]{1,0:T(8,128)(2,1)} %copy-done.17, bf16[2,384,256]{2,1,0:T(8,128)(2,1)} %get-tuple-element.51.refs_2_, bf16[2,384,256]{2,1,0:T(8,128)(2,1)} %copy-done.20), custom_call_target="tpu_custom_call" | custom-call | flops 1000 | tf_op jit(solution)/shard_map/per_out/pallas_call | solution.py:106
  97.0 9.9 %all-gather.5.cloned.1.call-done.refs_3_ = bf16[2,128,3072]{2,1,0:T(8,128)(2,1)} async-done(((bf16[1,128,3072]{2,1,0:T(8,128)(2,1)}), bf16[2,128,3072]{2,1,0:T(8,128)(2,1)}) %all-gather.5.cloned.1.call-update) | async-done | bytes 1572880 | tf_op jit(solution)/shard_map/all_gather | solution.py:318
  107.0 3.0 %turn.3 = (bf16[1536,256]{1,0:T(8,128)(2,1)}, bf16[1536,256]{1,0:T(8,128)(2,1)}) custom-call(s32[1]{0:T(128)} %bitcast.refs_0_, s32[1]{0:T(128)} %bitcast.1.refs_1_.refs_0_, bf16[2,128,3072]{2,1,0:T(8,128)(2,1)} %refs_2_.1, bf16[2,128,3072]{2,1,0:T(8,128)(2,1)} %all-gather.5.cloned.1.call-done.refs_3_), custom_call_target="tpu_custom_call" | custom-call | flops 1000 | tf_op jit(solution)/shard_map/turn/pallas_call | solution.py:106
  110.7 13.1 %all-to-all-done.refs_0_ = bf16[8,256,384]{2,1,0:T(8,128)(2,1)} async-done(((bf16[8,256,384]{2,1,0:T(8,128)(2,1)}), bf16[8,256,384]{2,1,0:T(8,128)(2,1)}, u32[]{:S(2)}, u32[]{:S(2)}) %all-to-all-start) | async-done | bytes 1572896 | tf_op jit(solution)/shard_map/all_to_all | solution.py:397
  125.7 2.9 %collective-permute-start.14 = (bf16[256,384]{1,0:T(8,128)(2,1)S(1)}, bf16[256,384]{1,0:T(8,128)(2,1)S(1)}, u32[]{:S(2)}, u32[]{:S(2)}) collective-permute-start(bf16[256,384]{1,0:T(8,128)(2,1)S(1)} %d_value_sum.1.refs_3_), channel_id=1, source_target_pairs={{0,8},{8,0},{1,9},{9,1},{2,10},{10,2},{3,11},{11,3},{4,12},{12,4},... | collective-permute-start | bytes 589832 | tf_op jit(solution)/shard_map/ppermute | solution.py:34
  130.3 3.2 %per_value.1 = (bf16[2,192,384]{2,1,0:T(8,128)(2,1)}, bf16[2,192,384]{2,1,0:T(8,128)(2,1)}, bf16[1,192,384]{2,1,0:T(8,128)(2,1)}, bf16[1,192,384]{2,1,0:T(8,128)...) custom-call(s32[1]{0:T(128)} %bitcast.2.refs_0_, bf16[1536,256]{1,0:T(8,128)(2,1)} %get-tuple-element.56.refs_1_, ...), custom_call_target="tpu_custom_call" | custom-call | flops 1000 | tf_op jit(solution)/shard_map/per_value/pallas_call | solution.py:106
  136.2 13.7 %collective-permute-done.17.refs_3_ = bf16[1,192,384]{2,1,0:T(8,128)(2,1)S(1)} collective-permute-done((bf16[1,192,384]{2,1,0:T(8,128)(2,1)}, bf16[1,192,384]{2,1,0:T(8,128)(2,1)S(1)}, u32[]{:S(2)}, u32[]{:S(2)}) %collective-permute-start.17) | collective-permute-done | bytes 147488 | tf_op jit(solution)/shard_map/ppermute | solution.py:30
  152.9 3.9 %collective-permute-start.19 = (bf16[1,192,384]{2,1,0:T(8,128)(2,1)}, bf16[1,192,384]{2,1,0:T(8,128)(2,1)S(1)}, u32[]{:S(2)}, u32[]{:S(2)}) collective-permute-start(bf16[1,192,384]{2,1,0:T(8,128)(2,1)} %get-tuple-element.66), channel_id=1, source_target_pairs={{0,96},{16,112},{32,0},{48,16},{64,32},{80,48},{96,64},{112,80},{1... | collective-permute-start | bytes 442376 | tf_op jit(solution)/shard_map/ppermute | solution.py:22
  156.8 7.6 %collective-permute-done.18.refs_5_ = bf16[1,192,384]{2,1,0:T(8,128)(2,1)S(1)} collective-permute-done((bf16[1,192,384]{2,1,0:T(8,128)(2,1)}, bf16[1,192,384]{2,1,0:T(8,128)(2,1)S(1)}, u32[]{:S(2)}, u32[]{:S(2)}) %collective-permute-start.18) | collective-permute-done | bytes 147488 | tf_op jit(solution)/shard_map/ppermute | solution.py:22
  167.3 5.7 %all-to-all-start.1 = ((f32[16,8,128]{2,1,0:T(8,128)}), f32[16,8,128]{2,1,0:T(8,128)S(1)}, u32[]{:S(2)}, u32[]{:S(2)}) async-start(f32[16,8,128]{2,1,0:T(8,128)} %get-tuple-element.67), calls=%async_computation.2 | async-start | bytes 131072 | tf_op jit(solution)/shard_map/all_to_all | solution.py:461
  173.0 5.0 %collective-permute-start.20 = (bf16[96,768]{1,0:T(8,128)(2,1)}, bf16[96,768]{1,0:T(8,128)(2,1)S(1)}, u32[]{:S(2)}, u32[]{:S(2)}) collective-permute-start(bf16[96,768]{1,0:T(8,128)(2,1)} %get-tuple-element.68), channel_id=1, source_target_pairs={{0,0},{8,128},{128,8},{136,136},{16,16},{24,144},{144,24},{152,152... | collective-permute-start | bytes 442376 | tf_op jit(solution)/shard_map/ppermute | solution.py:458
  181.5 7.1 %all-to-all-start.2 = ((f32[16,8,128]{2,1,0:T(8,128)}), f32[16,8,128]{2,1,0:T(8,128)S(1)}, u32[]{:S(2)}, u32[]{:S(2)}) async-start(f32[16,8,128]{2,1,0:T(8,128)} %squares.1), calls=%async_computation.3 | async-start | bytes 131072 | tf_op jit(solution)/shard_map/all_to_all | solution.py:463
  188.6 6.5 %all-to-all-done.2.refs_1_ = f32[16,8,128]{2,1,0:T(8,128)S(1)} async-done(((f32[16,8,128]{2,1,0:T(8,128)}), f32[16,8,128]{2,1,0:T(8,128)S(1)}, u32[]{:S(2)}, u32[]{:S(2)}) %all-to-all-start.2) | async-done | bytes 65568 | tf_op jit(solution)/shard_map/all_to_all | solution.py:463
  (119 shorter events, 57.2 us)
Async XLA Ops:
  7.2 78.5 %all-gather.3.cloned.1.call-start = ((), (), s32[]{:S(2)}) async-start(), calls=%async_computation.4 | async-start | bytes 2359296 | tf_op jit(solution)/shard_map/all_gather | solution.py:318
  12.6 7.5 %collective-permute-start = (bf16[128,768]{1,0:T(8,128)(2,1)S(1)}, bf16[128,768]{1,0:T(8,128)(2,1)S(1)}, u32[]{:S(2)}, u32[]{:S(2)}) collective-permute-start(bf16[128,768]{1,0:T(8,128)(2,1)S(1)} %get-tuple-element.75), channel_id=1, source_target_pairs={{0,128},{128,0},{1,129},{129,1},{2,130},{130,2},{3,131},{131,3},{4... | collective-permute-start | bytes 589832 | tf_op jit(solution)/shard_map/ppermute | solution.py:34
  20.1 14.2 %collective-permute-start.1 = (bf16[256,768]{1,0:T(8,128)(2,1)S(1)}, bf16[256,768]{1,0:T(8,128)(2,1)S(1)}, u32[]{:S(2)}, u32[]{:S(2)}) collective-permute-start(bf16[256,768]{1,0:T(8,128)(2,1)S(1)} %pad_maximum_fusion.1.refs_1_.refs_5_), channel_id=1, source_target_pairs={{0,16},{16,32},{32,48},{48,64},{64,80},{80,96},{96,112},{112,0},{1... | collective-permute-start | bytes 1179656 | tf_op jit(solution)/shard_map/ppermute | solution.py:22
  22.5 11.8 %collective-permute-start.2 = (bf16[256,768]{1,0:T(8,128)(2,1)S(1)}, bf16[256,768]{1,0:T(8,128)(2,1)}, u32[]{:S(2)}, u32[]{:S(2)}) collective-permute-start(bf16[256,768]{1,0:T(8,128)(2,1)S(1)} %pad_maximum_fusion.1.refs_1_.refs_5_), channel_id=1, source_target_pairs={{0,112},{16,0},{32,16},{48,32},{64,48},{80,64},{96,80},{112,96},{1... | collective-permute-start | bytes 1179656 | tf_op jit(solution)/shard_map/ppermute | solution.py:22
  27.3 6.1 %collective-permute-start.3 = (bf16[128,768]{1,0:T(8,128)(2,1)S(1)}, bf16[128,768]{1,0:T(8,128)(2,1)S(1)}, u32[]{:S(2)}, u32[]{:S(2)}) collective-permute-start(bf16[128,768]{1,0:T(8,128)(2,1)S(1)} %get-tuple-element.73), channel_id=1, source_target_pairs={{0,128},{128,0},{1,129},{129,1},{2,130},{130,2},{3,131},{131,3},{4... | collective-permute-start | bytes 589832 | tf_op jit(solution)/shard_map/ppermute | solution.py:34
  35.4 71.5 %all-gather.5.cloned.1.call-start = ((), (), s32[]{:S(2)}) async-start(), calls=%async_computation.5 | async-start | bytes 2359296 | tf_op jit(solution)/shard_map/all_gather | solution.py:318
  35.5 9.1 %collective-permute-start.5 = (bf16[256,768]{1,0:T(8,128)(2,1)S(1)}, bf16[256,768]{1,0:T(8,128)(2,1)}, u32[]{:S(2)}, u32[]{:S(2)}) collective-permute-start(bf16[256,768]{1,0:T(8,128)(2,1)S(1)} %collective-permute-done.1.refs_2_.refs_6_), channel_id=1, source_target_pairs={{0,16},{16,32},{32,48},{48,64},{64,80},{80,96},{96,112},{112,0},{1... | collective-permute-start | bytes 1179656 | tf_op jit(solution)/shard_map/ppermute | solution.py:22
  35.5 9.0 %collective-permute-start.7 = (bf16[256,768]{1,0:T(8,128)(2,1)}, bf16[256,768]{1,0:T(8,128)(2,1)}, u32[]{:S(2)}, u32[]{:S(2)}) collective-permute-start(bf16[256,768]{1,0:T(8,128)(2,1)} %collective-permute-done.2.refs_3_.refs_7_), channel_id=1, source_target_pairs={{0,112},{16,0},{32,16},{48,32},{64,48},{80,64},{96,80},{112,96},{1... | collective-permute-start | bytes 1179656 | tf_op jit(solution)/shard_map/ppermute | solution.py:22
  38.2 11.1 %collective-permute-start.4 = (bf16[256,768]{1,0:T(8,128)(2,1)}, bf16[256,768]{1,0:T(8,128)(2,1)}, u32[]{:S(2)}, u32[]{:S(2)}) collective-permute-start(bf16[256,768]{1,0:T(8,128)(2,1)} %pad_maximum_fusion.3), channel_id=1, source_target_pairs={{0,8},{8,0},{1,9},{9,1},{2,10},{10,2},{3,11},{11,3},{4,12},{12,4},... | collective-permute-start | bytes 1179656 | tf_op jit(solution)/shard_map/ppermute | solution.py:34
  44.6 10.7 %collective-permute-start.6 = (bf16[256,768]{1,0:T(8,128)(2,1)}, bf16[256,768]{1,0:T(8,128)(2,1)S(1)}, u32[]{:S(2)}, u32[]{:S(2)}) collective-permute-start(bf16[256,768]{1,0:T(8,128)(2,1)} %collective-permute-done.5.refs_1_.refs_8_), channel_id=1, source_target_pairs={{0,16},{16,32},{32,48},{48,64},{64,80},{80,96},{96,112},{112,0},{1... | collective-permute-start | bytes 1179656 | tf_op jit(solution)/shard_map/ppermute | solution.py:22
  44.6 10.8 %collective-permute-start.8 = (bf16[256,768]{1,0:T(8,128)(2,1)}, bf16[256,768]{1,0:T(8,128)(2,1)}, u32[]{:S(2)}, u32[]{:S(2)}) collective-permute-start(bf16[256,768]{1,0:T(8,128)(2,1)} %collective-permute-done.7.refs_2_.refs_9_), channel_id=1, source_target_pairs={{0,112},{16,0},{32,16},{48,32},{64,48},{80,64},{96,80},{112,96},{1... | collective-permute-start | bytes 1179656 | tf_op jit(solution)/shard_map/ppermute | solution.py:22
  56.5 7.1 %collective-permute-start.9 = (bf16[256,768]{1,0:T(8,128)(2,1)S(1)}, bf16[256,768]{1,0:T(8,128)(2,1)S(1)}, u32[]{:S(2)}, u32[]{:S(2)}) collective-permute-start(bf16[256,768]{1,0:T(8,128)(2,1)S(1)} %broadcast_select_fusion), channel_id=1, source_target_pairs={{0,16},{8,120},{16,32},{24,8},{32,48},{40,24},{48,64},{56,40},{64,... | collective-permute-start | bytes 1179656 | tf_op jit(solution)/shard_map/ppermute | solution.py:30
  80.2 43.6 %all-to-all-start = ((bf16[8,256,384]{2,1,0:T(8,128)(2,1)}), bf16[8,256,384]{2,1,0:T(8,128)(2,1)}, u32[]{:S(2)}, u32[]{:S(2)}) async-start(bf16[8,256,384]{2,1,0:T(8,128)(2,1)} %get-tuple-element.58), calls=%async_computation.1 | async-start | bytes 3145728 | tf_op jit(solution)/shard_map/all_to_all | solution.py:397
  85.4 79.0 %reduce-scatter.2.cloned.1.call-start = ((), (), s32[]{:S(2)}) async-start(), calls=%async_computation.6 | async-start | bytes 1327104 | tf_op jit(solution)/shard_map/reduce_scatter | solution.py:426
  109.9 18.6 %collective-permute-start.13 = (bf16[1536,256]{1,0:T(8,128)(2,1)}, bf16[1536,256]{1,0:T(8,128)(2,1)S(1)}, u32[]{:S(2)}, u32[]{:S(2)}) collective-permute-start(bf16[1536,256]{1,0:T(8,128)(2,1)} %get-tuple-element.57), channel_id=1, source_target_pairs={{0,8},{8,0},{1,9},{9,1},{2,10},{10,2},{3,11},{11,3},{4,12},{12,4},... | collective-permute-start | bytes 2359304 | tf_op jit(solution)/shard_map/ppermute | solution.py:34
  133.5 16.5 %collective-permute-start.15 = (bf16[2,192,384]{2,1,0:T(8,128)(2,1)}, bf16[2,192,384]{2,1,0:T(8,128)(2,1)S(1)}, u32[]{:S(2)}, u32[]{:S(2)}) collective-permute-start(bf16[2,192,384]{2,1,0:T(8,128)(2,1)} %get-tuple-element.60), channel_id=1, source_target_pairs={{0,16},{16,32},{32,48},{48,64},{64,80},{80,96},{96,112},{112,0},{1... | collective-permute-start | bytes 884744 | tf_op jit(solution)/shard_map/ppermute | solution.py:22
  133.8 16.1 %collective-permute-start.16 = (bf16[2,192,384]{2,1,0:T(8,128)(2,1)}, bf16[2,192,384]{2,1,0:T(8,128)(2,1)S(1)}, u32[]{:S(2)}, u32[]{:S(2)}) collective-permute-start(bf16[2,192,384]{2,1,0:T(8,128)(2,1)} %get-tuple-element.61), channel_id=1, source_target_pairs={{0,112},{16,0},{32,16},{48,32},{64,48},{80,64},{96,80},{112,96},{1... | collective-permute-start | bytes 884744 | tf_op jit(solution)/shard_map/ppermute | solution.py:22
  136.2 13.7 %collective-permute-start.17 = (bf16[1,192,384]{2,1,0:T(8,128)(2,1)}, bf16[1,192,384]{2,1,0:T(8,128)(2,1)S(1)}, u32[]{:S(2)}, u32[]{:S(2)}) collective-permute-start(bf16[1,192,384]{2,1,0:T(8,128)(2,1)} %get-tuple-element.62), channel_id=1, source_target_pairs={{0,32},{8,104},{16,48},{24,120},{32,64},{40,8},{48,80},{56,24},{64... | collective-permute-start | bytes 442376 | tf_op jit(solution)/shard_map/ppermute | solution.py:30
  152.8 11.6 %collective-permute-start.18 = (bf16[1,192,384]{2,1,0:T(8,128)(2,1)}, bf16[1,192,384]{2,1,0:T(8,128)(2,1)S(1)}, u32[]{:S(2)}, u32[]{:S(2)}) collective-permute-start(bf16[1,192,384]{2,1,0:T(8,128)(2,1)} %get-tuple-element.65), channel_id=1, source_target_pairs={{0,32},{16,48},{32,64},{48,80},{64,96},{80,112},{96,0},{112,16},{1... | collective-permute-start | bytes 442376 | tf_op jit(solution)/shard_map/ppermute | solution.py:22
  152.9 11.5 %collective-permute-start.19 = (bf16[1,192,384]{2,1,0:T(8,128)(2,1)}, bf16[1,192,384]{2,1,0:T(8,128)(2,1)S(1)}, u32[]{:S(2)}, u32[]{:S(2)}) collective-permute-start(bf16[1,192,384]{2,1,0:T(8,128)(2,1)} %get-tuple-element.66), channel_id=1, source_target_pairs={{0,96},{16,112},{32,0},{48,16},{64,32},{80,48},{96,64},{112,80},{1... | collective-permute-start | bytes 442376 | tf_op jit(solution)/shard_map/ppermute | solution.py:22
  167.3 13.5 %all-to-all-start.1 = ((f32[16,8,128]{2,1,0:T(8,128)}), f32[16,8,128]{2,1,0:T(8,128)S(1)}, u32[]{:S(2)}, u32[]{:S(2)}) async-start(f32[16,8,128]{2,1,0:T(8,128)} %get-tuple-element.67), calls=%async_computation.2 | async-start | bytes 131072 | tf_op jit(solution)/shard_map/all_to_all | solution.py:461
  173.0 15.6 %collective-permute-start.20 = (bf16[96,768]{1,0:T(8,128)(2,1)}, bf16[96,768]{1,0:T(8,128)(2,1)S(1)}, u32[]{:S(2)}, u32[]{:S(2)}) collective-permute-start(bf16[96,768]{1,0:T(8,128)(2,1)} %get-tuple-element.68), channel_id=1, source_target_pairs={{0,0},{8,128},{128,8},{136,136},{16,16},{24,144},{144,24},{152,152... | collective-permute-start | bytes 442376 | tf_op jit(solution)/shard_map/ppermute | solution.py:458
  178.0 10.6 %collective-permute-start.21 = (bf16[96,768]{1,0:T(8,128)(2,1)}, bf16[96,768]{1,0:T(8,128)(2,1)S(1)}, u32[]{:S(2)}, u32[]{:S(2)}) collective-permute-start(bf16[96,768]{1,0:T(8,128)(2,1)} %get-tuple-element.69), channel_id=1, source_target_pairs={{0,8},{8,136},{128,0},{136,128},{16,24},{24,152},{144,16},{152,144... | collective-permute-start | bytes 442376 | tf_op jit(solution)/shard_map/ppermute | solution.py:459
  181.5 13.6 %all-to-all-start.2 = ((f32[16,8,128]{2,1,0:T(8,128)}), f32[16,8,128]{2,1,0:T(8,128)S(1)}, u32[]{:S(2)}, u32[]{:S(2)}) async-start(f32[16,8,128]{2,1,0:T(8,128)} %squares.1), calls=%async_computation.3 | async-start | bytes 131072 | tf_op jit(solution)/shard_map/all_to_all | solution.py:463
  (32 other events, 215.5 us)
Sparse Core Ops, SparseCore 0:
  35.5 36.2 all-gather.2
  73.7 33.2 all-gather.4
  109.5 35.9 reduce-scatter.1

commit v6 on v4

--- a/solution.py
+++ b/solution.py
@@ -344,12 +344,11 @@
         backward = shift(backward, "z", Z, -1)
         pieces += [forward, backward]
         if step == 1:
-            forward, backward, queries_d, late_tokens, late_cotangent = lax.optimization_barrier(
-                (forward, backward, queries_d, tokens, cotangent)
+            forward, backward, queries_d, late_cotangent = lax.optimization_barrier(
+                (forward, backward, queries_d, cotangent)
             )
             queries_d = jnp.concatenate([queries_d, swap(queries_d, "core", CORE)], axis=0)
             cotangent_pair = cotangent, from_partner(late_cotangent)
-            tokens_pair = tokens, from_partner(late_tokens)
         if step == 3:
             stats = stats_of(pieces[:3])
             forward, backward, stats = lax.optimization_barrier((forward, backward, stats))
@@ -388,7 +387,10 @@
         {0: left_part(queries_d), 1: right_part(queries_d)},
         LARGE,
     )
-    attended, cotangent_pair = lax.optimization_barrier((attended, cotangent_pair))
+    attended, cotangent_pair, late_tokens = lax.optimization_barrier(
+        (attended, cotangent_pair, tokens)
+    )
+    tokens_pair = tokens, swap(pick(late_tokens, 1 - image), "yh", YH)[None]
     terms = lax.all_to_all(d_value, "z", 0, 0, tiled=True)
     attended_other = swap(attended, "core", CORE)
 
@@ -402,7 +404,7 @@
             (turned, turned),
             {
                 0: ((rows, width), lambda core, image: image),
-                1: ((rows, width), lambda core, image: 1 - image),
+                1: ((rows, width), lambda core, image: (pair[1].shape[0] - 1) * (1 - image)),
             },
             LARGE,
         )
@@ -417,7 +419,6 @@
         (shape((width // 2, columns), BF16),),
         vmem=LARGE,
     )
-    per_out, tokens_pair = lax.optimization_barrier((per_out, tokens_pair))
     out_shard = lax.psum_scatter(per_out, "z", scatter_dimension=0, tiled=True)
     tokens_half = half_width(tokens_pair)
 

time: 204 us -> 203 us (level)
  waiting for transfers between devices: 64.6 us -> 58.1 us
  starting transfers between devices: 62.5 us -> 67.3 us
    ppermute x8 -> x9, waiting for transfers between devices: 7.39 us -> 25 us  [swap(): return lax.ppermute(x, axis, [(i, i ^ mask) for i in range(size)])]
    all_gather x2 -> x1, waiting for transfers between devices: 9.96 us -> 0.02 us  [from_partner(): return lax.all_gather(pick(array, 1 - image), 'yh', axis=0)]
    all_to_all x1, waiting for transfers between devices: 13.1 us -> 4.99 us  [local(): terms = lax.all_to_all(d_value, 'z', 0, 0, tiled=True)]
    ppermute x2, waiting for transfers between devices: 16.5 us -> 13.5 us  [shift_by_core(): return lax.ppermute(x, ('z', 'core'), pairs)]
    all_to_all x1, starting transfers between devices: 5.67 us -> 8.32 us  [local(): squares = lax.all_to_all(square, ('z', 'core'), 0, 0, tiled=True)]
    ppermute x10, waiting for transfers between devices: 9.58 us -> 6.96 us  [shift(): return lax.ppermute(x, axis, [(i, (i + by) % size) for i in range(size)])]
    ppermute x8 -> x9, starting transfers between devices: 20 us -> 22.4 us  [swap(): return lax.ppermute(x, axis, [(i, i ^ mask) for i in range(size)])]
    dynamic_slice x2 -> x1, local copies, waits for them, and re-layouts: 3.15 us -> 0.95 us  [pick(): return lax.dynamic_index_in_dim(array, index, 0, keepdims=False)]
  transfers between devices with their start and end apart: 28 -> 28, of which waited for: 13 -> 13; matrix products, arithmetic and copies ran while one was open for 5% -> 6% of each run, Pallas kernels for 17% -> 16%
where the time goes in v6:
time: 203 us; the launch traced here: 202 us
  starting transfers between devices  67.3 us (33%)
  waiting for transfers between devices  58.1 us (29%)
  Pallas kernels  37.1 us (18%)
  local copies, waits for them, and re-layouts  15.8 us (8%)
  between operations  14.5 us (7%)
  matrix products  7.63 us (4%)
  other arithmetic  2.07 us (1%)
    pallas_call x13, Pallas kernels, call(): pl.pallas_call(kernel, out_shape=tuple(outputs), in_specs=[smem] * n_scal...  37.1 us
    ppermute x9, waiting for transfers between devices, swap(): return lax.ppermute(x, axis, [(i, i ^ mask) for i in range(size)])  25 us
    ppermute x9, starting transfers between devices, swap(): return lax.ppermute(x, axis, [(i, i ^ mask) for i in range(size)])  22.4 us
    ppermute x10, starting transfers between devices, shift(): return lax.ppermute(x, axis, [(i, (i + by) % size) for i in range(size)])  17.7 us
    ppermute x2, waiting for transfers between devices, shift_by_core(): return lax.ppermute(x, ('z', 'core'), pairs)  13.5 us
    unnamed x61, local copies, waits for them, and re-layouts  11.5 us
    all_to_all x1, starting transfers between devices, local(): squares = lax.all_to_all(square, ('z', 'core'), 0, 0, tiled=True)  8.32 us
    all_to_all x1, starting transfers between devices, local(): squares = lax.all_to_all(squares, ('yh', 'yl', 'x'), 0, 0, tiled=True)  7.21 us
  transfers between devices with their start and end apart: 28, of which 13 were waited for; matrix products, arithmetic and copies ran while one was open for 6% of the time, Pallas kernels for 16%

profile of v6, /device:TPU:1, one launch (start us, length us, event | category | flops | bytes accessed | tf_op | source)
XLA Modules:
  0.0 202.4 jit_solution(7380275755830527852)
XLA Ops:
  12.5 3.8 %collective-permute-start = (bf16[128,768]{1,0:T(8,128)(2,1)S(1)}, bf16[128,768]{1,0:T(8,128)(2,1)S(1)}, u32[]{:S(2)}, u32[]{:S(2)}) collective-permute-start(bf16[128,768]{1,0:T(8,128)(2,1)S(1)} %get-tuple-element.67), channel_id=1, source_target_pairs={{0,128},{128,0},{1,129},{129,1},{2,130},{130,2},{3,131},{131,3},{4... | collective-permute-start | bytes 589832 | tf_op jit(solution)/shard_map/ppermute | solution.py:34
  16.4 3.1 %convolution_convert_fusion.1 = bf16[256,384]{1,0:T(8,128)(2,1)S(1)} fusion(bf16[256,3072]{1,0:T(8,128)(2,1)} %bitcast.36, bf16[3072,384]{1,0:T(8,128)(2,1)} %param.9), kind=kOutput, calls=%fused_computation.1 | convolution fusion | flops 604078080 | bytes 4128768 | tf_op jit(solution)/shard_map/dot_general | solution.py:302
  22.5 4.0 %collective-permute-start.2 = (bf16[256,768]{1,0:T(8,128)(2,1)S(1)}, bf16[256,768]{1,0:T(8,128)(2,1)S(1)}, u32[]{:S(2)}, u32[]{:S(2)}) collective-permute-start(bf16[256,768]{1,0:T(8,128)(2,1)S(1)} %pad_maximum_fusion.1.refs_1_.refs_5_), channel_id=1, source_target_pairs={{0,112},{16,0},{32,16},{48,32},{64,48},{80,64},{96,80},{112,96},{1... | collective-permute-start | bytes 1179656 | tf_op jit(solution)/shard_map/ppermute | solution.py:22
  27.3 3.0 %collective-permute-start.3 = (bf16[128,768]{1,0:T(8,128)(2,1)S(1)}, bf16[128,768]{1,0:T(8,128)(2,1)S(1)}, u32[]{:S(2)}, u32[]{:S(2)}) collective-permute-start(bf16[128,768]{1,0:T(8,128)(2,1)S(1)} %get-tuple-element.65), channel_id=1, source_target_pairs={{0,128},{128,0},{1,129},{129,1},{2,130},{130,2},{3,131},{131,3},{4... | collective-permute-start | bytes 589832 | tf_op jit(solution)/shard_map/ppermute | solution.py:34
  30.3 3.1 %collective-permute-done.3 = bf16[128,768]{1,0:T(8,128)(2,1)S(1)} collective-permute-done((bf16[128,768]{1,0:T(8,128)(2,1)S(1)}, bf16[128,768]{1,0:T(8,128)(2,1)S(1)}, u32[]{:S(2)}, u32[]{:S(2)}) %collective-permute-start.3) | collective-permute-done | bytes 196640 | tf_op jit(solution)/shard_map/ppermute | solution.py:34
  38.0 3.5 %collective-permute-start.4 = (bf16[256,768]{1,0:T(8,128)(2,1)}, bf16[256,768]{1,0:T(8,128)(2,1)}, u32[]{:S(2)}, u32[]{:S(2)}) collective-permute-start(bf16[256,768]{1,0:T(8,128)(2,1)} %pad_maximum_fusion.3), channel_id=1, source_target_pairs={{0,8},{8,0},{1,9},{9,1},{2,10},{10,2},{3,11},{11,3},{4,12},{12,4},... | collective-permute-start | bytes 1179656 | tf_op jit(solution)/shard_map/ppermute | solution.py:34
  55.4 3.8 %stats.4.refs_2_ = f32[8,512]{1,0:T(8,128)S(1)} custom-call(bf16[512,768]{1,0:T(8,128)(2,1)S(1)} %constant_dynamic-update-slice_fusion.refs_0_.refs_1_.refs_2_, bf16[256,768]{1,0:T(8,128)(2,1)} %collective-permute-done.5.refs_1_.refs_8_, bf16[256,768]{1,0:T(8,128)(2,1)} %collective-permute-done.7.refs_2_.refs_9_, ...), custom_call_target="tpu_custom_call" | custom-call | flops 1000 | tf_op jit(solution)/shard_map/stats/pallas_call | solution.py:106
  62.7 5.3 %collective-permute-start.10 = (f32[8,512]{1,0:T(8,128)S(1)}, f32[8,512]{1,0:T(8,128)S(1)}, u32[]{:S(2)}, u32[]{:S(2)}) collective-permute-start(f32[8,512]{1,0:T(8,128)S(1)} %stats.5.refs_3_), channel_id=1, source_target_pairs={{0,8},{8,0},{1,9},{9,1},{2,10},{10,2},{3,11},{11,3},{4,12},{12,4},... | collective-permute-start | bytes 49160 | tf_op jit(solution)/shard_map/ppermute | solution.py:34
  69.5 9.1 %d_value.1 = (bf16[8,256,384]{2,1,0:T(8,128)(2,1)}, bf16[2,384,256]{2,1,0:T(8,128)(2,1)}) custom-call(s32[1]{0:T(128)} %bitcast.2.refs_0_, bf16[512,768]{1,0:T(8,128)(2,1)} %copy-done.1, bf16[512,768]{1,0:T(8,128)(2,1)} %copy-done.1, f32[8,512]{1,0:T(8,128)} %copy-done.13, f32[8,512]{1,0:T(8,128)} %copy-done.27, bf16[256,768]{1,0:T(8,128)(2,1)} %copy-done.3, ...), custom_call_target="tpu_custom_call" | custom-call | flops 1000 | tf_op jit(solution)/shard_map/d_value/pallas_call | solution.py:106
  78.6 5.1 %all-to-all-start = ((bf16[8,256,384]{2,1,0:T(8,128)(2,1)}), bf16[8,256,384]{2,1,0:T(8,128)(2,1)}, u32[]{:S(2)}, u32[]{:S(2)}) async-start(bf16[8,256,384]{2,1,0:T(8,128)(2,1)} %get-tuple-element.51), calls=%async_computation.1 | async-start | bytes 3145728 | tf_op jit(solution)/shard_map/all_to_all | solution.py:394
  84.0 2.9 %turn.2 = (bf16[1536,256]{1,0:T(8,128)(2,1)}, bf16[1536,256]{1,0:T(8,128)(2,1)}) custom-call(s32[1]{0:T(128)} %bitcast.refs_0_, s32[1]{0:T(128)} %bitcast.1.refs_1_, bf16[2,128,3072]{2,1,0:T(8,128)(2,1)} %refs_2_.1, bf16[2,128,3072]{2,1,0:T(8,128)(2,1)} %all-gather.2.cloned.1.call-done.refs_3_), custom_call_target="tpu_custom_call" | custom-call | flops 1000 | tf_op jit(solution)/shard_map/turn/pallas_call | solution.py:106
  91.2 4.0 %per_out.1 = bf16[1536,384]{1,0:T(8,128)(2,1)} custom-call(bf16[1536,256]{1,0:T(8,128)(2,1)} %get-tuple-element.45.refs_0_, bf16[1536,256]{1,0:T(8,128)(2,1)} %copy-done.18, bf16[2,384,256]{2,1,0:T(8,128)(2,1)} %get-tuple-element.47.refs_2_, bf16[2,384,256]{2,1,0:T(8,128)(2,1)} %copy-done.22), custom_call_target="tpu_custom_call" | custom-call | flops 1000 | tf_op jit(solution)/shard_map/per_out/pallas_call | solution.py:106
  96.4 3.3 %collective-permute-start.13 = (bf16[128,3072]{1,0:T(8,128)(2,1)S(1)}, bf16[128,3072]{1,0:T(8,128)(2,1)S(1)}, u32[]{:S(2)}, u32[]{:S(2)}) collective-permute-start(bf16[128,3072]{1,0:T(8,128)(2,1)S(1)} %dynamic-slice_bitcast_fusion), channel_id=1, source_target_pairs={{0,128},{128,0},{1,129},{129,1},{2,130},{130,2},{3,131},{131,3},{4... | collective-permute-start | bytes 2359304 | tf_op jit(solution)/shard_map/ppermute | solution.py:34
  99.7 17.6 %collective-permute-done.13 = bf16[128,3072]{1,0:T(8,128)(2,1)S(1)} collective-permute-done((bf16[128,3072]{1,0:T(8,128)(2,1)S(1)}, bf16[128,3072]{1,0:T(8,128)(2,1)S(1)}, u32[]{:S(2)}, u32[]{:S(2)}) %collective-permute-start.13) | collective-permute-done | bytes 786464 | tf_op jit(solution)/shard_map/ppermute | solution.py:34
  118.1 2.9 %turn.3 = (bf16[1536,256]{1,0:T(8,128)(2,1)}, bf16[1536,256]{1,0:T(8,128)(2,1)}) custom-call(s32[1]{0:T(128)} %bitcast.refs_0_, s32[1]{0:T(128)} %bitcast.1.refs_1_, bf16[2,128,3072]{2,1,0:T(8,128)(2,1)} %refs_2_.2, bf16[1,128,3072]{2,1,0:T(8,128)(2,1)} %bitcast.40), custom_call_target="tpu_custom_call" | custom-call | flops 1000 | tf_op jit(solution)/shard_map/turn/pallas_call | solution.py:106
  122.0 5.0 %all-to-all-done.refs_0_ = bf16[8,256,384]{2,1,0:T(8,128)(2,1)} async-done(((bf16[8,256,384]{2,1,0:T(8,128)(2,1)}), bf16[8,256,384]{2,1,0:T(8,128)(2,1)}, u32[]{:S(2)}, u32[]{:S(2)}) %all-to-all-start) | async-done | bytes 1572896 | tf_op jit(solution)/shard_map/all_to_all | solution.py:394
  132.3 3.2 %per_value.1 = (bf16[2,192,384]{2,1,0:T(8,128)(2,1)}, bf16[2,192,384]{2,1,0:T(8,128)(2,1)}, bf16[1,192,384]{2,1,0:T(8,128)(2,1)}, bf16[1,192,384]{2,1,0:T(8,128)...) custom-call(s32[1]{0:T(128)} %bitcast.2.refs_0_, bf16[1536,256]{1,0:T(8,128)(2,1)} %get-tuple-element.49.refs_1_, ...), custom_call_target="tpu_custom_call" | custom-call | flops 1000 | tf_op jit(solution)/shard_map/per_value/pallas_call | solution.py:106
  138.2 10.7 %collective-permute-done.18.refs_3_ = bf16[1,192,384]{2,1,0:T(8,128)(2,1)S(1)} collective-permute-done((bf16[1,192,384]{2,1,0:T(8,128)(2,1)}, bf16[1,192,384]{2,1,0:T(8,128)(2,1)S(1)}, u32[]{:S(2)}, u32[]{:S(2)}) %collective-permute-start.18) | collective-permute-done | bytes 147488 | tf_op jit(solution)/shard_map/ppermute | solution.py:30
  152.2 3.3 %collective-permute-start.20 = (bf16[1,192,384]{2,1,0:T(8,128)(2,1)}, bf16[1,192,384]{2,1,0:T(8,128)(2,1)S(1)}, u32[]{:S(2)}, u32[]{:S(2)}) collective-permute-start(bf16[1,192,384]{2,1,0:T(8,128)(2,1)} %get-tuple-element.59), channel_id=1, source_target_pairs={{0,96},{16,112},{32,0},{48,16},{64,32},{80,48},{96,64},{112,80},{1... | collective-permute-start | bytes 442376 | tf_op jit(solution)/shard_map/ppermute | solution.py:22
  155.5 5.0 %collective-permute-done.19.refs_4_ = bf16[1,192,384]{2,1,0:T(8,128)(2,1)S(1)} collective-permute-done((bf16[1,192,384]{2,1,0:T(8,128)(2,1)}, bf16[1,192,384]{2,1,0:T(8,128)(2,1)S(1)}, u32[]{:S(2)}, u32[]{:S(2)}) %collective-permute-start.19) | collective-permute-done | bytes 147488 | tf_op jit(solution)/shard_map/ppermute | solution.py:22
  163.3 8.3 %all-to-all-start.1 = ((f32[16,8,128]{2,1,0:T(8,128)}), f32[16,8,128]{2,1,0:T(8,128)S(1)}, u32[]{:S(2)}, u32[]{:S(2)}) async-start(f32[16,8,128]{2,1,0:T(8,128)} %get-tuple-element.60), calls=%async_computation.2 | async-start | bytes 131072 | tf_op jit(solution)/shard_map/all_to_all | solution.py:457
  172.7 5.6 %collective-permute-start.21 = (bf16[96,768]{1,0:T(8,128)(2,1)S(1)}, bf16[96,768]{1,0:T(8,128)(2,1)S(1)}, u32[]{:S(2)}, u32[]{:S(2)}) collective-permute-start(bf16[96,768]{1,0:T(8,128)(2,1)S(1)} %get-tuple-element.69), channel_id=1, source_target_pairs={{0,0},{8,128},{128,8},{136,136},{16,16},{24,144},{144,24},{152,152... | collective-permute-start | bytes 442376 | tf_op jit(solution)/shard_map/ppermute | solution.py:454
  180.1 7.2 %all-to-all-start.2 = ((f32[16,8,128]{2,1,0:T(8,128)}), f32[16,8,128]{2,1,0:T(8,128)S(1)}, u32[]{:S(2)}, u32[]{:S(2)}) async-start(f32[16,8,128]{2,1,0:T(8,128)} %squares.1), calls=%async_computation.3 | async-start | bytes 131072 | tf_op jit(solution)/shard_map/all_to_all | solution.py:459
  187.4 6.5 %all-to-all-done.2.refs_1_ = f32[16,8,128]{2,1,0:T(8,128)S(1)} async-done(((f32[16,8,128]{2,1,0:T(8,128)}), f32[16,8,128]{2,1,0:T(8,128)S(1)}, u32[]{:S(2)}, u32[]{:S(2)}) %all-to-all-start.2) | async-done | bytes 65568 | tf_op jit(solution)/shard_map/all_to_all | solution.py:459
  (123 shorter events, 58.6 us)
Async XLA Ops:
  7.2 76.8 %all-gather.2.cloned.1.call-start = ((), (), s32[]{:S(2)}) async-start(), calls=%async_computation.4 | async-start | bytes 2359296 | tf_op jit(solution)/shard_map/all_gather | solution.py:313
  12.5 8.0 %collective-permute-start = (bf16[128,768]{1,0:T(8,128)(2,1)S(1)}, bf16[128,768]{1,0:T(8,128)(2,1)S(1)}, u32[]{:S(2)}, u32[]{:S(2)}) collective-permute-start(bf16[128,768]{1,0:T(8,128)(2,1)S(1)} %get-tuple-element.67), channel_id=1, source_target_pairs={{0,128},{128,0},{1,129},{129,1},{2,130},{130,2},{3,131},{131,3},{4... | collective-permute-start | bytes 589832 | tf_op jit(solution)/shard_map/ppermute | solution.py:34
  20.6 13.7 %collective-permute-start.1 = (bf16[256,768]{1,0:T(8,128)(2,1)S(1)}, bf16[256,768]{1,0:T(8,128)(2,1)S(1)}, u32[]{:S(2)}, u32[]{:S(2)}) collective-permute-start(bf16[256,768]{1,0:T(8,128)(2,1)S(1)} %pad_maximum_fusion.1.refs_1_.refs_5_), channel_id=1, source_target_pairs={{0,16},{16,32},{32,48},{48,64},{64,80},{80,96},{96,112},{112,0},{1... | collective-permute-start | bytes 1179656 | tf_op jit(solution)/shard_map/ppermute | solution.py:22
  22.5 11.8 %collective-permute-start.2 = (bf16[256,768]{1,0:T(8,128)(2,1)S(1)}, bf16[256,768]{1,0:T(8,128)(2,1)S(1)}, u32[]{:S(2)}, u32[]{:S(2)}) collective-permute-start(bf16[256,768]{1,0:T(8,128)(2,1)S(1)} %pad_maximum_fusion.1.refs_1_.refs_5_), channel_id=1, source_target_pairs={{0,112},{16,0},{32,16},{48,32},{64,48},{80,64},{96,80},{112,96},{1... | collective-permute-start | bytes 1179656 | tf_op jit(solution)/shard_map/ppermute | solution.py:22
  34.3 9.1 %collective-permute-start.5 = (bf16[256,768]{1,0:T(8,128)(2,1)S(1)}, bf16[256,768]{1,0:T(8,128)(2,1)}, u32[]{:S(2)}, u32[]{:S(2)}) collective-permute-start(bf16[256,768]{1,0:T(8,128)(2,1)S(1)} %collective-permute-done.1.refs_2_.refs_6_), channel_id=1, source_target_pairs={{0,16},{16,32},{32,48},{48,64},{64,80},{80,96},{96,112},{112,0},{1... | collective-permute-start | bytes 1179656 | tf_op jit(solution)/shard_map/ppermute | solution.py:22
  34.4 9.0 %collective-permute-start.7 = (bf16[256,768]{1,0:T(8,128)(2,1)S(1)}, bf16[256,768]{1,0:T(8,128)(2,1)}, u32[]{:S(2)}, u32[]{:S(2)}) collective-permute-start(bf16[256,768]{1,0:T(8,128)(2,1)S(1)} %collective-permute-done.2.refs_3_.refs_7_), channel_id=1, source_target_pairs={{0,112},{16,0},{32,16},{48,32},{64,48},{80,64},{96,80},{112,96},{1... | collective-permute-start | bytes 1179656 | tf_op jit(solution)/shard_map/ppermute | solution.py:22
  38.0 9.1 %collective-permute-start.4 = (bf16[256,768]{1,0:T(8,128)(2,1)}, bf16[256,768]{1,0:T(8,128)(2,1)}, u32[]{:S(2)}, u32[]{:S(2)}) collective-permute-start(bf16[256,768]{1,0:T(8,128)(2,1)} %pad_maximum_fusion.3), channel_id=1, source_target_pairs={{0,8},{8,0},{1,9},{9,1},{2,10},{10,2},{3,11},{11,3},{4,12},{12,4},... | collective-permute-start | bytes 1179656 | tf_op jit(solution)/shard_map/ppermute | solution.py:34
  43.4 10.2 %collective-permute-start.6 = (bf16[256,768]{1,0:T(8,128)(2,1)}, bf16[256,768]{1,0:T(8,128)(2,1)S(1)}, u32[]{:S(2)}, u32[]{:S(2)}) collective-permute-start(bf16[256,768]{1,0:T(8,128)(2,1)} %collective-permute-done.5.refs_1_.refs_8_), channel_id=1, source_target_pairs={{0,16},{16,32},{32,48},{48,64},{64,80},{80,96},{96,112},{112,0},{1... | collective-permute-start | bytes 1179656 | tf_op jit(solution)/shard_map/ppermute | solution.py:22
  43.4 10.2 %collective-permute-start.8 = (bf16[256,768]{1,0:T(8,128)(2,1)}, bf16[256,768]{1,0:T(8,128)(2,1)}, u32[]{:S(2)}, u32[]{:S(2)}) collective-permute-start(bf16[256,768]{1,0:T(8,128)(2,1)} %collective-permute-done.7.refs_2_.refs_9_), channel_id=1, source_target_pairs={{0,112},{16,0},{32,16},{48,32},{64,48},{80,64},{96,80},{112,96},{1... | collective-permute-start | bytes 1179656 | tf_op jit(solution)/shard_map/ppermute | solution.py:22
  54.8 7.1 %collective-permute-start.9 = (bf16[256,768]{1,0:T(8,128)(2,1)S(1)}, bf16[256,768]{1,0:T(8,128)(2,1)S(1)}, u32[]{:S(2)}, u32[]{:S(2)}) collective-permute-start(bf16[256,768]{1,0:T(8,128)(2,1)S(1)} %broadcast_select_fusion), channel_id=1, source_target_pairs={{0,16},{8,120},{16,32},{24,8},{32,48},{40,24},{48,64},{56,40},{64,... | collective-permute-start | bytes 1179656 | tf_op jit(solution)/shard_map/ppermute | solution.py:30
  62.7 6.2 %collective-permute-start.10 = (f32[8,512]{1,0:T(8,128)S(1)}, f32[8,512]{1,0:T(8,128)S(1)}, u32[]{:S(2)}, u32[]{:S(2)}) collective-permute-start(f32[8,512]{1,0:T(8,128)S(1)} %stats.5.refs_3_), channel_id=1, source_target_pairs={{0,8},{8,0},{1,9},{9,1},{2,10},{10,2},{3,11},{11,3},{4,12},{12,4},... | collective-permute-start | bytes 49160 | tf_op jit(solution)/shard_map/ppermute | solution.py:34
  78.6 48.4 %all-to-all-start = ((bf16[8,256,384]{2,1,0:T(8,128)(2,1)}), bf16[8,256,384]{2,1,0:T(8,128)(2,1)}, u32[]{:S(2)}, u32[]{:S(2)}) async-start(bf16[8,256,384]{2,1,0:T(8,128)(2,1)} %get-tuple-element.51), calls=%async_computation.1 | async-start | bytes 3145728 | tf_op jit(solution)/shard_map/all_to_all | solution.py:394
  83.7 76.7 %reduce-scatter.2.cloned.1.call-start = ((), (), s32[]{:S(2)}) async-start(), calls=%async_computation.5 | async-start | bytes 1327104 | tf_op jit(solution)/shard_map/reduce_scatter | solution.py:422
  96.4 20.9 %collective-permute-start.13 = (bf16[128,3072]{1,0:T(8,128)(2,1)S(1)}, bf16[128,3072]{1,0:T(8,128)(2,1)S(1)}, u32[]{:S(2)}, u32[]{:S(2)}) collective-permute-start(bf16[128,3072]{1,0:T(8,128)(2,1)S(1)} %dynamic-slice_bitcast_fusion), channel_id=1, source_target_pairs={{0,128},{128,0},{1,129},{129,1},{2,130},{130,2},{3,131},{131,3},{4... | collective-permute-start | bytes 2359304 | tf_op jit(solution)/shard_map/ppermute | solution.py:34
  121.0 9.5 %collective-permute-start.14 = (bf16[1536,256]{1,0:T(8,128)(2,1)}, bf16[1536,256]{1,0:T(8,128)(2,1)S(1)}, u32[]{:S(2)}, u32[]{:S(2)}) collective-permute-start(bf16[1536,256]{1,0:T(8,128)(2,1)} %get-tuple-element.50), channel_id=1, source_target_pairs={{0,8},{8,0},{1,9},{9,1},{2,10},{10,2},{3,11},{11,3},{4,12},{12,4},... | collective-permute-start | bytes 2359304 | tf_op jit(solution)/shard_map/ppermute | solution.py:34
  135.4 13.5 %collective-permute-start.16 = (bf16[2,192,384]{2,1,0:T(8,128)(2,1)}, bf16[2,192,384]{2,1,0:T(8,128)(2,1)S(1)}, u32[]{:S(2)}, u32[]{:S(2)}) collective-permute-start(bf16[2,192,384]{2,1,0:T(8,128)(2,1)} %get-tuple-element.53), channel_id=1, source_target_pairs={{0,16},{16,32},{32,48},{48,64},{64,80},{80,96},{96,112},{112,0},{1... | collective-permute-start | bytes 884744 | tf_op jit(solution)/shard_map/ppermute | solution.py:22
  137.2 11.7 %collective-permute-start.17 = (bf16[2,192,384]{2,1,0:T(8,128)(2,1)}, bf16[2,192,384]{2,1,0:T(8,128)(2,1)S(1)}, u32[]{:S(2)}, u32[]{:S(2)}) collective-permute-start(bf16[2,192,384]{2,1,0:T(8,128)(2,1)} %get-tuple-element.54), channel_id=1, source_target_pairs={{0,112},{16,0},{32,16},{48,32},{64,48},{80,64},{96,80},{112,96},{1... | collective-permute-start | bytes 884744 | tf_op jit(solution)/shard_map/ppermute | solution.py:22
  138.2 10.7 %collective-permute-start.18 = (bf16[1,192,384]{2,1,0:T(8,128)(2,1)}, bf16[1,192,384]{2,1,0:T(8,128)(2,1)S(1)}, u32[]{:S(2)}, u32[]{:S(2)}) collective-permute-start(bf16[1,192,384]{2,1,0:T(8,128)(2,1)} %get-tuple-element.55), channel_id=1, source_target_pairs={{0,32},{8,104},{16,48},{24,120},{32,64},{40,8},{48,80},{56,24},{64... | collective-permute-start | bytes 442376 | tf_op jit(solution)/shard_map/ppermute | solution.py:30
  151.8 8.6 %collective-permute-start.19 = (bf16[1,192,384]{2,1,0:T(8,128)(2,1)}, bf16[1,192,384]{2,1,0:T(8,128)(2,1)S(1)}, u32[]{:S(2)}, u32[]{:S(2)}) collective-permute-start(bf16[1,192,384]{2,1,0:T(8,128)(2,1)} %get-tuple-element.58), channel_id=1, source_target_pairs={{0,32},{16,48},{32,64},{48,80},{64,96},{80,112},{96,0},{112,16},{1... | collective-permute-start | bytes 442376 | tf_op jit(solution)/shard_map/ppermute | solution.py:22
  152.2 8.2 %collective-permute-start.20 = (bf16[1,192,384]{2,1,0:T(8,128)(2,1)}, bf16[1,192,384]{2,1,0:T(8,128)(2,1)S(1)}, u32[]{:S(2)}, u32[]{:S(2)}) collective-permute-start(bf16[1,192,384]{2,1,0:T(8,128)(2,1)} %get-tuple-element.59), channel_id=1, source_target_pairs={{0,96},{16,112},{32,0},{48,16},{64,32},{80,48},{96,64},{112,80},{1... | collective-permute-start | bytes 442376 | tf_op jit(solution)/shard_map/ppermute | solution.py:22
  163.3 16.1 %all-to-all-start.1 = ((f32[16,8,128]{2,1,0:T(8,128)}), f32[16,8,128]{2,1,0:T(8,128)S(1)}, u32[]{:S(2)}, u32[]{:S(2)}) async-start(f32[16,8,128]{2,1,0:T(8,128)} %get-tuple-element.60), calls=%async_computation.2 | async-start | bytes 131072 | tf_op jit(solution)/shard_map/all_to_all | solution.py:457
  172.7 14.7 %collective-permute-start.21 = (bf16[96,768]{1,0:T(8,128)(2,1)S(1)}, bf16[96,768]{1,0:T(8,128)(2,1)S(1)}, u32[]{:S(2)}, u32[]{:S(2)}) collective-permute-start(bf16[96,768]{1,0:T(8,128)(2,1)S(1)} %get-tuple-element.69), channel_id=1, source_target_pairs={{0,0},{8,128},{128,8},{136,136},{16,16},{24,144},{144,24},{152,152... | collective-permute-start | bytes 442376 | tf_op jit(solution)/shard_map/ppermute | solution.py:454
  178.2 9.1 %collective-permute-start.22 = (bf16[96,768]{1,0:T(8,128)(2,1)S(1)}, bf16[96,768]{1,0:T(8,128)(2,1)S(1)}, u32[]{:S(2)}, u32[]{:S(2)}) collective-permute-start(bf16[96,768]{1,0:T(8,128)(2,1)S(1)} %get-tuple-element.68), channel_id=1, source_target_pairs={{0,8},{8,136},{128,0},{136,128},{16,24},{24,152},{144,16},{152,144... | collective-permute-start | bytes 442376 | tf_op jit(solution)/shard_map/ppermute | solution.py:455
  180.1 13.7 %all-to-all-start.2 = ((f32[16,8,128]{2,1,0:T(8,128)}), f32[16,8,128]{2,1,0:T(8,128)S(1)}, u32[]{:S(2)}, u32[]{:S(2)}) async-start(f32[16,8,128]{2,1,0:T(8,128)} %squares.1), calls=%async_computation.3 | async-start | bytes 131072 | tf_op jit(solution)/shard_map/all_to_all | solution.py:459
  (34 other events, 192.3 us)
Sparse Core Ops, SparseCore 0:
  38.2 36.8 all-gather.1
  95.3 43.4 reduce-scatter.1
